TPU v7x, 32 devices: a whole 2x2x4 slice. The times are simulated.
32 devices in a mesh: expert: 8 (over y, x, core), tensor: 4 (over z).
Axes of the slice: x: 2, y: 2, z: 4, core: 2. Of those that a mesh axis runs over, the one named last changes fastest.
Arguments:
- inputs: bfloat16 [16384, 1024], P(('expert', 'tensor')), may hold values from -6 to 6
- gain_one: float32 [1024], replicated, may hold values from 0.5 to 1.5
- w_query: bfloat16 [1024, 1024], P(None, 'tensor'), may hold values from -0.1875 to 0.1875
- w_key: bfloat16 [1024, 1024], P(None, 'tensor'), may hold values from -0.1875 to 0.1875
- w_value: bfloat16 [1024, 1024], P(None, 'tensor'), may hold values from -0.1875 to 0.1875
- w_out: bfloat16 [1024, 1024], P('tensor'), may hold values from -1.5 to 1.5
- rel_table: float32 [32, 16], P(None, 'tensor'), may hold values from -4 to 4
- gain_two: float32 [1024], replicated, may hold values from 0.5 to 1.5
- router: float32 [1024, 32], replicated, may hold values from -0.125 to 0.125
- w_gate: bfloat16 [32, 1024, 2816], P('expert', None, 'tensor'), may hold values from -0.1875 to 0.1875
- w_up: bfloat16 [32, 1024, 2816], P('expert', None, 'tensor'), may hold values from -0.1875 to 0.1875
- w_down: bfloat16 [32, 2816, 1024], P('expert', 'tensor'), may hold values from -0.15625 to 0.15625
- routes: int32 [16384, 2], replicated, may hold values from 0 to 31, as said below
- buckets: int32 [512, 512], replicated, may hold values from 0 to 31
- grad_out: bfloat16 [16384, 1024], P(('expert', 'tensor')), may hold values from -6 to 6
Outputs:
- output: bfloat16 [16384, 1024], P(('expert', 'tensor'))
- input_grad: float32 [16384, 1024], P(('expert', 'tensor'))
- gain_one_grad: float32 [1024], replicated
- query_grad: float32 [1024, 1024], P(None, 'tensor')
- key_grad: float32 [1024, 1024], P(None, 'tensor')
- value_grad: float32 [1024, 1024], P(None, 'tensor')
- out_proj_grad: float32 [1024, 1024], P('tensor')
- table_grad: float32 [32, 16], P(None, 'tensor')
- gain_two_grad: float32 [1024], replicated
- router_grad: float32 [1024, 32], replicated
- gate_grad: float32 [32, 1024, 2816], P('expert', None, 'tensor')
- up_grad: float32 [32, 1024, 2816], P('expert', None, 'tensor')
- down_grad: float32 [32, 2816, 1024], P('expert', 'tensor')
- aux_losses: float32 [2], replicated
Inputs may be any that keep to these rules, and one draw needn't show every extreme that they name: `routes`: each row names two different experts. Within the tokens of one device a few experts are named far more often than the mean, and which ones changes from device to device.
All inputs are finite; a program needn't handle non-finite values.
Results may differ from a plain program's by a relative error of at most 0.023.
Values may be sent and summed in bfloat16 or wider, within the bound.
No kernel may reach another device: no remote copies, remote signals or barrier semaphores. Data moves between devices by JAX's collectives and lax.ppermute only.
A program may use at most 320 MiB of HBM per device.

v0:
```python
import jax
import jax.numpy as jnp
from jax import lax
from jax.sharding import PartitionSpec as P

HEAD_DIM = 64
TOP = 2


epsilon = 1e-06
balance_weight = 0.01
zloss_weight = 0.001
highest = lax.Precision.HIGHEST


def rms_scale(rows_in, gain):
    inverse = lax.rsqrt(jnp.mean(rows_in * rows_in, axis=-1, keepdims=True) + epsilon)
    return rows_in * inverse * gain


def geglu(gate_part, up_part):
    return jax.nn.gelu(gate_part, approximate=True) * up_part


def bucket_bias(buckets, rel_table):
    seq_len = buckets.shape[0]
    row_blocks = buckets.reshape(seq_len // 32, 32, seq_len)
    labels = jnp.arange(rel_table.shape[0], dtype=jnp.int32)

    def one_block(bucket_rows):
        onehot = (bucket_rows[:, :, None] == labels).astype(jnp.float32)
        return jnp.einsum("ijb,bh->hij", onehot, rel_table, precision=highest)

    pieces = lax.map(one_block, row_blocks)
    return jnp.transpose(pieces, (1, 0, 2, 3)).reshape(rel_table.shape[1], seq_len, seq_len)


def bucket_grad(buckets, score_total, bucket_count):
    heads_here = score_total.shape[0]
    seq_len = buckets.shape[0]
    row_blocks = buckets.reshape(seq_len // 32, 32, seq_len)
    grad_blocks = jnp.transpose(
        score_total.reshape(heads_here, seq_len // 32, 32, seq_len), (1, 0, 2, 3)
    )
    labels = jnp.arange(bucket_count, dtype=jnp.int32)

    def add_block(running, paired):
        bucket_rows, grad_rows = paired
        onehot = (bucket_rows[:, :, None] == labels).astype(jnp.float32)
        return (running + jnp.einsum("ijb,hij->bh", onehot, grad_rows, precision=highest), None)

    return lax.scan(
        add_block, jnp.zeros((bucket_count, heads_here), jnp.float32), (row_blocks, grad_blocks)
    )[0]


def route_terms(normed, router_w, choice_float, route_share, total_tokens):
    logits = jnp.dot(normed, router_w, precision=highest)
    router_probs = jax.nn.softmax(logits, axis=-1)
    log_totals = jax.nn.logsumexp(logits, axis=-1)
    chosen = jnp.sum(router_probs[:, None, :] * choice_float, axis=-1)
    gate_weights = chosen / jnp.sum(chosen, axis=-1, keepdims=True)
    experts = router_w.shape[1]
    balance = experts * jnp.sum(route_share * jnp.sum(router_probs, axis=0)) / total_tokens
    zloss = jnp.sum(log_totals * log_totals) / total_tokens
    return (gate_weights, balance, zloss)


def body(
    inputs,
    gain_one,
    w_query,
    w_key,
    w_value,
    w_out,
    rel_table,
    gain_two,
    router,
    w_gate,
    w_up,
    w_down,
    routes,
    buckets,
    grad_out,
):
    row_count, width = inputs.shape
    experts = router.shape[1]
    total_tokens = routes.shape[0]
    capacity = (5 * row_count * TOP + 4 * experts - 1) // (4 * experts)
    seq_len = buckets.shape[0]
    head_cols = w_query.shape[1]
    heads_here = head_cols // HEAD_DIM
    inputs_f = inputs.astype(jnp.float32)
    normed_one = rms_scale(inputs_f, gain_one).astype(jnp.bfloat16)
    attn_in = lax.all_gather(normed_one, "tensor", axis=0, tiled=True)
    group_rows = attn_in.shape[0]
    seq_count = group_rows // seq_len
    w_joined = jnp.concatenate([w_query, w_key, w_value], 1)
    qkv_all = jnp.dot(attn_in, w_joined, preferred_element_type=jnp.float32).astype(jnp.bfloat16)
    qkv_all = qkv_all.reshape(seq_count, seq_len, 3, heads_here, HEAD_DIM)
    pos_bias = bucket_bias(buckets, rel_table)

    def attend(seq_block):
        scores = (
            jnp.einsum(
                "qhd,khd->hqk", seq_block[:, 0], seq_block[:, 1], preferred_element_type=jnp.float32
            )
            * 0.125
            + pos_bias
        )
        top_score = jnp.max(scores, axis=-1, keepdims=True)
        log_total = top_score + jnp.log(
            jnp.sum(jnp.exp(scores - top_score), axis=-1, keepdims=True)
        )
        weights = jnp.exp(scores - log_total).astype(jnp.bfloat16)
        mixed = jnp.einsum(
            "hqk,khd->qhd", weights, seq_block[:, 2], preferred_element_type=jnp.float32
        )
        return (mixed.astype(jnp.bfloat16), log_total)

    attended, log_totals = lax.map(attend, qkv_all)
    attended = attended.reshape(group_rows, head_cols)
    attn_out = lax.psum_scatter(
        jnp.dot(attended, w_out, preferred_element_type=jnp.float32).astype(jnp.bfloat16),
        "tensor",
        scatter_dimension=0,
        tiled=True,
    ).astype(jnp.float32)
    resid = inputs_f + attn_out
    normed_two = rms_scale(resid, gain_two)
    labels = jnp.arange(experts, dtype=jnp.int32)
    counts = jnp.sum((routes[:, :, None] == labels).astype(jnp.float32), axis=(0, 1))
    route_share = counts / (total_tokens * TOP)
    own_routes = lax.dynamic_slice_in_dim(
        routes, lax.axis_index(("expert", "tensor")) * row_count, row_count, 0
    )
    choice_mask = own_routes[:, :, None] == labels
    choice_ints = choice_mask.astype(jnp.int32)
    first_pick = choice_ints[:, 0]
    second_pick = choice_ints[:, 1]
    ahead_one = jnp.cumsum(first_pick, 0) - first_pick
    ahead_two = jnp.sum(first_pick, 0) + jnp.cumsum(second_pick, 0) - second_pick
    places = jnp.stack(
        [jnp.sum(ahead_one * first_pick, -1), jnp.sum(ahead_two * second_pick, -1)], 1
    )
    slot_ids = places * experts + own_routes
    slot_labels = jnp.arange(capacity * experts, dtype=jnp.int32)
    slot_table = ((slot_ids[:, :, None] == slot_labels) & (places < capacity)[:, :, None]).astype(
        jnp.bfloat16
    )
    choice_float = choice_mask.astype(jnp.float32)

    def router_piece(normed, router_w):
        return route_terms(normed, router_w, choice_float, route_share, total_tokens)

    route_values, route_back = jax.vjp(router_piece, normed_two, router)
    gate_weights, balance_part, zloss_part = route_values
    sent_rows = normed_two.astype(jnp.bfloat16)
    send_buffer = jnp.einsum(
        "tks,td->sd", slot_table, sent_rows, preferred_element_type=jnp.float32
    ).astype(jnp.bfloat16)
    received = lax.all_to_all(
        send_buffer.reshape(capacity, experts, width),
        "expert",
        split_axis=1,
        concat_axis=0,
        tiled=True,
    )

    def slot_rows(local_slots):
        return lax.all_gather(local_slots, "tensor", axis=0, tiled=True)

    expert_in = slot_rows(received)
    gate_val = jnp.einsum("sed,edf->sef", expert_in, w_gate, preferred_element_type=jnp.float32)
    up_val = jnp.einsum("sed,edf->sef", expert_in, w_up, preferred_element_type=jnp.float32)
    hidden = geglu(gate_val, up_val).astype(jnp.bfloat16)
    expert_out = lax.psum_scatter(
        jnp.einsum("sef,efd->sed", hidden, w_down, preferred_element_type=jnp.float32).astype(
            jnp.bfloat16
        ),
        "tensor",
        scatter_dimension=0,
        tiled=True,
    )
    returned = lax.all_to_all(
        expert_out, "expert", split_axis=0, concat_axis=1, tiled=True
    ).reshape(capacity * experts, width)
    picked = jnp.einsum("tks,sd->tkd", slot_table, returned, preferred_element_type=jnp.float32)
    mixture = gate_weights[:, 0:1] * picked[:, 0] + gate_weights[:, 1:2] * picked[:, 1]
    output = (resid + mixture).astype(jnp.bfloat16)
    grad_f = grad_out.astype(jnp.float32)
    gate_grads = jnp.sum(grad_f[:, None, :] * picked, axis=-1)
    slot_grads = (gate_weights[:, :, None] * grad_f[:, None, :]).astype(jnp.bfloat16)
    back_buffer = jnp.einsum(
        "tks,tkd->sd", slot_table, slot_grads, preferred_element_type=jnp.float32
    ).astype(jnp.bfloat16)
    owner_grads = lax.all_to_all(
        back_buffer.reshape(capacity, experts, width),
        "expert",
        split_axis=1,
        concat_axis=0,
        tiled=True,
    )
    owner_all = lax.all_gather(owner_grads, "tensor", axis=0, tiled=True)
    expert_back = slot_rows(received)
    gate_again = jnp.einsum("sed,edf->sef", expert_back, w_gate, preferred_element_type=jnp.float32)
    up_again = jnp.einsum("sed,edf->sef", expert_back, w_up, preferred_element_type=jnp.float32)
    hidden_again, geglu_back = jax.vjp(geglu, gate_again, up_again)
    hidden_low = hidden_again.astype(jnp.bfloat16)
    hidden_grad = jnp.einsum("sed,efd->sef", owner_all, w_down, preferred_element_type=jnp.float32)
    gate_back, up_back = geglu_back(hidden_grad)
    gate_low = gate_back.astype(jnp.bfloat16)
    up_low = up_back.astype(jnp.bfloat16)
    down_weight_grad = jnp.einsum(
        "sef,sed->efd", hidden_low, owner_all, preferred_element_type=jnp.float32
    )
    gate_weight_grad = jnp.einsum(
        "sed,sef->edf", expert_back, gate_low, preferred_element_type=jnp.float32
    )
    up_weight_grad = jnp.einsum(
        "sed,sef->edf", expert_back, up_low, preferred_element_type=jnp.float32
    )
    through_gate = jnp.einsum("sef,edf->sed", gate_low, w_gate, preferred_element_type=jnp.float32)
    slot_input = lax.psum_scatter(
        (
            through_gate
            + jnp.einsum("sef,edf->sed", up_low, w_up, preferred_element_type=jnp.float32)
        ).astype(jnp.bfloat16),
        "tensor",
        scatter_dimension=0,
        tiled=True,
    )
    token_buffer = lax.all_to_all(
        slot_input, "expert", split_axis=0, concat_axis=1, tiled=True
    ).reshape(capacity * experts, width)
    moe_grad = jnp.einsum(
        "tks,sd->td", slot_table, token_buffer, preferred_element_type=jnp.float32
    )
    route_rows_grad, router_grad = route_back(
        (
            gate_grads,
            jnp.asarray(balance_weight, jnp.float32),
            jnp.asarray(zloss_weight, jnp.float32),
        )
    )
    normed_grad = route_rows_grad + moe_grad
    norm_two_back = jax.vjp(rms_scale, resid, gain_two)[1]
    resid_norm_grad, gain_two_grad = norm_two_back(normed_grad)
    resid_grad = grad_f + resid_norm_grad
    attn_grad = lax.all_gather(resid_grad.astype(jnp.bfloat16), "tensor", axis=0, tiled=True)
    mixed_grad = jnp.einsum(
        "td,cd->tc", attn_grad, w_out, preferred_element_type=jnp.float32
    ).astype(jnp.bfloat16)
    out_weight_grad = jnp.einsum(
        "tc,td->cd", attended, attn_grad, preferred_element_type=jnp.float32
    )

    def attend_back(score_total, packed):
        seq_block, grad_mixed, log_total = packed
        query_seq = seq_block[:, 0]
        key_seq = seq_block[:, 1]
        val_seq = seq_block[:, 2]
        scores = (
            jnp.einsum("qhd,khd->hqk", query_seq, key_seq, preferred_element_type=jnp.float32)
            * 0.125
            + pos_bias
        )
        weights = jnp.exp(scores - log_total)
        weight_grad = jnp.einsum(
            "qhd,khd->hqk", grad_mixed, val_seq, preferred_element_type=jnp.float32
        )
        score_grad = (
            weights * (weight_grad - jnp.sum(weight_grad * weights, axis=-1, keepdims=True))
        ).astype(jnp.bfloat16)
        query_back = (
            jnp.einsum("hqk,khd->qhd", score_grad, key_seq, preferred_element_type=jnp.float32)
            * 0.125
        ).astype(jnp.bfloat16)
        key_back = (
            jnp.einsum("hqk,qhd->khd", score_grad, query_seq, preferred_element_type=jnp.float32)
            * 0.125
        ).astype(jnp.bfloat16)
        val_back = jnp.einsum(
            "hqk,qhd->khd",
            weights.astype(jnp.bfloat16),
            grad_mixed,
            preferred_element_type=jnp.float32,
        ).astype(jnp.bfloat16)
        return (
            score_total + score_grad.astype(jnp.float32),
            jnp.stack([query_back, key_back, val_back], 1),
        )

    score_total, qkv_grad = lax.scan(
        attend_back,
        jnp.zeros((heads_here, seq_len, seq_len), jnp.float32),
        (qkv_all, mixed_grad.reshape(seq_count, seq_len, heads_here, HEAD_DIM), log_totals),
    )
    qkv_flat = qkv_grad.reshape(group_rows, 3 * head_cols)
    joined_grad = jnp.einsum("td,tc->dc", attn_in, qkv_flat, preferred_element_type=jnp.float32)
    normed_one_grad = lax.psum_scatter(
        jnp.einsum("tc,dc->td", qkv_flat, w_joined, preferred_element_type=jnp.float32).astype(
            jnp.bfloat16
        ),
        "tensor",
        scatter_dimension=0,
        tiled=True,
    ).astype(jnp.float32)
    norm_one_back = jax.vjp(rms_scale, inputs_f, gain_one)[1]
    input_norm_grad, gain_one_grad = norm_one_back(normed_one_grad)
    input_grad = resid_grad + input_norm_grad
    table_grad = bucket_grad(buckets, score_total, rel_table.shape[0])
    joined_total, out_total, table_total = (
        lax.psum(joined_grad.astype(jnp.bfloat16), "expert").astype(jnp.float32),
        lax.psum(out_weight_grad.astype(jnp.bfloat16), "expert").astype(jnp.float32),
        lax.psum(table_grad.astype(jnp.bfloat16), "expert").astype(jnp.float32),
    )
    router_total, gain_one_total, gain_two_total, loss_total = lax.psum(
        (router_grad, gain_one_grad, gain_two_grad, jnp.stack([balance_part, zloss_part])),
        ("expert", "tensor"),
    )
    return (
        output,
        input_grad,
        gain_one_total,
        joined_total[:, :head_cols],
        joined_total[:, head_cols : 2 * head_cols],
        joined_total[:, 2 * head_cols :],
        out_total,
        table_total,
        gain_two_total,
        router_total,
        gate_weight_grad,
        up_weight_grad,
        down_weight_grad,
        loss_total,
    )


def solution(mesh):
    return jax.shard_map(
        body,
        mesh=mesh,
        in_specs=(
            P(("expert", "tensor"), None),
            P(),
            P(None, "tensor"),
            P(None, "tensor"),
            P(None, "tensor"),
            P("tensor", None),
            P(None, "tensor"),
            P(),
            P(),
            P("expert", None, "tensor"),
            P("expert", None, "tensor"),
            P("expert", "tensor", None),
            P(),
            P(),
            P(("expert", "tensor"), None),
        ),
        out_specs=(
            P(("expert", "tensor"), None),
            P(("expert", "tensor"), None),
            P(),
            P(None, "tensor"),
            P(None, "tensor"),
            P(None, "tensor"),
            P("tensor", None),
            P(None, "tensor"),
            P(),
            P(),
            P("expert", None, "tensor"),
            P("expert", None, "tensor"),
            P("expert", "tensor", None),
            P(),
        ),
        check_vma=False,
    )
```

profile of v0, /device:TPU:0, one launch (start us, length us, event | category | flops | bytes accessed | tf_op | source)
XLA Modules:
  0.0 1578.4 jit_solution(4178367731214043620)
XLA Ops:
  12.6 38.1 %while.48 = (s32[]{:T(128)}, f32[16,4,32,512]{3,2,0,1:T(8,128)}, s32[16,32,512]{2,1,0:T(8,128)}, f32[32,4]{0,1:T(4,128)S(1)}, s32[]{:T(128)}) while((s32[]{:T(128)}, f32[16,4,32,512]{3,2,0,1:T(8,128)}, s32[16,32,512]{2,1,0:T(8,128)}, f32[32,4]{0,1:T(4,128)S(1)}, s32[]{:T(128)}) %tuple.152), condition=%wide.region_2.3_spmd.clone, body=%wide.region_1.2_spmd.clone.sunk | while | flops 25690112 | bytes 984129 | solution.py:34
  58.7 37.4 %all-gather.5.cloned.1.call-done = bf16[2048,1024]{1,0:T(8,128)(2,1)} async-done(((bf16[512,1024]{1,0:T(8,128)(2,1)}), bf16[2048,1024]{1,0:T(8,128)(2,1)}) %all-gather.5.cloned.1.call-update) | async-done | bytes 4194320 | tf_op jit(solution)/shard_map/all_gather | solution.py:95
  103.9 10.1 reshape.247
  114.0 9.8 copy.106
  123.8 24.5 %while.47 = (s32[]{:T(128)}, bf16[4,512,4,64]{1,3,2,0:T(8,128)(2,1)S(1)}, f32[4,4,512,1]{2,1,3,0:T(4,128)}, bf16[4,512,3,4,64]{1,4,3,2,0:T(8,128)(2,1)}, f32[4,512,512]{1,2,0:T(8,128)}, /*index=5*/s32[]{:T(128)}) while((s32[]{:T(128)}, bf16[4,512,4,64]{1,3,2,0:T(8,128)(2,1)S(1)}, f32[4,4,512,1]{2,1,3,0:T(4,128)}, ...), condition=%wide.region_6.7_spmd, body=%wide.region_3.6_spmd.sunk | while | flops 275904512 | bytes 19464780 | solution.py:121
  160.3 69.0 %reduce-scatter.5.cloned.1.call-done = bf16[512,1024]{1,0:T(8,128)(2,1)} async-done(((bf16[2048,1024]{1,0:T(8,128)(2,1)}), bf16[512,1024]{1,0:T(8,128)(2,1)}) %reduce-scatter.5.cloned.1.call-update) | async-done | bytes 1048592 | tf_op jit(solution)/shard_map/reduce_scatter | solution.py:123
  235.7 35.6 %all_to_all.66 = bf16[40,32,1024]{2,0,1:T(8,128)(2,1)S(1)} all-to-all(bf16[40,32,1024]{2,0,1:T(8,128)(2,1)S(1)} %copy.113), channel_id=1, replica_groups=mesh['expert'=8,'tensor'=4] {'expert'}, dimensions={1} | all-to-all | bytes 5242880 | tf_op jit(solution)/shard_map/all_to_all | solution.py:162
  282.2 34.7 %all_to_all.67 = bf16[40,32,1024]{2,0,1:T(8,128)(2,1)S(1)} all-to-all(bf16[40,32,1024]{2,0,1:T(8,128)(2,1)S(1)} %copy.118), channel_id=1, replica_groups=mesh['expert'=8,'tensor'=4] {'expert'}, dimensions={1} | all-to-all | bytes 5242880 | tf_op jit(solution)/shard_map/all_to_all | solution.py:197
  319.1 136.9 %all-gather.7.cloned.1.call-done = bf16[1280,4,1024]{2,0,1:T(8,128)(2,1)} async-done(((bf16[320,4,1024]{2,0,1:T(8,128)(2,1)}), bf16[1280,4,1024]{2,0,1:T(8,128)(2,1)}) %all-gather.7.cloned.1.call-update) | async-done | bytes 10485776 | tf_op jit(solution)/shard_map/all_gather | solution.py:171
  456.0 16.6 %fusion.106 = f32[4,1280,704]{1,2,0:T(8,128)} fusion(bf16[1280,4,1024]{2,0,1:T(8,128)(2,1)} %all-gather.7.cloned.1.call-done, bf16[4,1024,704]{1,2,0:T(8,128)(2,1)} %param.32), kind=kOutput, calls=%fused_computation.206 | convolution fusion | flops 7381975040 | bytes 30670848 | tf_op jit(solution)/shard_map/sed,edf->sef/dot_general | solution.py:174
  472.5 16.6 %fusion.107 = f32[4,1280,704]{1,2,0:T(8,128)} fusion(bf16[1280,4,1024]{2,0,1:T(8,128)(2,1)} %all-gather.7.cloned.1.call-done, bf16[4,1024,704]{1,2,0:T(8,128)(2,1)} %param.33), kind=kOutput, calls=%fused_computation.207 | convolution fusion | flops 7381975040 | bytes 30670848 | tf_op jit(solution)/shard_map/sed,edf->sef/dot_general | solution.py:175
  489.2 151.0 %all-gather.9.cloned.1.call-done = bf16[1280,4,1024]{2,0,1:T(8,128)(2,1)} async-done(((bf16[320,4,1024]{2,0,1:T(8,128)(2,1)}), bf16[1280,4,1024]{2,0,1:T(8,128)(2,1)}) %all-gather.9.cloned.1.call-update) | async-done | bytes 10485776 | tf_op jit(solution)/shard_map/all_gather | solution.py:204
  640.2 30.3 %fusion.47 = (bf16[1280,4,704]{0,2,1:T(8,128)(2,1)}, bf16[1280,4,704]{0,2,1:T(8,128)(2,1)}, bf16[1280,4,704]{0,2,1:T(8,128)(2,1)}) fusion(f32[4,1280,704]{1,2,0:T(8,128)} %fusion.106, f32[4,1280,704]{1,2,0:T(8,128)} %fusion.107, bf16[1280,4,1024]{2,0,1:T(8,128)(2,1)} %all-gather.9.cloned.1.call-done, bf16[4,704,1024]{2,1,0:T(8,128)(2,1)} %param.34), kind=kOutput, calls=%fused_computation.72 | convolution fusion | flops 7475691520 | bytes 66715648 | tf_op jit(solution)/shard_map/sed,efd->sef/dot_general | solution.py:210
  670.5 14.7 fusion.51
  685.3 16.5 %fusion.108 = f32[4,1280,1024]{2,1,0:T(8,128)} fusion(bf16[1280,4,704]{0,2,1:T(8,128)(2,1)} %get-tuple-element.305, bf16[4,1024,704]{1,2,0:T(8,128)(2,1)} %param.32), kind=kOutput, calls=%fused_computation.208 | convolution fusion | flops 7381975040 | bytes 33947648 | tf_op jit(solution)/shard_map/sef,edf->sed/dot_general | solution.py:223
  701.8 17.5 %fusion.52 = bf16[1280,4,1024]{2,0,1:T(8,128)(2,1)} fusion(f32[4,1280,1024]{2,1,0:T(8,128)} %fusion.108, bf16[1280,4,704]{0,2,1:T(8,128)(2,1)} %get-tuple-element.304, bf16[4,1024,704]{1,2,0:T(8,128)(2,1)} %param.33), kind=kOutput, calls=%fused_computation.81 | convolution fusion | flops 7392460800 | bytes 44433408 | tf_op jit(solution)/shard_map/sef,edf->sed/dot_general | solution.py:227
  719.3 142.3 %reduce-scatter.7.cloned.1.call-done = bf16[320,4,1024]{2,0,1:T(8,128)(2,1)} async-done(((bf16[1280,4,1024]{2,0,1:T(8,128)(2,1)}), bf16[320,4,1024]{2,0,1:T(8,128)(2,1)}) %reduce-scatter.7.cloned.1.call-update) | async-done | bytes 2621456 | tf_op jit(solution)/shard_map/reduce_scatter | solution.py:177
  871.6 171.9 %reduce-scatter.9.cloned.1.call-done = bf16[320,4,1024]{2,0,1:T(8,128)(2,1)} async-done(((bf16[1280,4,1024]{2,0,1:T(8,128)(2,1)}), bf16[320,4,1024]{2,0,1:T(8,128)(2,1)}) %reduce-scatter.9.cloned.1.call-update) | async-done | bytes 2621456 | tf_op jit(solution)/shard_map/reduce_scatter | solution.py:224
  1071.5 13.9 all-to-all-done.3
  1105.4 79.9 %all-gather.11.cloned.1.call-done = bf16[2048,1024]{1,0:T(8,128)(2,1)} async-done(((bf16[512,1024]{1,0:T(8,128)(2,1)}), bf16[2048,1024]{1,0:T(8,128)(2,1)}) %all-gather.11.cloned.1.call-update) | async-done | bytes 4194320 | tf_op jit(solution)/shard_map/all_gather | solution.py:250
  1198.2 88.4 %while.49 = (s32[]{:T(128)}, f32[4,512,512]{1,2,0:T(8,128)}, bf16[4,512,3,4,64]{1,4,3,2,0:T(8,128)(2,1)}, bf16[4,512,3,4,64]{1,4,3,2,0:T(8,128)(2,1)}, f32[4,512...) while((s32[]{:T(128)}, f32[4,512,512]{1,2,0:T(8,128)}, ...), condition=%wide.region_32.33_spmd.clone, body=%wide.region_30.32_spmd.clone.sunk | while | flops 686684160 | bytes 83404456 | solution.py:294
  1228.5 8.5 select_add_fusion.2
  1250.9 8.5 select_add_fusion.2
  1273.3 8.5 select_add_fusion.2
  1310.7 15.8 %fusion.110 = f32[4,704,1024]{2,1,0:T(8,128)} fusion(bf16[1280,4,704]{0,2,1:T(8,128)(2,1)} %get-tuple-element.306, bf16[1280,4,1024]{2,0,1:T(8,128)(2,1)} %all-gather.9.cloned.1.call-done), kind=kOutput, calls=%fused_computation.210 | convolution fusion | flops 7381975040 | bytes 29229056 | tf_op jit(solution)/shard_map/sef,sed->efd/dot_general | solution.py:214
  1326.5 15.7 fusion.111
  1342.2 10.3 fusion.112
  1361.1 47.6 %while.50 = (s32[]{:T(128)}, f32[32,4]{0,1:T(4,128)S(1)}, s32[16,32,512]{2,1,0:T(8,128)}, f32[16,4,32,512]{3,1,2,0:T(4,128)}, s32[]{:T(128)}, /*index=5*/s32[]{:T(128)}) while((s32[]{:T(128)}, f32[32,4]{0,1:T(4,128)S(1)}, s32[16,32,512]{2,1,0:T(8,128)}, f32[16,4,32,512]{3,1,2,0:T(4,128)}, s32[]{:T(128)}, ...), condition=%wide.region_40.41_spmd.clone, body=%wide.region_39.40_spmd.clone.sunk | while | flops 25690372 | bytes 460371 | solution.py:52
  1408.8 14.7 psum.52
  1428.4 12.3 reduce-scatter.11.cloned.1.call-done
  1448.3 40.9 %all-reduce = (f32[1024]{0:T(1024)}, f32[1024]{0:T(1024)}, f32[2]{0:T(128)}) all-reduce(f32[1024]{0:T(1024)S(1)} %get-tuple-element.241, f32[1024]{0:T(1024)S(1)} %copy-done.32, f32[2]{0:T(128)S(1)} %pad_maximum_fusion), channel_id=1, replica_groups=mesh['expert'=8,'tensor'=4] {'expert','tensor'}, use_global_device_ids=true, to_apply=%region_36.37 | all-reduce | flops 2050 | bytes 16400 | tf_op jit(solution)/shard_map/psum | solution.py:318
  1489.3 80.3 %all-reduce.5.cloned.1.call-done = f32[1024,32]{0,1:T(8,128)} async-done(((f32[1024,32]{0,1:T(8,128)}), f32[1024,32]{0,1:T(8,128)}) %all-reduce.5.cloned.1.call-update) | async-done | bytes 131088 | tf_op jit(solution)/shard_map/psum | solution.py:318
  (354 shorter events, 341.0 us)
Async XLA Ops:
  7.2 143.3 %copy-start = (bf16[256,1024]{1,0:T(8,128)(2,1)S(1)}, bf16[256,1024]{1,0:T(8,128)(2,1)}, u32[]{:S(2)}) copy-start(bf16[256,1024]{1,0:T(8,128)(2,1)} %param.28) | copy-start | bytes 1572868
  7.2 88.9 %all-gather.5.cloned.1.call-start = ((), (), s32[]{:S(2)}) async-start(), calls=%async_computation.8 | async-start | bytes 5242880 | tf_op jit(solution)/shard_map/all_gather | solution.py:95
  12.5 216.8 %reduce-scatter.5.cloned.1.call-start = ((), (), s32[]{:S(2)}) async-start(), calls=%async_computation.9 | async-start | bytes 5242880 | tf_op jit(solution)/shard_map/reduce_scatter | solution.py:123
  153.8 75.5 %copy-start.4 = (bf16[512,1024]{1,0:T(8,128)(2,1)S(1)}, bf16[512,1024]{1,0:T(8,128)(2,1)}, u32[]{:S(2)}) copy-start(bf16[512,1024]{1,0:T(8,128)(2,1)} %param.23) | copy-start | bytes 3145732
  153.8 77.2 %copy-start.19 = (f32[1024]{0:T(1024)S(1)}, f32[1024]{0:T(1024)}, u32[]{:S(2)}) copy-start(f32[1024]{0:T(1024)} %param.30) | copy-start | bytes 12292
  153.8 302.2 %all-gather.7.cloned.1.call-start = ((), (), s32[]{:S(2)}) async-start(), calls=%async_computation.10 | async-start | bytes 13107200 | tf_op jit(solution)/shard_map/all_gather | solution.py:171
  273.1 367.1 %all-gather.9.cloned.1.call-start = ((), (), s32[]{:S(2)}) async-start(), calls=%async_computation.12 | async-start | bytes 13107200 | tf_op jit(solution)/shard_map/all_gather | solution.py:204
  318.7 542.9 %reduce-scatter.7.cloned.1.call-start = ((), (), s32[]{:S(2)}) async-start(), calls=%async_computation.11 | async-start | bytes 13107200 | tf_op jit(solution)/shard_map/reduce_scatter | solution.py:177
  685.2 358.3 %reduce-scatter.9.cloned.1.call-start = ((), (), s32[]{:S(2)}) async-start(), calls=%async_computation.13 | async-start | bytes 13107200 | tf_op jit(solution)/shard_map/reduce_scatter | solution.py:224
  866.8 182.0 %all-to-all-start.1 = ((bf16[320,4,1024]{2,1,0:T(4,128)(2,1)}), bf16[320,4,1024]{2,1,0:T(4,128)(2,1)}, u32[]{:S(2)}, u32[]{:S(2)}) async-start(bf16[320,4,1024]{2,1,0:T(4,128)(2,1)} %copy.115), calls=%async_computation.3 | async-start | bytes 5242880 | tf_op jit(solution)/shard_map/all_to_all | solution.py:185
  1048.8 36.7 %all-to-all-start.3 = ((bf16[320,4,1024]{2,1,0:T(4,128)(2,1)}), bf16[320,4,1024]{2,1,0:T(4,128)(2,1)}, u32[]{:S(2)}, u32[]{:S(2)}) async-start(bf16[320,4,1024]{2,1,0:T(4,128)(2,1)} %copy.120), calls=%async_computation.6 | async-start | bytes 5242880 | tf_op jit(solution)/shard_map/all_to_all | solution.py:233
  1053.2 132.1 %all-gather.11.cloned.1.call-start = ((), (), s32[]{:S(2)}) async-start(), calls=%async_computation.14 | async-start | bytes 5242880 | tf_op jit(solution)/shard_map/all_gather | solution.py:250
  1054.4 44.3 %copy-start.37 = (f32[32]{0:T(128)}, f32[32]{0:T(128)S(1)}, u32[]{:S(2)}) copy-start(f32[32]{0:T(128)S(1)} %get-tuple-element.320) | copy-start | bytes 388
  1054.4 44.3 %copy-start.24 = (f32[512]{0:T(512)}, f32[512]{0:T(512)S(1)}, u32[]{:S(2)}) copy-start(f32[512]{0:T(512)S(1)} %get-tuple-element.328) | copy-start | bytes 6148
  1070.9 27.8 %copy-start.33 = (f32[512]{0:T(512)}, f32[512]{0:T(512)S(1)}, u32[]{:S(2)}) copy-start(f32[512]{0:T(512)S(1)} %neg.17) | copy-start | bytes 6148
  1071.5 27.2 %copy-start.35 = (f32[512]{0:T(512)}, f32[512]{0:T(512)S(1)}, u32[]{:S(2)}) copy-start(f32[512]{0:T(512)S(1)} %get-tuple-element.316) | copy-start | bytes 6148
  1105.2 318.9 %all-reduce.7.cloned.1.call-start = ((), (), s32[]{:S(2)}) async-start(), calls=%async_computation.17 | async-start | bytes 4194304 | tf_op jit(solution)/shard_map/psum | solution.py:314
  1302.0 138.6 %reduce-scatter.11.cloned.1.call-start = ((), (), s32[]{:S(2)}) async-start(), calls=%async_computation.15 | async-start | bytes 5242880 | tf_op jit(solution)/shard_map/reduce_scatter | solution.py:301
  1309.9 259.6 %all-reduce.5.cloned.1.call-start = ((), (), s32[]{:S(2)}) async-start(), calls=%async_computation.16 | async-start | bytes 262144 | tf_op jit(solution)/shard_map/psum | solution.py:318
  1310.6 31.5 %slice-start = ((s8[10485760]{0:T(1024)(128)(4,1)}), s8[4194304]{0:T(1024)(128)(4,1)S(1)}, s32[]{:S(2)}) async-start(s8[10485760]{0:T(1024)(128)(4,1)} %bitcast.332), calls=%async_computation.18 | async-start | bytes 8388608
  1310.6 31.5 %slice-start.1 = ((s8[10485760]{0:T(1024)(128)(4,1)}), s8[4194304]{0:T(1024)(128)(4,1)S(1)}, s32[]{:S(2)}) async-start(s8[10485760]{0:T(1024)(128)(4,1)} %bitcast.332), calls=%async_computation.19 | async-start | bytes 8388608
  1310.7 31.5 %slice-start.3 = ((s8[7208960]{0:T(1024)(128)(4,1)}), s8[4194304]{0:T(1024)(128)(4,1)S(1)}, s32[]{:S(2)}) async-start(s8[7208960]{0:T(1024)(128)(4,1)} %bitcast.334), calls=%async_computation.21 | async-start | bytes 8388608
  1326.5 15.7 slice-start.2
  1326.5 15.7 slice-start.4
  1342.2 10.4 copy-start.25
  1342.2 10.4 copy-start.34
  1342.2 10.4 copy-start.36
  1424.1 16.6 %copy-start.18 = (f32[1024]{0:T(1024)S(1)}, f32[1024]{0:T(1024)}, u32[]{:S(2)}) copy-start(f32[1024]{0:T(1024)} %param.24) | copy-start | bytes 12292
  1424.1 16.6 %copy-start.21 = (f32[512]{0:T(512)S(1)}, f32[512]{0:T(512)}, u32[]{:S(2)}) copy-start(f32[512]{0:T(512)} %copy-done.20) | copy-start | bytes 6148
  1427.3 15.5 copy-start.27
  1427.3 15.5 copy-start.23
  1442.8 128.3 %copy-start.1 = (bf16[256,1024]{1,0:T(8,128)(2,1)S(1)}, bf16[256,1024]{1,0:T(8,128)(2,1)}, u32[]{:S(2)}) copy-start(bf16[256,1024]{1,0:T(8,128)(2,1)} %param.28) | copy-start | bytes 1572868
  (33 other events, 107.4 us)
Sparse Core Ops, SparseCore 0:
  12.6 83.4 all-gather.4
  153.9 75.3 reduce-scatter.4
  273.2 182.6 all-gather.6
  458.1 182.1 all-gather.8
  685.3 176.1 reduce-scatter.6
  864.5 179.0 reduce-scatter.8
  1105.3 80.0 all-gather.10
  1302.2 60.0 all-reduce.6
  1364.6 75.9 reduce-scatter.10
  1446.6 122.9 all-reduce.4
where the time goes:
time: 1590 us; the launch traced here: 1580 us
  waiting for transfers between devices  895 us (56%)
  matrix products  310 us (19%)
  local copies, waits for them, and re-layouts  153 us (10%)
  blocking collectives  126 us (8%)
  other arithmetic  67.1 us (4%)
  between operations  16.4 us (1%)
    reduce_scatter x1, waiting for transfers between devices, body(): lax.psum_scatter((through_gate + jnp.einsum('sef,edf->sed', up_low, w_up,...  172 us
    all_gather x1, waiting for transfers between devices, body(): owner_all = lax.all_gather(owner_grads, 'tensor', axis=0, tiled=True)  151 us
    reduce_scatter x1, waiting for transfers between devices, body(): lax.psum_scatter(jnp.einsum('sef,efd->sed', hidden, w_down, preferred_ele...  142 us
    all_gather x1, waiting for transfers between devices, slot_rows(): return lax.all_gather(local_slots, 'tensor', axis=0, tiled=True)  137 us
    psum x1, waiting for transfers between devices, body(): lax.psum((router_grad, gain_one_grad, gain_two_grad, jnp.stack([balance_p...  80.3 us
    all_gather x1, waiting for transfers between devices, body(): lax.all_gather(resid_grad.astype(jnp.bfloat16), 'tensor', axis=0, tiled=T...  79.9 us
    reduce_scatter x1, waiting for transfers between devices, body(): lax.psum_scatter(jnp.dot(attended, w_out, preferred_element_type=jnp.floa...  69 us
    psum x1, blocking collectives, body(): lax.psum((router_grad, gain_one_grad, gain_two_grad, jnp.stack([balance_p...  40.9 us
  transfers between devices with their start and end apart: 12, of which 10 were waited for; matrix products, arithmetic and copies ran while one was open for 17% of the time, Pallas kernels for 0%

commit v1 on v0

v1 whole, which is shorter than its diff:
```python
import functools

import jax
import jax.numpy as jnp
from jax import lax
from jax.experimental import pallas as pl
from jax.experimental.pallas import tpu as pltpu
from jax.sharding import PartitionSpec as P

HEAD_DIM = 64
TOP = 2
LANES = 128
MIB = 2**20

epsilon = 1e-06
balance_weight = 0.01
zloss_weight = 0.001
highest = lax.Precision.HIGHEST

BF = jnp.bfloat16
F32 = jnp.float32
NN = (((1,), (0,)), ((), ()))
NT = (((1,), (1,)), ((), ()))
TN = (((0,), (0,)), ((), ()))


def dot(left, right, dims=NN):
    return lax.dot_general(left, right, dims, preferred_element_type=F32)


def rms_scale(rows_in, gain):
    inverse = lax.rsqrt(jnp.mean(rows_in * rows_in, axis=-1, keepdims=True) + epsilon)
    return rows_in * inverse * gain


def lookup(row, index):
    table = jnp.broadcast_to(row, (index.shape[0], LANES))
    parts = [
        jnp.take_along_axis(table, index[:, at : at + LANES], axis=1)
        for at in range(0, index.shape[1], LANES)
    ]
    return jnp.concatenate(parts, axis=1)


def attend_kernel(q_ref, k_ref, v_ref, bucket_ref, table_ref, out_ref, prob_ref, *, tile):
    low = lax.broadcasted_iota(jnp.int32, (tile, LANES), 1) < HEAD_DIM
    for start in range(0, q_ref.shape[0], tile):
        rows = pl.ds(start, tile)
        query = q_ref[rows, :]
        mixed = []
        for head in range(2):
            part = jnp.where(low if head == 0 else ~low, query, jnp.zeros_like(query))
            scores = dot(part, k_ref[...], NT) * 0.125 + lookup(
                table_ref[0, head : head + 1, :], bucket_ref[rows, :]
            )
            scores = jnp.exp(scores - jnp.max(scores, axis=-1, keepdims=True))
            weights = (scores / jnp.sum(scores, axis=-1, keepdims=True)).astype(BF)
            prob_ref[head, rows, :] = weights
            mixed.append(dot(weights, v_ref[...]))
        out_ref[rows, :] = jnp.where(low, mixed[0], mixed[1]).astype(BF)


def attend(qkv, buckets, table):
    seq, cols = qkv.shape
    pairs = cols // (3 * LANES)

    def col(part):
        return pl.BlockSpec((seq, LANES), lambda p: (0, part * pairs + p))

    return pl.pallas_call(
        functools.partial(attend_kernel, tile=128),
        grid=(pairs,),
        in_specs=[
            col(0),
            col(1),
            col(2),
            pl.BlockSpec((seq, seq), lambda p: (0, 0)),
            pl.BlockSpec((1, 2, LANES), lambda p: (p, 0, 0)),
        ],
        out_specs=[col(0), pl.BlockSpec((2, seq, seq), lambda p: (p, 0, 0))],
        out_shape=[
            jax.ShapeDtypeStruct((seq, pairs * LANES), BF),
            jax.ShapeDtypeStruct((2 * pairs, seq, seq), BF),
        ],
        compiler_params=pltpu.CompilerParams(vmem_limit_bytes=40 * MIB),
        name="attend",
    )(qkv, qkv, qkv, buckets, table)


def attend_back_kernel(
    q_ref, k_ref, v_ref, grad_ref, prob_ref, dq_ref, dk_ref, dv_ref, score_ref, *, tile
):
    seq = q_ref.shape[0]
    low = lax.broadcasted_iota(jnp.int32, (tile, LANES), 1) < HEAD_DIM
    for start in range(0, seq, tile):
        rows = pl.ds(start, tile)
        grad = grad_ref[rows, :]
        back = []
        for head in range(2):
            part = jnp.where(low if head == 0 else ~low, grad, jnp.zeros_like(grad))
            weights = prob_ref[head, rows, :].astype(F32)
            weight_grad = dot(part, v_ref[...], NT)
            score = weights * (
                weight_grad - jnp.sum(weights * weight_grad, axis=-1, keepdims=True)
            )
            score = score.astype(BF)
            score_ref[head, rows, :] = score
            back.append(dot(score, k_ref[...]))
        dq_ref[rows, :] = (jnp.where(low, back[0], back[1]) * 0.125).astype(BF)
    wide = lax.broadcasted_iota(jnp.int32, (seq, LANES), 1) < HEAD_DIM
    keys = [dot(score_ref[head], q_ref[...], TN) for head in range(2)]
    dk_ref[...] = (jnp.where(wide, keys[0], keys[1]) * 0.125).astype(BF)
    vals = [dot(prob_ref[head], grad_ref[...], TN) for head in range(2)]
    dv_ref[...] = jnp.where(wide, vals[0], vals[1]).astype(BF)


def attend_back(qkv, grad, probs):
    seq, cols = qkv.shape
    pairs = cols // (3 * LANES)

    def col(part):
        return pl.BlockSpec((seq, LANES), lambda p: (0, part * pairs + p))

    square = pl.BlockSpec((2, seq, seq), lambda p: (p, 0, 0))
    return pl.pallas_call(
        functools.partial(attend_back_kernel, tile=128),
        grid=(pairs,),
        in_specs=[col(0), col(1), col(2), col(0), square],
        out_specs=[col(0), col(0), col(0), square],
        out_shape=[jax.ShapeDtypeStruct((seq, pairs * LANES), BF)] * 3
        + [jax.ShapeDtypeStruct((2 * pairs, seq, seq), BF)],
        compiler_params=pltpu.CompilerParams(vmem_limit_bytes=40 * MIB),
        name="attend_back",
    )(qkv, qkv, qkv, grad, probs)


def table_kernel(*refs, count):
    *score_refs, bucket_ref, out_ref = refs
    marks = bucket_ref[...]
    tile, seq = marks.shape
    ids = lax.broadcasted_iota(jnp.int32, (tile, count, seq), 1)
    onehot = (jnp.broadcast_to(marks[:, None, :], ids.shape) == ids).astype(F32)
    onehot = onehot.astype(BF).reshape(tile * count, seq)

    @pl.when(pl.program_id(0) == 0)
    def _():
        out_ref[...] = jnp.zeros_like(out_ref)

    at = 0
    for ref in score_refs:
        block = ref[...].reshape(ref.shape[0] * tile, seq)
        out_ref[at : at + block.shape[0], :] += dot(block, onehot, NT)
        at += block.shape[0]


def table_back(scores, buckets, count):
    seq = buckets.shape[0]
    heads = sum(s.shape[0] for s in scores)
    tile = 16
    sums = pl.pallas_call(
        functools.partial(table_kernel, count=count),
        grid=(seq // tile,),
        in_specs=[pl.BlockSpec((s.shape[0], tile, seq), lambda i: (0, i, 0)) for s in scores]
        + [pl.BlockSpec((tile, seq), lambda i: (i, 0))],
        out_specs=pl.BlockSpec((heads * tile, tile * count), lambda i: (0, 0)),
        out_shape=jax.ShapeDtypeStruct((heads * tile, tile * count), F32),
        compiler_params=pltpu.CompilerParams(vmem_limit_bytes=40 * MIB),
        name="table_back",
    )(*scores, buckets)
    sums = sums.reshape(heads, tile, tile, count)
    same = jnp.eye(tile, dtype=F32)[None, :, :, None]
    return jnp.sum(sums * same, axis=(1, 2)).T


def flat(ref):
    block = ref[...]
    return block.astype(F32).reshape(-1, block.shape[-1]).astype(BF)


def expert_kernel(
    base_ref,
    x_ref,
    g_ref,
    other_ref,
    gate_ref,
    up_ref,
    down_ref,
    router_ref,
    out_ref,
    back_ref,
    hidden_ref,
    gate_back_ref,
    up_back_ref,
    route_ref,
):
    expert = pl.program_id(0)
    x = flat(x_ref)
    g = flat(g_ref)
    lanes = lax.broadcasted_iota(jnp.int32, (x.shape[0], LANES), 1)
    sign = (lanes == base_ref[0] + expert).astype(F32) - (lanes == other_ref[0]).astype(F32)
    logits = dot(x, router_ref[...])
    apart = jnp.sum(sign * (logits[:, :LANES] + logits[:, LANES:]), axis=-1, keepdims=True)
    weight = 1.0 / (1.0 + jnp.exp(-apart))
    gate = dot(x, gate_ref[0], NT)
    up = dot(x, up_ref[0], NT)
    grad = dot(g, down_ref[0], NT)
    scale = 0.7978845608028654
    square = gate * gate
    bent = jnp.tanh(scale * gate * (1.0 + 0.044715 * square))
    half = 0.5 + 0.5 * bent
    act = gate * half
    slope = half + 0.5 * gate * (1.0 - bent * bent) * (scale + 3 * 0.044715 * scale * square)
    hidden = act * up
    mark = weight * (1.0 - weight) * jnp.sum(hidden * grad, axis=-1, keepdims=True)
    mark = (mark * sign).astype(BF)
    grad = grad * weight
    up_back = (grad * act).astype(BF)
    gate_back = (grad * up * slope).astype(BF)
    hidden_ref[0] = (hidden * weight).astype(BF)
    gate_back_ref[0] = gate_back
    up_back_ref[0] = up_back
    out = dot(hidden.astype(BF), down_ref[0]) * weight
    out_ref[...] = out.reshape(out_ref.shape).astype(BF)
    back = dot(gate_back, gate_ref[0]) + dot(up_back, up_ref[0])
    back += dot(mark, router_ref[:, :LANES], NT)
    back_ref[...] = back.reshape(back_ref.shape).astype(BF)
    part = dot(mark, x, TN)

    @pl.when(expert == 0)
    def _():
        route_ref[...] = jnp.zeros_like(route_ref)

    route_ref[...] += part


def expert_chunk(base, x, g, other, gate_w, up_w, down_w, router_pair):
    sources, here, slots, width = x.shape
    hidden = down_w.shape[1]
    count = sources * slots
    rows = pl.BlockSpec((sources, 1, slots, width), lambda e: (0, e, 0, 0))
    middle = pl.BlockSpec((1, count, hidden), lambda e: (e, 0, 0))
    weights = pl.BlockSpec((1, hidden, width), lambda e: (e, 0, 0))
    return pl.pallas_call(
        expert_kernel,
        grid=(here,),
        in_specs=[
            pl.BlockSpec(memory_space=pltpu.SMEM),
            rows,
            rows,
            pl.BlockSpec((1, count, 1), lambda e: (e, 0, 0)),
            weights,
            weights,
            weights,
            pl.BlockSpec((width, 2 * LANES), lambda e: (0, 0)),
        ],
        out_specs=[rows, rows, middle, middle, middle, pl.BlockSpec((LANES, width), lambda e: (0, 0))],
        out_shape=[jax.ShapeDtypeStruct(x.shape, BF)] * 2
        + [jax.ShapeDtypeStruct((here, count, hidden), BF)] * 3
        + [jax.ShapeDtypeStruct((LANES, width), F32)],
        compiler_params=pltpu.CompilerParams(vmem_limit_bytes=56 * MIB),
        name="experts",
    )(base, x, g, other, gate_w, up_w, down_w, router_pair)


def weight_kernel(*refs, chunks):
    xs, gs, hidden, gates, ups = (refs[i * chunks : (i + 1) * chunks] for i in range(5))
    gate_ref, up_ref, down_ref = refs[5 * chunks :]
    x = jnp.concatenate([flat(ref) for ref in xs], 0)
    gate_ref[0] = dot(jnp.concatenate([ref[0] for ref in gates], 0), x, TN)
    up_ref[0] = dot(jnp.concatenate([ref[0] for ref in ups], 0), x, TN)
    g = jnp.concatenate([flat(ref) for ref in gs], 0)
    down_ref[0] = dot(jnp.concatenate([ref[0] for ref in hidden], 0), g, TN)


def weight_grads(xs, gs, hidden, gates, ups):
    sources, here, slots, width = xs[0].shape
    depth = hidden[0].shape[2]
    rows = pl.BlockSpec((sources, 1, slots, width), lambda e: (0, e, 0, 0))
    middle = pl.BlockSpec((1, sources * slots, depth), lambda e: (e, 0, 0))
    chunks = len(xs)
    return pl.pallas_call(
        functools.partial(weight_kernel, chunks=chunks),
        grid=(here,),
        in_specs=[rows] * (2 * chunks) + [middle] * (3 * chunks),
        out_specs=[pl.BlockSpec((1, depth, width), lambda e: (e, 0, 0))] * 3,
        out_shape=[jax.ShapeDtypeStruct((here, depth, width), F32)] * 3,
        compiler_params=pltpu.CompilerParams(vmem_limit_bytes=58 * MIB),
        name="expert_weight_grads",
    )(*xs, *gs, *hidden, *gates, *ups)


def body(
    n_expert,
    n_tensor,
    inputs,
    gain_one,
    w_query,
    w_key,
    w_value,
    w_out,
    rel_table,
    gain_two,
    router,
    w_gate,
    w_up,
    w_down,
    routes,
    buckets,
    grad_out,
):
    rows, width = inputs.shape
    experts = router.shape[1]
    here = w_gate.shape[0]
    tokens = routes.shape[0]
    cap = (5 * rows * TOP + 4 * experts - 1) // (4 * experts)
    seq = buckets.shape[0]
    share = seq // rows
    count = rel_table.shape[0]
    head_cols = w_query.shape[1]
    at_expert = lax.axis_index("expert")
    at_tensor = lax.axis_index("tensor")
    both = ("tensor", "expert")

    def swap(value, step):
        return lax.ppermute(value, "tensor", [(i, i ^ step) for i in range(n_tensor)])

    def exchange(value):
        return lax.all_to_all(value, "expert", split_axis=0, concat_axis=0, tiled=True)

    packed = jnp.concatenate([w_query, w_key, w_value, w_out.T], 1)
    strip = width // n_expert
    packed = lax.dynamic_slice_in_dim(packed, at_expert * strip, strip, 0)
    attn_w = lax.all_gather(packed, both, axis=0, tiled=True).reshape(n_tensor, width, 4 * head_cols)
    table_all = lax.all_gather(rel_table.T, "tensor", axis=0, tiled=True)

    labels = jnp.arange(experts, dtype=jnp.int32)
    grouped = routes.T.reshape(TOP, n_expert * n_tensor, rows)
    marks = (grouped[:, :, None, :] == labels[:, None]).astype(BF)
    order = jnp.arange(rows, dtype=jnp.int32)
    earlier = (order[:, None] < order[None, :]).astype(BF)
    ahead = jnp.einsum("kges,st->kget", marks, earlier, preferred_element_type=F32)
    first_count = jnp.sum(marks[0].astype(F32), axis=-1, keepdims=True)
    ahead = ahead + jnp.stack([jnp.zeros_like(first_count), first_count])
    places = jnp.sum(ahead * marks.astype(F32), axis=2).astype(jnp.int32)
    slot_ids = jnp.where(places < cap, grouped * cap + places, -1)
    slot_ids = slot_ids.reshape(TOP, n_expert, n_tensor, rows)
    choices = grouped.reshape(TOP, n_expert, n_tensor, rows)
    local = slot_ids - at_expert * (here * cap)
    slot_here = jnp.arange(here * cap, dtype=jnp.int32)[:, None]
    partner = jnp.sum(
        jnp.where(local[0][:, :, None, :] == slot_here, choices[1][:, :, None, :], 0)
        + jnp.where(local[1][:, :, None, :] == slot_here, choices[0][:, :, None, :], 0),
        axis=-1,
    ).reshape(n_expert, n_tensor, here, cap)
    slot_all = jnp.arange(experts * cap, dtype=jnp.int32)[:, None]
    own_ids = lax.dynamic_index_in_dim(slot_ids, at_expert, 1, keepdims=False)
    tables, partners = [], []
    for step in range(n_tensor):
        ids = lax.dynamic_index_in_dim(own_ids, at_tensor ^ step, 1, keepdims=False)
        tables.append(((ids[0] == slot_all) | (ids[1] == slot_all)).astype(BF))
        pick = lax.dynamic_index_in_dim(partner, at_tensor ^ step, 1, keepdims=False)
        partners.append(jnp.transpose(pick, (1, 0, 2)).reshape(here, n_expert * cap, 1))

    def dispatch(value):
        def buffer(table, part):
            return exchange(dot(table, part).astype(BF).reshape(n_expert, here, cap, width))

        far = [swap(value, step) for step in range(2, n_tensor)]
        own = buffer(tables[0], value)
        return [own, swap(own, 1)] + [
            buffer(tables[step], part) for step, part in zip(range(2, n_tensor), far)
        ]

    def collect(parts):
        total = None
        for step in list(range(n_tensor - 1, 1, -1)):
            back = exchange(parts[step]).reshape(experts * cap, width)
            mixed = swap(dot(tables[step], back, TN).astype(BF), step).astype(F32)
            total = mixed if total is None else total + mixed
        near = (parts[0].astype(F32) + swap(parts[1], 1).astype(F32)).astype(BF)
        near = dot(tables[0], exchange(near).reshape(experts * cap, width), TN)
        return near if total is None else near + total

    def whole_seq(value):
        if share == 1:
            return value
        groups = [[i * share + j for j in range(share)] for i in range(n_tensor // share)]
        return lax.all_gather(value, "tensor", axis=0, tiled=True, axis_index_groups=groups)

    def own_rows(value):
        if share == 1:
            return value
        return lax.dynamic_slice_in_dim(value, (at_tensor % share) * rows, rows, 0)

    grad_slots = dispatch(grad_out)

    inputs_f = inputs.astype(F32)
    normed_one = rms_scale(inputs_f, gain_one).astype(BF)
    attn_in = whole_seq(normed_one)
    pairs = head_cols // LANES
    bias_rows = jnp.pad(table_all, ((0, 0), (0, LANES - count)))
    bias_rows = bias_rows.reshape(n_tensor, pairs, 2, LANES)
    qkv, probs, attended = [], [], []
    resid = inputs_f
    for group in range(n_tensor):
        projected = dot(attn_in, attn_w[group, :, : 3 * head_cols]).astype(BF)
        mixed, weights = attend(projected, buckets, bias_rows[group])
        mixed = own_rows(mixed)
        qkv.append(projected)
        probs.append(weights)
        attended.append(mixed)
        resid = resid + dot(mixed, attn_w[group, :, 3 * head_cols :], NT)

    normed_two = rms_scale(resid, gain_two)
    token_slots = dispatch(normed_two.astype(BF))

    counts = jnp.sum((routes.T[:, None, :] == labels[:, None]).astype(F32), axis=(0, 2))
    route_share = counts / (tokens * TOP)

    def losses(normed, router_w):
        logits = jnp.dot(normed, router_w, precision=highest)
        router_probs = jax.nn.softmax(logits, axis=-1)
        log_totals = jax.nn.logsumexp(logits, axis=-1)
        balance = experts * jnp.sum(route_share * jnp.sum(router_probs, axis=0)) / tokens
        return balance, jnp.sum(log_totals * log_totals) / tokens

    (balance_part, zloss_part), losses_back = jax.vjp(losses, normed_two, router)
    normed_grad, router_grad = losses_back(
        (jnp.asarray(balance_weight, F32), jnp.asarray(zloss_weight, F32))
    )

    router_high = router.astype(BF)
    router_low = (router - router_high.astype(F32)).astype(BF)
    fill = ((0, 0), (0, LANES - experts))
    router_pair = jnp.concatenate([jnp.pad(router_high, fill), jnp.pad(router_low, fill)], 1)
    base = jnp.full((1,), at_expert * here, jnp.int32)
    gate_w = jnp.swapaxes(w_gate, 1, 2)
    up_w = jnp.swapaxes(w_up, 1, 2)

    def rows_in(value):
        if cap % 8 == 0:
            return value
        return jnp.swapaxes(value, 0, 1).reshape(1, here, n_expert * cap, width)

    def rows_out(value):
        if cap % 8 == 0:
            return value
        return jnp.swapaxes(value.reshape(here, n_expert, cap, width), 0, 1)

    token_slots = [rows_in(v) for v in token_slots]
    grad_slots = [rows_in(v) for v in grad_slots]
    done = [
        expert_chunk(base, x, g, other, gate_w, up_w, w_down, router_pair)
        for x, g, other in zip(token_slots, grad_slots, partners)
    ]
    moe_grad = collect([rows_out(d[1]) for d in done])
    mixture = collect([rows_out(d[0]) for d in done])
    router_grad = router_grad + sum(d[5] for d in done)[:experts].T
    gate_grad, up_grad, down_grad = weight_grads(
        token_slots, grad_slots, [d[2] for d in done], [d[3] for d in done], [d[4] for d in done]
    )

    grad_f = grad_out.astype(F32)
    resid_norm_grad, gain_two_grad = jax.vjp(rms_scale, resid, gain_two)[1](normed_grad + moe_grad)
    resid_grad = grad_f + resid_norm_grad
    attn_grad = resid_grad.astype(BF)
    attn_grad_seq = whole_seq(attn_grad)

    normed_one_grad = jnp.zeros((rows, width), F32)
    scattered, score_grads = [], []
    for group in range(n_tensor):
        out_w = attn_w[group, :, 3 * head_cols :]
        mixed_grad = dot(attn_grad_seq, out_w).astype(BF)
        *parts, score = attend_back(qkv[group], mixed_grad, probs[group])
        score_grads.append(score)
        back = own_rows(jnp.concatenate(parts, 1))
        normed_one_grad = normed_one_grad + dot(back, attn_w[group, :, : 3 * head_cols], NT)
        weight_part = jnp.concatenate(
            [dot(normed_one, back, TN).astype(BF), dot(attn_grad, attended[group], TN).astype(BF)], 1
        )
        scattered.append(lax.psum_scatter(weight_part, "expert", scatter_dimension=0, tiled=True))
    summed = lax.psum_scatter(jnp.stack(scattered), "tensor", scatter_dimension=0, tiled=False)
    attn_w_grad = lax.all_gather(summed, "expert", axis=0, tiled=True).astype(F32)

    input_norm_grad, gain_one_grad = jax.vjp(rms_scale, inputs_f, gain_one)[1](normed_one_grad)
    input_grad = resid_grad + input_norm_grad
    table_grad = table_back(score_grads, buckets, count) / share
    output = (resid + mixture).astype(BF)

    small = lax.psum(
        (router_grad, gain_one_grad, gain_two_grad, jnp.stack([balance_part, zloss_part]), table_grad),
        ("expert", "tensor"),
    )
    router_total, gain_one_total, gain_two_total, loss_total, table_total = small
    table_own = lax.dynamic_slice_in_dim(
        table_total, at_tensor * rel_table.shape[1], rel_table.shape[1], 1
    )
    return (
        output,
        input_grad,
        gain_one_total,
        attn_w_grad[:, :head_cols],
        attn_w_grad[:, head_cols : 2 * head_cols],
        attn_w_grad[:, 2 * head_cols : 3 * head_cols],
        attn_w_grad[:, 3 * head_cols :].T,
        table_own,
        gain_two_total,
        router_total,
        jnp.swapaxes(gate_grad, 1, 2),
        jnp.swapaxes(up_grad, 1, 2),
        down_grad,
        loss_total,
    )


def solution(mesh):
    return jax.shard_map(
        functools.partial(body, mesh.shape["expert"], mesh.shape["tensor"]),
        mesh=mesh,
        in_specs=(
            P(("expert", "tensor"), None),
            P(),
            P(None, "tensor"),
            P(None, "tensor"),
            P(None, "tensor"),
            P("tensor", None),
            P(None, "tensor"),
            P(),
            P(),
            P("expert", None, "tensor"),
            P("expert", None, "tensor"),
            P("expert", "tensor", None),
            P(),
            P(),
            P(("expert", "tensor"), None),
        ),
        out_specs=(
            P(("expert", "tensor"), None),
            P(("expert", "tensor"), None),
            P(),
            P(None, "tensor"),
            P(None, "tensor"),
            P(None, "tensor"),
            P("tensor", None),
            P(None, "tensor"),
            P(),
            P(),
            P("expert", None, "tensor"),
            P("expert", None, "tensor"),
            P("expert", "tensor", None),
            P(),
        ),
        check_vma=False,
    )
```

time: 1590 us -> 1150 us (0.72)
  waiting for transfers between devices: 895 us -> 527 us
  matrix products: 310 us -> 100 us
  Pallas kernels: 0 us -> 196 us
  starting transfers between devices: 10.4 us -> 92.1 us
  local copies, waits for them, and re-layouts: 153 us -> 85.4 us
  blocking collectives: 126 us -> 78 us
  other arithmetic: 67.1 us -> 41.1 us
    all_gather x4 -> x2, waiting for transfers between devices: 405 us -> 0.01 us  [the longest x1 0.01 us: body(): lax.all_gather(packed, both, axis=0, tiled=True)]
    reduce_scatter x4 -> x1, waiting for transfers between devices: 395 us -> 23.2 us  [body(): lax.psum_scatter(jnp.stack(scattered), 'tensor', scatter_dimension=0, til...]
    ppermute x0 -> x12, waiting for transfers between devices: none -> 330 us  [swap(): lax.ppermute(value, 'tensor', [(i, i ^ step) for i in range(n_tensor)])]
    dot_general x82 -> x40, matrix products: 310 us -> 100 us  [the longest x36 87.4 us: dot(): return lax.dot_general(left, right, dims, preferred_element_type=F32)]
    pallas_call x0 -> x14, Pallas kernels: none -> 196 us  [the longest x4 83.5 us: expert_chunk(): pl.pallas_call(expert_kernel, grid=(here,), in_specs=[pl.BlockSpec(memory...]
    unnamed x10 -> x12, waiting for transfers between devices: 0.16 us -> 140 us
    all_to_all x2 -> x0, blocking collectives: 70.3 us -> none  [the longest x1 35.6 us: body(): lax.all_to_all(send_buffer.reshape(capacity, experts, width), 'expert', s...]
    psum x1, waiting for transfers between devices: 80.3 us -> 23.1 us  [body(): lax.psum((router_grad, gain_one_grad, gain_two_grad, jnp.stack([balance_p...]
  transfers between devices with their start and end apart: 12 -> 32, of which waited for: 10 -> 16; matrix products, arithmetic and copies ran while one was open for 17% -> 16% of each run, Pallas kernels for 0% -> 17%
where the time goes in v1:
time: 1150 us; the launch traced here: 1140 us
  waiting for transfers between devices  527 us (46%)
  Pallas kernels  196 us (17%)
  matrix products  100 us (9%)
  starting transfers between devices  92.1 us (8%)
  local copies, waits for them, and re-layouts  85.4 us (7%)
  blocking collectives  78 us (7%)
  other arithmetic  41.1 us (4%)
  between operations  17.6 us (2%)
    ppermute x12, waiting for transfers between devices, swap(): lax.ppermute(value, 'tensor', [(i, i ^ step) for i in range(n_tensor)])  330 us
    unnamed x12, waiting for transfers between devices  140 us
    dot_general x36, matrix products, dot(): return lax.dot_general(left, right, dims, preferred_element_type=F32)  87.4 us
    pallas_call x4, Pallas kernels, expert_chunk(): pl.pallas_call(expert_kernel, grid=(here,), in_specs=[pl.BlockSpec(memory...  83.5 us
    all_to_all x12, starting transfers between devices, exchange(): lax.all_to_all(value, 'expert', split_axis=0, concat_axis=0, tiled=True)  55.5 us
    unnamed x217, local copies, waits for them, and re-layouts  47.2 us
    psum x1, blocking collectives, body(): lax.psum((router_grad, gain_one_grad, gain_two_grad, jnp.stack([balance_p...  39.7 us
    all_gather x1, blocking collectives, body(): table_all = lax.all_gather(rel_table.T, 'tensor', axis=0, tiled=True)  38.3 us
  transfers between devices with their start and end apart: 32, of which 16 were waited for; matrix products, arithmetic and copies ran while one was open for 16% of the time, Pallas kernels for 17%

profile of v1, /device:TPU:0, one launch (start us, length us, event | category | flops | bytes accessed | tf_op | source)
XLA Modules:
  0.0 1137.6 jit_solution(4672256690054209494)
XLA Ops:
  27.3 100.5 %collective-permute-done.7 = bf16[512,1024]{1,0:T(8,128)(2,1)S(1)} collective-permute-done((bf16[512,1024]{1,0:T(8,128)(2,1)}, bf16[512,1024]{1,0:T(8,128)(2,1)S(1)}, u32[]{:S(2)}, u32[]{:S(2)}) %collective-permute-start.7) | collective-permute-done | bytes 1048608 | tf_op jit(solution)/shard_map/ppermute | solution.py:325
  137.2 38.3 %all-gather.1 = f32[4,4,32]{2,1,0:T(4,128)S(1)} all-gather(f32[1,4,32]{2,1,0:T(4,128)S(1)} %bitcast.218), channel_id=1, replica_groups=mesh['expert'=8,'tensor'=4] {'tensor'}, dimensions={0}, use_global_device_ids=true | all-gather | bytes 2560 | tf_op jit(solution)/shard_map/all_gather | solution.py:334
  181.3 12.0 %copy.105 = bf16[4096,1024]{1,0:T(8,128)(2,1)} copy(bf16[4096,1024]{0,1:T(8,128)(2,1)} %all-gather.5.cloned.1.call-done) | data formatting | bytes 16777216 | tf_op jit(solution)/shard_map/all_gather | solution.py:333
  208.1 6.8 attend.7
  216.3 6.8 attend.6
  224.4 6.8 attend.5
  232.5 7.0 attend.4
  256.6 46.1 %collective-permute-done.6 = bf16[512,1024]{1,0:T(8,128)(2,1)S(1)} collective-permute-done((bf16[512,1024]{1,0:T(8,128)(2,1)}, bf16[512,1024]{1,0:T(8,128)(2,1)S(1)}, u32[]{:S(2)}, u32[]{:S(2)}) %collective-permute-start.6) | collective-permute-done | bytes 1048608 | tf_op jit(solution)/shard_map/ppermute | solution.py:325
  312.9 24.8 %collective-permute-done.3 = bf16[512,1024]{1,0:T(8,128)(2,1)S(1)} collective-permute-done((bf16[512,1024]{1,0:T(8,128)(2,1)}, bf16[512,1024]{1,0:T(8,128)(2,1)S(1)}, u32[]{:S(2)}, u32[]{:S(2)}) %collective-permute-start.3) | collective-permute-done | bytes 1048608 | tf_op jit(solution)/shard_map/ppermute | solution.py:325
  354.8 18.9 %collective-permute-start.1 = (bf16[8,4,40,1024]{3,2,1,0:T(8,128)(2,1)}, bf16[8,4,40,1024]{3,2,1,0:T(8,128)(2,1)}, u32[]{:S(2)}, u32[]{:S(2)}) collective-permute-start(bf16[8,4,40,1024]{3,2,1,0:T(8,128)(2,1)} %copy-done.28), channel_id=1, source_target_pairs={{0,1},{1,0},{2,3},{3,2},{4,5},{5,4},{6,7},{7,6},{8,9},{9,8},{10,11... | collective-permute-start | bytes 7864328 | tf_op jit(solution)/shard_map/ppermute | solution.py:325
  387.8 20.9 %experts.7 = (bf16[8,4,40,1024]{3,2,1,0:T(8,128)(2,1)}, bf16[8,4,40,1024]{3,2,1,0:T(8,128)(2,1)}, bf16[4,320,704]{2,1,0:T(8,128)(2,1)}, bf16[4,320,704]{2,1,0:T(...) custom-call(s32[1]{0:T(128)} %bitcast.24.base_ref, ...), custom_call_target="tpu_custom_call" | custom-call | tf_op jit(solution)/shard_map/experts/pallas_call | solution.py:243
  416.4 15.3 %collective-permute-done.1.g_ref.refs_5_ = bf16[8,4,40,1024]{3,2,1,0:T(8,128)(2,1)} collective-permute-done((bf16[8,4,40,1024]{3,2,1,0:T(8,128)(2,1)}, bf16[8,4,40,1024]{3,2,1,0:T(8,128)(2,1)}, u32[]{:S(2)}, u32[]{:S(2)}) %collective-permute-start.1) | collective-permute-done | bytes 2621472 | tf_op jit(solution)/shard_map/ppermute | solution.py:325
  431.8 55.9 %collective-permute-done.x_ref.refs_1_ = bf16[8,4,40,1024]{3,2,1,0:T(8,128)(2,1)} collective-permute-done((bf16[8,4,40,1024]{3,2,1,0:T(8,128)(2,1)}, bf16[8,4,40,1024]{3,2,1,0:T(8,128)(2,1)}, u32[]{:S(2)}, u32[]{:S(2)}) %collective-permute-start) | collective-permute-done | bytes 2621472 | tf_op jit(solution)/shard_map/ppermute | solution.py:325
  487.7 20.9 %experts.5 = (bf16[8,4,40,1024]{3,2,1,0:T(8,128)(2,1)}, bf16[8,4,40,1024]{3,2,1,0:T(8,128)(2,1)}, bf16[4,320,704]{2,1,0:T(8,128)(2,1)}, bf16[4,320,704]{2,1,0:T(...) custom-call(s32[1]{0:T(128)} %bitcast.24.base_ref, ...), custom_call_target="tpu_custom_call" | custom-call | tf_op jit(solution)/shard_map/experts/pallas_call | solution.py:243
  512.8 20.9 %experts.6 = (bf16[8,4,40,1024]{3,2,1,0:T(8,128)(2,1)}, bf16[8,4,40,1024]{3,2,1,0:T(8,128)(2,1)}, bf16[4,320,704]{2,1,0:T(8,128)(2,1)}, bf16[4,320,704]{2,1,0:T(...) custom-call(s32[1]{0:T(128)} %bitcast.24.base_ref, ...), custom_call_target="tpu_custom_call" | custom-call | tf_op jit(solution)/shard_map/experts/pallas_call | solution.py:243
  542.8 20.9 %experts.4 = (bf16[8,4,40,1024]{3,2,1,0:T(8,128)(2,1)}, bf16[8,4,40,1024]{3,2,1,0:T(8,128)(2,1)}, bf16[4,320,704]{2,1,0:T(8,128)(2,1)}, bf16[4,320,704]{2,1,0:T(...) custom-call(s32[1]{0:T(128)} %bitcast.24.base_ref, bf16[8,4,40,1024]{3,2,1,0:T(8,128)(2,1)} %all-to-all-done.x_ref.refs_0_, ...), custom_call_target="tpu_custom_call" | custom-call | tf_op jit(solution)/shard_map/experts/pallas_call | solution.py:243
  596.8 60.0 %collective-permute-done.11 = bf16[512,1024]{1,0:T(8,128)(2,1)S(1)} collective-permute-done((bf16[512,1024]{1,0:T(8,128)(2,1)S(1)}, bf16[512,1024]{1,0:T(8,128)(2,1)S(1)}, u32[]{:S(2)}, u32[]{:S(2)}) %collective-permute-start.11) | collective-permute-done | bytes 1048608 | tf_op jit(solution)/shard_map/ppermute | solution.py:325
  668.0 6.4 attend_back.7
  684.4 5.9 attend_back.6
  700.7 6.1 attend_back.5
  718.7 5.9 attend_back.4
  732.8 9.4 reduce-scatter.22.cloned.1.call-done
  743.3 43.8 %reduce-scatter.20.cloned.1.call-done = bf16[128,1024]{1,0:T(8,128)(2,1)} async-done(((bf16[1024,1024]{1,0:T(8,128)(2,1)}), bf16[128,1024]{1,0:T(8,128)(2,1)}) %reduce-scatter.20.cloned.1.call-update) | async-done | bytes 262160
  788.2 43.3 %reduce-scatter.18.cloned.1.call-done = bf16[128,1024]{1,0:T(8,128)(2,1)} async-done(((bf16[1024,1024]{1,0:T(8,128)(2,1)}), bf16[128,1024]{1,0:T(8,128)(2,1)}) %reduce-scatter.18.cloned.1.call-update) | async-done | bytes 262160
  832.6 43.6 %reduce-scatter.16.cloned.1.call-done = bf16[128,1024]{1,0:T(8,128)(2,1)} async-done(((bf16[1024,1024]{1,0:T(8,128)(2,1)}), bf16[128,1024]{1,0:T(8,128)(2,1)}) %reduce-scatter.16.cloned.1.call-update) | async-done | bytes 262160
  882.9 23.2 %reduce-scatter.14.cloned.1.call-done = bf16[1,128,1024]{1,2,0:T(8,128)(2,1)} async-done(((bf16[4,128,1024]{1,2,0:T(8,128)(2,1)}), bf16[1,128,1024]{1,2,0:T(8,128)(2,1)}) %reduce-scatter.14.cloned.1.call-update) | async-done | bytes 262160 | tf_op jit(solution)/shard_map/reduce_scatter | solution.py:482
  906.1 9.0 all-to-all-done.8
  927.4 31.5 %expert_weight_grads.1 = (f32[4,704,1024]{2,1,0:T(8,128)}, f32[4,704,1024]{2,1,0:T(8,128)}, f32[4,704,1024]{2,1,0:T(8,128)}) custom-call(bf16[8,4,40,1024]{3,2,1,0:T(8,128)(2,1)} %all-to-all-done.x_ref.refs_0_, bf16[8,4,40,1024]{3,2,1,0:T(8,128)(2,1)} %collective-permute-done.x_ref.refs_1_, bf16[8,4,40,1024]{3,2,1,0:T(8,128)(2,1)} %all-to-all-done.6.x_ref.refs_2_, ...), custom_call_target="tpu_custom_call" | custom-call | tf_op jit(solution)/shard_map/expert_weight_grads/pallas_call | solution.py:281
  970.6 23.4 %collective-permute-done.2 = bf16[8,4,40,1024]{3,2,1,0:T(8,128)(2,1)} collective-permute-done((bf16[8,4,40,1024]{3,2,1,0:T(8,128)(2,1)}, bf16[8,4,40,1024]{3,2,1,0:T(8,128)(2,1)}, u32[]{:S(2)}, u32[]{:S(2)}) %collective-permute-start.2) | collective-permute-done | bytes 2621472 | tf_op jit(solution)/shard_map/ppermute | solution.py:325
  1015.2 28.9 %table_back.1 = f32[256,512]{1,0:T(8,128)S(1)} custom-call(bf16[4,512,512]{2,1,0:T(8,128)(2,1)S(1)} %get-tuple-element.93.refs_0_, bf16[4,512,512]{2,1,0:T(8,128)(2,1)S(1)} %copy-done.7, bf16[4,512,512]{2,1,0:T(8,128)(2,1)S(1)} %copy-done.5, bf16[4,512,512]{2,1,0:T(8,128)(2,1)S(1)} %copy-done.3, s32[512,512]{1,0:T(8,128)S(1)} %copy-done.1), custom_call_target="tpu_custom_call" | custom-call | tf_op jit(solution)/shard_map/table_back/pallas_call | solution.py:160
  1048.0 39.7 %all-reduce.4 = (f32[1024]{0:T(1024)}, f32[32,16]{0,1:T(8,128)S(1)}, f32[1024]{0:T(1024)}, f32[2]{0:T(128)}) all-reduce(f32[1024]{0:T(1024)S(1)} %get-tuple-element.202, f32[32,16]{0,1:T(8,128)S(1)} %bitcast.216, f32[1024]{0:T(1024)S(1)} %get-tuple-element.200, ...), channel_id=1, replica_groups=mesh['expert'=8,'tensor'=4] {'expert','tensor'}, use_global_device_ids=true, to_apply=%region_13.14 | all-reduce | flops 2562 | bytes 20496 | tf_op jit(solution)/shard_map/psum | solution.py:490
  1105.6 23.1 %all-reduce.7.cloned.1.call-done = f32[1024,32]{0,1:T(8,128)} async-done(((f32[1024,32]{0,1:T(8,128)}), f32[1024,32]{0,1:T(8,128)}) %all-reduce.7.cloned.1.call-update) | async-done | bytes 131088 | tf_op jit(solution)/shard_map/psum | solution.py:490
  (380 shorter events, 293.9 us)
Async XLA Ops:
  7.2 174.1 %all-gather.5.cloned.1.call-start = ((), (), s32[]{:S(2)}) async-start(), calls=%async_computation.17 | async-start | bytes 8650752 | tf_op jit(solution)/shard_map/all_gather | solution.py:333
  18.1 112.7 %all-to-all-start.1 = ((bf16[8,4,40,1024]{3,2,1,0:T(8,128)(2,1)}), bf16[8,4,40,1024]{3,2,1,0:T(8,128)(2,1)S(1)}, u32[]{:S(2)}, u32[]{:S(2)}) async-start(bf16[8,4,40,1024]{3,2,1,0:T(8,128)(2,1)} %bitcast.200), calls=%async_computation.1 | async-start | bytes 5242880 | tf_op jit(solution)/shard_map/all_to_all | solution.py:328
  23.3 104.5 %collective-permute-start.7 = (bf16[512,1024]{1,0:T(8,128)(2,1)}, bf16[512,1024]{1,0:T(8,128)(2,1)S(1)}, u32[]{:S(2)}, u32[]{:S(2)}) collective-permute-start(bf16[512,1024]{1,0:T(8,128)(2,1)} %param.29), channel_id=1, source_target_pairs={{0,2},{1,3},{2,0},{3,1},{4,6},{5,7},{6,4},{7,5},{8,10},{9,11},{10,... | collective-permute-start | bytes 3145736 | tf_op jit(solution)/shard_map/ppermute | solution.py:325
  25.9 151.1 %collective-permute-start.4 = (bf16[512,1024]{1,0:T(8,128)(2,1)}, bf16[512,1024]{1,0:T(8,128)(2,1)}, u32[]{:S(2)}, u32[]{:S(2)}) collective-permute-start(bf16[512,1024]{1,0:T(8,128)(2,1)} %param.29), channel_id=1, source_target_pairs={{0,3},{1,2},{2,1},{3,0},{4,7},{5,6},{6,5},{7,4},{8,11},{9,10},{10,... | collective-permute-start | bytes 3145736 | tf_op jit(solution)/shard_map/ppermute | solution.py:325
  132.3 68.5 %all-to-all-start.7 = ((bf16[8,4,40,1024]{3,2,1,0:T(8,128)(2,1)}), bf16[8,4,40,1024]{3,2,1,0:T(8,128)(2,1)}, u32[]{:S(2)}, u32[]{:S(2)}) async-start(bf16[8,4,40,1024]{3,2,1,0:T(8,128)(2,1)} %bitcast.197), calls=%async_computation.7 | async-start | bytes 5242880 | tf_op jit(solution)/shard_map/all_to_all | solution.py:328
  200.8 51.2 %all-to-all-start.4 = ((bf16[8,4,40,1024]{3,2,1,0:T(8,128)(2,1)}), bf16[8,4,40,1024]{3,2,1,0:T(8,128)(2,1)}, u32[]{:S(2)}, u32[]{:S(2)}) async-start(bf16[8,4,40,1024]{3,2,1,0:T(8,128)(2,1)} %bitcast.196), calls=%async_computation.4 | async-start | bytes 5242880 | tf_op jit(solution)/shard_map/all_to_all | solution.py:328
  252.1 53.7 %all-to-all-start = ((bf16[8,4,40,1024]{3,2,1,0:T(8,128)(2,1)}), bf16[8,4,40,1024]{3,2,1,0:T(8,128)(2,1)}, u32[]{:S(2)}, u32[]{:S(2)}) async-start(bf16[8,4,40,1024]{3,2,1,0:T(8,128)(2,1)} %bitcast.199), calls=%async_computation | async-start | bytes 5242880 | tf_op jit(solution)/shard_map/all_to_all | solution.py:328
  256.5 46.2 %collective-permute-start.6 = (bf16[512,1024]{1,0:T(8,128)(2,1)}, bf16[512,1024]{1,0:T(8,128)(2,1)S(1)}, u32[]{:S(2)}, u32[]{:S(2)}) collective-permute-start(bf16[512,1024]{1,0:T(8,128)(2,1)} %copy-done.48), channel_id=1, source_target_pairs={{0,2},{1,3},{2,0},{3,1},{4,6},{5,7},{6,4},{7,5},{8,10},{9,11},{10,... | collective-permute-start | bytes 3145736 | tf_op jit(solution)/shard_map/ppermute | solution.py:325
  305.7 36.7 %all-to-all-start.6 = ((bf16[8,4,40,1024]{3,2,1,0:T(8,128)(2,1)}), bf16[8,4,40,1024]{3,2,1,0:T(8,128)(2,1)}, u32[]{:S(2)}, u32[]{:S(2)}) async-start(bf16[8,4,40,1024]{3,2,1,0:T(8,128)(2,1)} %bitcast.198), calls=%async_computation.6 | async-start | bytes 5242880 | tf_op jit(solution)/shard_map/all_to_all | solution.py:328
  310.1 27.6 %collective-permute-start.3 = (bf16[512,1024]{1,0:T(8,128)(2,1)}, bf16[512,1024]{1,0:T(8,128)(2,1)S(1)}, u32[]{:S(2)}, u32[]{:S(2)}) collective-permute-start(bf16[512,1024]{1,0:T(8,128)(2,1)} %copy-done.48), channel_id=1, source_target_pairs={{0,3},{1,2},{2,1},{3,0},{4,7},{5,6},{6,5},{7,4},{8,11},{9,10},{10,... | collective-permute-start | bytes 3145736 | tf_op jit(solution)/shard_map/ppermute | solution.py:325
  342.4 66.3 %all-to-all-start.3 = ((bf16[8,4,40,1024]{3,2,1,0:T(8,128)(2,1)}), bf16[8,4,40,1024]{3,2,1,0:T(8,128)(2,1)}, u32[]{:S(2)}, u32[]{:S(2)}) async-start(bf16[8,4,40,1024]{3,2,1,0:T(8,128)(2,1)} %bitcast.195), calls=%async_computation.3 | async-start | bytes 5242880 | tf_op jit(solution)/shard_map/all_to_all | solution.py:328
  354.8 76.9 %collective-permute-start.1 = (bf16[8,4,40,1024]{3,2,1,0:T(8,128)(2,1)}, bf16[8,4,40,1024]{3,2,1,0:T(8,128)(2,1)}, u32[]{:S(2)}, u32[]{:S(2)}) collective-permute-start(bf16[8,4,40,1024]{3,2,1,0:T(8,128)(2,1)} %copy-done.28), channel_id=1, source_target_pairs={{0,1},{1,0},{2,3},{3,2},{4,5},{5,4},{6,7},{7,6},{8,9},{9,8},{10,11... | collective-permute-start | bytes 7864328 | tf_op jit(solution)/shard_map/ppermute | solution.py:325
  373.7 114.0 %collective-permute-start = (bf16[8,4,40,1024]{3,2,1,0:T(8,128)(2,1)}, bf16[8,4,40,1024]{3,2,1,0:T(8,128)(2,1)}, u32[]{:S(2)}, u32[]{:S(2)}) collective-permute-start(bf16[8,4,40,1024]{3,2,1,0:T(8,128)(2,1)} %all-to-all-done.x_ref.refs_0_), channel_id=1, source_target_pairs={{0,1},{1,0},{2,3},{3,2},{4,5},{5,4},{6,7},{7,6},{8,9},{9,8},{10,11... | collective-permute-start | bytes 7864328 | tf_op jit(solution)/shard_map/ppermute | solution.py:325
  408.7 124.9 %all-to-all-start.11 = ((bf16[8,4,40,1024]{3,2,1,0:T(8,128)(2,1)}), bf16[8,4,40,1024]{3,2,1,0:T(8,128)(2,1)}, u32[]{:S(2)}, u32[]{:S(2)}) async-start(bf16[8,4,40,1024]{3,2,1,0:T(8,128)(2,1)} %get-tuple-element.76), calls=%async_computation.11 | async-start | bytes 5242880 | tf_op jit(solution)/shard_map/all_to_all | solution.py:328
  508.6 59.0 %collective-permute-start.9 = (bf16[8,4,40,1024]{3,2,1,0:T(8,128)(2,1)}, bf16[8,4,40,1024]{3,2,1,0:T(8,128)(2,1)}, u32[]{:S(2)}, u32[]{:S(2)}) collective-permute-start(bf16[8,4,40,1024]{3,2,1,0:T(8,128)(2,1)} %get-tuple-element.74), channel_id=1, source_target_pairs={{0,1},{1,0},{2,3},{3,2},{4,5},{5,4},{6,7},{7,6},{8,9},{9,8},{10,11... | collective-permute-start | bytes 7864328 | tf_op jit(solution)/shard_map/ppermute | solution.py:325
  533.6 39.3 %all-to-all-start.10 = ((bf16[8,4,40,1024]{3,2,1,0:T(8,128)(2,1)}), bf16[8,4,40,1024]{3,2,1,0:T(8,128)(2,1)}, u32[]{:S(2)}, u32[]{:S(2)}) async-start(bf16[8,4,40,1024]{3,2,1,0:T(8,128)(2,1)} %get-tuple-element.75), calls=%async_computation.10 | async-start | bytes 5242880 | tf_op jit(solution)/shard_map/all_to_all | solution.py:328
  572.9 84.9 %all-to-all-start.9 = ((bf16[8,4,40,1024]{3,2,1,0:T(8,128)(2,1)}), bf16[8,4,40,1024]{3,2,1,0:T(8,128)(2,1)}, u32[]{:S(2)}, u32[]{:S(2)}) async-start(bf16[8,4,40,1024]{3,2,1,0:T(8,128)(2,1)} %add_convert_fusion), calls=%async_computation.9 | async-start | bytes 5242880 | tf_op jit(solution)/shard_map/all_to_all | solution.py:328
  577.3 164.8 %reduce-scatter.22.cloned.1.call-start = ((), (), s32[]{:S(2)}) async-start(), calls=%async_computation.24 | async-start | bytes 2359296
  584.9 71.9 %collective-permute-start.11 = (bf16[512,1024]{1,0:T(8,128)(2,1)S(1)}, bf16[512,1024]{1,0:T(8,128)(2,1)S(1)}, u32[]{:S(2)}, u32[]{:S(2)}) collective-permute-start(bf16[512,1024]{1,0:T(8,128)(2,1)S(1)} %convolution_convert_fusion.10), channel_id=1, source_target_pairs={{0,2},{1,3},{2,0},{3,1},{4,6},{5,7},{6,4},{7,5},{8,10},{9,11},{10,... | collective-permute-start | bytes 3145736 | tf_op jit(solution)/shard_map/ppermute | solution.py:325
  589.5 68.2 %collective-permute-start.10 = (bf16[512,1024]{1,0:T(8,128)(2,1)S(1)}, bf16[512,1024]{1,0:T(8,128)(2,1)}, u32[]{:S(2)}, u32[]{:S(2)}) collective-permute-start(bf16[512,1024]{1,0:T(8,128)(2,1)S(1)} %convolution_convert_fusion.11), channel_id=1, source_target_pairs={{0,3},{1,2},{2,1},{3,0},{4,7},{5,6},{6,5},{7,4},{8,11},{9,10},{10,... | collective-permute-start | bytes 3145736 | tf_op jit(solution)/shard_map/ppermute | solution.py:325
  681.4 105.6 %reduce-scatter.20.cloned.1.call-start = ((), (), s32[]{:S(2)}) async-start(), calls=%async_computation.23 | async-start | bytes 2359296
  698.9 132.5 %reduce-scatter.18.cloned.1.call-start = ((), (), s32[]{:S(2)}) async-start(), calls=%async_computation.22 | async-start | bytes 2359296
  715.6 160.6 %reduce-scatter.16.cloned.1.call-start = ((), (), s32[]{:S(2)}) async-start(), calls=%async_computation.21 | async-start | bytes 2359296
  732.7 173.3 %reduce-scatter.14.cloned.1.call-start = ((), (), s32[]{:S(2)}) async-start(), calls=%async_computation.18 | async-start | bytes 1310720 | tf_op jit(solution)/shard_map/reduce_scatter | solution.py:482
  878.4 36.7 %all-to-all-start.8 = ((bf16[8,4,40,1024]{3,2,1,0:T(8,128)(2,1)}), bf16[8,4,40,1024]{3,2,1,0:T(8,128)(2,1)}, u32[]{:S(2)}, u32[]{:S(2)}) async-start(bf16[8,4,40,1024]{3,2,1,0:T(8,128)(2,1)} %get-tuple-element.72), calls=%async_computation.8 | async-start | bytes 5242880 | tf_op jit(solution)/shard_map/all_to_all | solution.py:328
  882.8 215.3 %all-gather.7.cloned.1.call-start = ((), (), s32[]{:S(2)}) async-start(), calls=%async_computation.20 | async-start | bytes 2359296 | tf_op jit(solution)/shard_map/all_gather | solution.py:483
  915.2 50.5 %all-to-all-start.5 = ((bf16[8,4,40,1024]{3,2,1,0:T(8,128)(2,1)}), bf16[8,4,40,1024]{3,2,1,0:T(8,128)(2,1)}, u32[]{:S(2)}, u32[]{:S(2)}) async-start(bf16[8,4,40,1024]{3,2,1,0:T(8,128)(2,1)} %get-tuple-element.71), calls=%async_computation.5 | async-start | bytes 5242880 | tf_op jit(solution)/shard_map/all_to_all | solution.py:328
  919.7 209.0 %all-reduce.7.cloned.1.call-start = ((), (), s32[]{:S(2)}) async-start(), calls=%async_computation.19 | async-start | bytes 262144 | tf_op jit(solution)/shard_map/psum | solution.py:490
  919.8 74.2 %collective-permute-start.2 = (bf16[8,4,40,1024]{3,2,1,0:T(8,128)(2,1)}, bf16[8,4,40,1024]{3,2,1,0:T(8,128)(2,1)}, u32[]{:S(2)}, u32[]{:S(2)}) collective-permute-start(bf16[8,4,40,1024]{3,2,1,0:T(8,128)(2,1)} %get-tuple-element.70), channel_id=1, source_target_pairs={{0,1},{1,0},{2,3},{3,2},{4,5},{5,4},{6,7},{7,6},{8,9},{9,8},{10,11... | collective-permute-start | bytes 7864328 | tf_op jit(solution)/shard_map/ppermute | solution.py:325
  963.3 129.9 %collective-permute-start.8 = (bf16[512,1024]{1,0:T(8,128)(2,1)}, bf16[512,1024]{1,0:T(8,128)(2,1)}, u32[]{:S(2)}, u32[]{:S(2)}) collective-permute-start(bf16[512,1024]{1,0:T(8,128)(2,1)} %convolution_convert_fusion.12), channel_id=1, source_target_pairs={{0,2},{1,3},{2,0},{3,1},{4,6},{5,7},{6,4},{7,5},{8,10},{9,11},{10,... | collective-permute-start | bytes 3145736 | tf_op jit(solution)/shard_map/ppermute | solution.py:325
  970.1 123.1 %collective-permute-start.5 = (bf16[512,1024]{1,0:T(8,128)(2,1)}, bf16[512,1024]{1,0:T(8,128)(2,1)}, u32[]{:S(2)}, u32[]{:S(2)}) collective-permute-start(bf16[512,1024]{1,0:T(8,128)(2,1)} %convolution_convert_fusion.13), channel_id=1, source_target_pairs={{0,3},{1,2},{2,1},{3,0},{4,7},{5,6},{6,5},{7,4},{8,11},{9,10},{10,... | collective-permute-start | bytes 3145736 | tf_op jit(solution)/shard_map/ppermute | solution.py:325
  998.5 94.7 %all-to-all-start.2 = ((bf16[8,4,40,1024]{3,2,1,0:T(8,128)(2,1)}), bf16[8,4,40,1024]{3,2,1,0:T(8,128)(2,1)}, u32[]{:S(2)}, u32[]{:S(2)}) async-start(bf16[8,4,40,1024]{3,2,1,0:T(8,128)(2,1)} %add_convert_fusion.1), calls=%async_computation.2 | async-start | bytes 5242880 | tf_op jit(solution)/shard_map/all_to_all | solution.py:328
  (96 other events, 2555.7 us)
Sparse Core Ops, SparseCore 0:
  11.5 150.6 all-gather.4
  681.5 60.5 reduce-scatter.21
  745.8 41.2 reduce-scatter.19
  790.2 41.1 reduce-scatter.17
  834.9 41.2 reduce-scatter.15
  878.9 27.1 reduce-scatter.13
  908.1 39.5 all-gather.6
  954.8 173.9 all-reduce.6

commit v2 on v1

v2 whole, which is shorter than its diff:
```python
import functools

import jax
import jax.numpy as jnp
from jax import lax
from jax.experimental import pallas as pl
from jax.experimental.pallas import tpu as pltpu
from jax.sharding import PartitionSpec as P

HEAD_DIM = 64
TOP = 2
LANES = 128
MIB = 2**20

epsilon = 1e-06
balance_weight = 0.01
zloss_weight = 0.001
highest = lax.Precision.HIGHEST

BF = jnp.bfloat16
F32 = jnp.float32
NN = (((1,), (0,)), ((), ()))
NT = (((1,), (1,)), ((), ()))
TN = (((0,), (0,)), ((), ()))


def dot(left, right, dims=NN):
    return lax.dot_general(left, right, dims, preferred_element_type=F32)


def rms_scale(rows_in, gain):
    inverse = lax.rsqrt(jnp.mean(rows_in * rows_in, axis=-1, keepdims=True) + epsilon)
    return rows_in * inverse * gain


def drop(kernel, at, count):
    def run(*refs):
        kernel(*refs[:at], *refs[at + count :])

    return run


def launch(kernel, operands, after, *, grid, in_specs, out_specs, out_shape, name, flops, scratch=(), moved=0):
    held = [value for value in after if value is not None]
    sizes = [jax.ShapeDtypeStruct(v.shape, v.dtype) for v in operands] + jax.tree.leaves(out_shape)
    moved = moved or sum(v.size * v.dtype.itemsize for v in sizes)
    return pl.pallas_call(
        drop(kernel, len(operands), len(held)),
        grid=grid,
        in_specs=list(in_specs) + [pl.BlockSpec(memory_space=pl.ANY)] * len(held),
        out_specs=out_specs,
        out_shape=out_shape,
        scratch_shapes=scratch,
        compiler_params=pltpu.CompilerParams(vmem_limit_bytes=58 * MIB),
        cost_estimate=pl.CostEstimate(flops=flops, bytes_accessed=moved, transcendentals=0),
        name=name,
    )(*operands, *held)


def lookup(row, index):
    table = jnp.broadcast_to(row, (index.shape[0], LANES))
    parts = [
        jnp.take_along_axis(table, index[:, at : at + LANES], axis=1)
        for at in range(0, index.shape[1], LANES)
    ]
    return jnp.concatenate(parts, axis=1)


def attend_kernel(x_ref, w_ref, bucket_ref, table_ref, qkv_ref, mixed_ref, prob_ref, out_ref):
    seq = x_ref.shape[0]
    tile = 128
    low = lax.broadcasted_iota(jnp.int32, (tile, LANES), 1) < HEAD_DIM
    for part in range(3):
        qkv_ref[part] = dot(x_ref[...], w_ref[part, 0, 0], NT).astype(BF)
    for start in range(0, seq, tile):
        rows = pl.ds(start, tile)
        query = qkv_ref[0, rows, :]
        mixed = []
        for head in range(2):
            part = jnp.where(low if head == 0 else ~low, query, jnp.zeros_like(query))
            scores = dot(part, qkv_ref[1], NT) * 0.125 + lookup(
                table_ref[0, head : head + 1, :], bucket_ref[rows, :]
            )
            scores = jnp.exp(scores - jnp.max(scores, axis=-1, keepdims=True))
            weights = (scores / jnp.sum(scores, axis=-1, keepdims=True)).astype(BF)
            prob_ref[head, rows, :] = weights
            mixed.append(dot(weights, qkv_ref[2]))
        mixed_ref[rows, :] = jnp.where(low, mixed[0], mixed[1]).astype(BF)
    out = dot(mixed_ref[...], w_ref[3, 0, 0])

    @pl.when(pl.program_id(0) == 0)
    def _():
        out_ref[...] = out

    @pl.when(pl.program_id(0) > 0)
    def _():
        out_ref[...] += out


def attend(x, weights, buckets, table, after):
    seq, width = x.shape
    _, pairs, groups, _, _ = weights.shape
    steps = pairs * groups
    full = pl.BlockSpec((seq, width), lambda i: (0, 0))
    col = pl.BlockSpec((seq, LANES), lambda i: (0, i))
    return launch(
        attend_kernel,
        (x, weights, buckets, table),
        after,
        grid=(steps,),
        in_specs=[
            full,
            pl.BlockSpec((4, 1, 1, LANES, width), lambda i: (0, i % pairs, i // pairs, 0, 0)),
            pl.BlockSpec((seq, seq), lambda i: (0, 0)),
            pl.BlockSpec((1, 2, LANES), lambda i: (i, 0, 0)),
        ],
        out_specs=[
            pl.BlockSpec((3, seq, LANES), lambda i: (0, 0, i)),
            col,
            pl.BlockSpec((2, seq, seq), lambda i: (i, 0, 0)),
            full,
        ],
        out_shape=[
            jax.ShapeDtypeStruct((3, seq, steps * LANES), BF),
            jax.ShapeDtypeStruct((seq, steps * LANES), BF),
            jax.ShapeDtypeStruct((2 * steps, seq, seq), BF),
            jax.ShapeDtypeStruct((seq, width), F32),
        ],
        name="attend",
        flops=steps * seq * LANES * 2 * (4 * width + 4 * seq),
    )


def attend_back_kernel(
    x_ref, grad_ref, w_ref, qkv_ref, mixed_ref, prob_ref, weight_ref, score_ref, normed_ref, part_ref
):
    seq = x_ref.shape[0]
    tile = 128
    low = lax.broadcasted_iota(jnp.int32, (tile, LANES), 1) < HEAD_DIM
    mixed_grad = dot(grad_ref[...], w_ref[3, 0, 0], NT).astype(BF)
    part_ref[...] = mixed_grad
    queries = []
    for start in range(0, seq, tile):
        rows = pl.ds(start, tile)
        grad = part_ref[rows, :]
        back = []
        for head in range(2):
            part = jnp.where(low if head == 0 else ~low, grad, jnp.zeros_like(grad))
            weights = prob_ref[head, rows, :].astype(F32)
            weight_grad = dot(part, qkv_ref[2], NT)
            score = weights * (
                weight_grad - jnp.sum(weights * weight_grad, axis=-1, keepdims=True)
            )
            score = score.astype(BF)
            score_ref[head, rows, :] = score
            back.append(dot(score, qkv_ref[1]))
        queries.append((jnp.where(low, back[0], back[1]) * 0.125).astype(BF))
    wide = lax.broadcasted_iota(jnp.int32, (seq, LANES), 1) < HEAD_DIM
    keys = [dot(score_ref[head], qkv_ref[0], TN) for head in range(2)]
    vals = [dot(prob_ref[head], mixed_grad, TN) for head in range(2)]
    back = jnp.concatenate(
        [
            jnp.concatenate(queries, 0),
            (jnp.where(wide, keys[0], keys[1]) * 0.125).astype(BF),
            jnp.where(wide, vals[0], vals[1]).astype(BF),
        ],
        1,
    )
    weight_ref[:3, 0, 0] = dot(back, x_ref[...], TN).reshape(3, LANES, -1).astype(BF)
    weight_ref[3, 0, 0] = dot(mixed_ref[...], grad_ref[...], TN).astype(BF)
    normed = dot(back, w_ref[:3, 0, 0].reshape(3 * LANES, -1))

    @pl.when(pl.program_id(0) == 0)
    def _():
        normed_ref[...] = normed

    @pl.when(pl.program_id(0) > 0)
    def _():
        normed_ref[...] += normed


def attend_back(x, grad, weights, qkv, mixed, probs, after):
    seq, width = x.shape
    _, pairs, groups, _, _ = weights.shape
    steps = pairs * groups
    full = pl.BlockSpec((seq, width), lambda i: (0, 0))
    col = pl.BlockSpec((seq, LANES), lambda i: (0, i))
    strip = pl.BlockSpec((4, 1, 1, LANES, width), lambda i: (0, i % pairs, i // pairs, 0, 0))
    square = pl.BlockSpec((2, seq, seq), lambda i: (i, 0, 0))
    return launch(
        attend_back_kernel,
        (x, grad, weights, qkv, mixed, probs),
        after,
        grid=(steps,),
        in_specs=[full, full, strip, pl.BlockSpec((3, seq, LANES), lambda i: (0, 0, i)), col, square],
        out_specs=[strip, square, full],
        out_shape=[
            jax.ShapeDtypeStruct((4, pairs, groups, LANES, width), BF),
            jax.ShapeDtypeStruct(probs.shape, BF),
            jax.ShapeDtypeStruct((seq, width), F32),
        ],
        scratch=[pltpu.VMEM((seq, LANES), BF)],
        name="attend_back",
        flops=steps * seq * LANES * 2 * (8 * width + 8 * seq),
    )


def table_kernel(*refs):
    *score_refs, bucket_ref, out_ref = refs
    marks = bucket_ref[...]
    tile, seq = marks.shape
    count = out_ref.shape[1] // tile
    ids = lax.broadcasted_iota(jnp.int32, (tile, count, seq), 1)
    onehot = (jnp.broadcast_to(marks[:, None, :], ids.shape) == ids).astype(F32)
    onehot = onehot.astype(BF).reshape(tile * count, seq)
    block = jnp.concatenate([ref[...].reshape(-1, seq) for ref in score_refs], 0)
    sums = dot(block, onehot, NT)

    @pl.when(pl.program_id(0) == 0)
    def _():
        out_ref[...] = sums

    @pl.when(pl.program_id(0) > 0)
    def _():
        out_ref[...] += sums


def table_back(scores, buckets, count, after):
    heads = sum(part.shape[0] for part in scores)
    seq = buckets.shape[0]
    tile = 16
    sums = launch(
        table_kernel,
        (*scores, buckets),
        after,
        grid=(seq // tile,),
        in_specs=[pl.BlockSpec((part.shape[0], tile, seq), lambda i: (0, i, 0)) for part in scores]
        + [pl.BlockSpec((tile, seq), lambda i: (i, 0))],
        out_specs=pl.BlockSpec((heads * tile, tile * count), lambda i: (0, 0)),
        out_shape=jax.ShapeDtypeStruct((heads * tile, tile * count), F32),
        name="table_back",
        flops=heads * tile * seq * seq * count * 2 * 4,
    )
    sums = sums.reshape(heads, tile, tile, count)
    same = jnp.eye(tile, dtype=F32)[None, :, :, None]
    return jnp.sum(sums * same, axis=(1, 2)).T


def assemble(place, halves, after):
    sources, groups, strip, _ = halves[0].shape
    width = sum(half.shape[3] for half in halves)
    held = [value for value in after if value is not None]

    def kernel(place_ref, *refs):
        refs[-1][0] = jnp.concatenate([ref[0] for ref in refs[: len(halves)]], -1)

    return pl.pallas_call(
        kernel,
        grid_spec=pltpu.PrefetchScalarGridSpec(
            num_scalar_prefetch=1,
            grid=(sources,),
            in_specs=[
                pl.BlockSpec((1, groups, strip, half.shape[3]), lambda i, at, side=side: (at[side, i], 0, 0, 0))
                for side, half in enumerate(halves)
            ]
            + [pl.BlockSpec(memory_space=pl.ANY)] * len(held),
            out_specs=pl.BlockSpec((1, groups, strip, width), lambda i, at: (i, 0, 0, 0)),
        ),
        out_shape=jax.ShapeDtypeStruct((sources, groups, strip, width), BF),
        cost_estimate=pl.CostEstimate(flops=0, bytes_accessed=4 * sources * groups * strip * width, transcendentals=0),
        name="assemble",
    )(place, *halves, *held)


def copy_kernel(from_ref, to_ref):
    to_ref[...] = from_ref[...]


def hold(value, after):
    full = pl.BlockSpec(value.shape, lambda i: (0,) * value.ndim)
    return launch(
        copy_kernel,
        (value,),
        after,
        grid=(1,),
        in_specs=[full],
        out_specs=full,
        out_shape=jax.ShapeDtypeStruct(value.shape, value.dtype),
        name="hold",
        flops=0,
    )


def stack(place, parts, after):
    shape = parts[0].shape
    held = [value for value in after if value is not None]
    count = len(parts)

    def kernel(place_ref, *refs):
        for i in range(count):

            @pl.when(pl.program_id(0) == i)
            def _():
                refs[-1][...] = refs[i][...]

    full = pl.BlockSpec(shape, lambda s, at: (0,) * len(shape))
    return pl.pallas_call(
        kernel,
        grid_spec=pltpu.PrefetchScalarGridSpec(
            num_scalar_prefetch=1,
            grid=(count,),
            in_specs=[full] * count + [pl.BlockSpec(memory_space=pl.ANY)] * len(held),
            out_specs=pl.BlockSpec(shape, lambda s, at: (at[s],) + (0,) * (len(shape) - 1)),
        ),
        out_shape=jax.ShapeDtypeStruct((count * shape[0],) + shape[1:], BF),
        compiler_params=pltpu.CompilerParams(vmem_limit_bytes=58 * MIB),
        name="stack",
    )(place, *parts, *held)


def sum_kernel(*refs):
    *parts, out_ref = refs
    total = parts[0][...].astype(F32)
    for ref in parts[1:]:
        total += ref[...].astype(F32)
    out_ref[...] = total.astype(out_ref.dtype)


def add(*operands):
    *parts, after = operands
    shape = parts[0].shape
    if parts[0].ndim > 2:
        block = pl.BlockSpec((1,) + shape[1:], lambda i: (i,) + (0,) * (len(shape) - 1))
    else:
        block = pl.BlockSpec(shape, lambda i: (0, 0))
    return launch(
        sum_kernel,
        parts,
        after,
        grid=(shape[0] if len(shape) > 2 else 1,),
        in_specs=[block] * len(parts),
        out_specs=block,
        out_shape=jax.ShapeDtypeStruct(shape, parts[0].dtype),
        name="add",
        flops=parts[0].size,
    )


def dispatch_kernel(id_ref, x_ref, out_ref):
    count = out_ref.shape[0]
    slot = lax.broadcasted_iota(jnp.int32, (count, x_ref.shape[0]), 0) + pl.program_id(0) * count
    onehot = (slot == id_ref[0:1, :]) | (slot == id_ref[1:2, :])
    out_ref[...] = dot(onehot.astype(F32).astype(BF), x_ref[...]).astype(BF)


def to_slots(ids, value, slots, after):
    rows, width = value.shape
    steps = 4
    return launch(
        dispatch_kernel,
        (ids, value),
        after,
        grid=(steps,),
        in_specs=[
            pl.BlockSpec((TOP, rows), lambda i: (0, 0)),
            pl.BlockSpec((rows, width), lambda i: (0, 0)),
        ],
        out_specs=pl.BlockSpec((slots // steps, width), lambda i: (i, 0)),
        out_shape=jax.ShapeDtypeStruct((slots, width), BF),
        name="to_slots",
        flops=slots * rows * width * 2,
    )


def collect_kernel(id_ref, slot_ref, *refs):
    *more, out_ref = refs
    rows = out_ref.shape[0]
    slot = lax.broadcasted_iota(jnp.int32, (rows, slot_ref.shape[0]), 1)
    onehot = (slot == id_ref[:, 0:1]) | (slot == id_ref[:, 1:2])
    total = dot(onehot.astype(F32).astype(BF), slot_ref[...])
    for ref in more:
        total += ref[...].astype(F32)
    out_ref[...] = total.astype(out_ref.dtype)


def to_tokens(ids, slots, more, kind, after):
    rows = ids.shape[0]
    count, width = slots.shape
    steps = 2
    block = pl.BlockSpec((rows // steps, width), lambda i: (i, 0))
    return launch(
        collect_kernel,
        (ids, slots, *more),
        after,
        grid=(steps,),
        in_specs=[
            pl.BlockSpec((rows // steps, TOP), lambda i: (i, 0)),
            pl.BlockSpec((count, width), lambda i: (0, 0)),
        ]
        + [block] * len(more),
        out_specs=block,
        out_shape=jax.ShapeDtypeStruct((rows, width), kind),
        name="to_tokens",
        flops=count * rows * width * 2,
    )


def flat(ref):
    block = ref[...]
    return block.astype(F32).reshape(-1, block.shape[-1]).astype(BF)


def expert_kernel(
    base_ref,
    x_ref,
    g_ref,
    other_ref,
    gate_ref,
    up_ref,
    down_ref,
    router_ref,
    out_ref,
    back_ref,
    hidden_ref,
    gate_back_ref,
    up_back_ref,
    route_ref,
):
    expert = pl.program_id(0)
    x = flat(x_ref)
    g = flat(g_ref)
    lanes = lax.broadcasted_iota(jnp.int32, (x.shape[0], LANES), 1)
    sign = (lanes == base_ref[0] + expert).astype(F32) - (lanes == other_ref[0]).astype(F32)
    logits = dot(x, router_ref[...])
    apart = jnp.sum(sign * (logits[:, :LANES] + logits[:, LANES:]), axis=-1, keepdims=True)
    weight = 1.0 / (1.0 + jnp.exp(-apart))
    gate = dot(x, gate_ref[0], NT)
    up = dot(x, up_ref[0], NT)
    grad = dot(g, down_ref[0], NT)
    scale = 0.7978845608028654
    square = gate * gate
    bent = jnp.tanh(scale * gate * (1.0 + 0.044715 * square))
    half = 0.5 + 0.5 * bent
    act = gate * half
    slope = half + 0.5 * gate * (1.0 - bent * bent) * (scale + 3 * 0.044715 * scale * square)
    hidden = act * up
    mark = weight * (1.0 - weight) * jnp.sum(hidden * grad, axis=-1, keepdims=True)
    mark = (mark * sign).astype(BF)
    grad = grad * weight
    up_back = (grad * act).astype(BF)
    gate_back = (grad * up * slope).astype(BF)
    hidden_ref[0] = (hidden * weight).astype(BF)
    gate_back_ref[0] = gate_back
    up_back_ref[0] = up_back
    out = dot(hidden.astype(BF), down_ref[0]) * weight
    out_ref[...] = out.reshape(out_ref.shape).astype(BF)
    back = dot(gate_back, gate_ref[0]) + dot(up_back, up_ref[0])
    back += dot(mark, router_ref[:, :LANES], NT)
    back_ref[...] = back.reshape(back_ref.shape).astype(BF)
    part = dot(mark, x, TN)

    @pl.when(expert == 0)
    def _():
        route_ref[...] = jnp.zeros_like(route_ref)

    route_ref[...] += part


def expert_chunk(base, x, g, other, gate_w, up_w, down_w, router_pair, after):
    sources, here, slots, width = x.shape
    hidden = down_w.shape[1]
    count = sources * slots
    rows = pl.BlockSpec((sources, 1, slots, width), lambda e: (0, e, 0, 0))
    middle = pl.BlockSpec((1, count, hidden), lambda e: (e, 0, 0))
    weights = pl.BlockSpec((1, hidden, width), lambda e: (e, 0, 0))
    return launch(
        expert_kernel,
        (base, x, g, other, gate_w, up_w, down_w, router_pair),
        after,
        grid=(here,),
        in_specs=[
            pl.BlockSpec(memory_space=pltpu.SMEM),
            rows,
            rows,
            pl.BlockSpec((1, count, 1), lambda e: (e, 0, 0)),
            weights,
            weights,
            weights,
            pl.BlockSpec((width, 2 * LANES), lambda e: (0, 0)),
        ],
        out_specs=[rows, rows, middle, middle, middle, pl.BlockSpec((LANES, width), lambda e: (0, 0))],
        out_shape=[jax.ShapeDtypeStruct(x.shape, BF)] * 2
        + [jax.ShapeDtypeStruct((here, count, hidden), BF)] * 3
        + [jax.ShapeDtypeStruct((LANES, width), F32)],
        name="experts",
        flops=12 * here * count * width * hidden * 2,
    )


def weight_kernel(*refs, chunks):
    xs, gs, hidden, gates, ups = (refs[i * chunks : (i + 1) * chunks] for i in range(5))
    gate_ref, up_ref, down_ref = refs[5 * chunks :]
    x = jnp.concatenate([flat(ref) for ref in xs], 0)
    gate_ref[0] = dot(jnp.concatenate([ref[0] for ref in gates], 0), x, TN)
    up_ref[0] = dot(jnp.concatenate([ref[0] for ref in ups], 0), x, TN)
    g = jnp.concatenate([flat(ref) for ref in gs], 0)
    down_ref[0] = dot(jnp.concatenate([ref[0] for ref in hidden], 0), g, TN)


def weight_grads(xs, gs, hidden, gates, ups, after):
    sources, here, slots, width = xs[0].shape
    depth = hidden[0].shape[2]
    rows = pl.BlockSpec((sources, 1, slots, width), lambda e: (0, e, 0, 0))
    middle = pl.BlockSpec((1, sources * slots, depth), lambda e: (e, 0, 0))
    chunks = len(xs)
    return launch(
        functools.partial(weight_kernel, chunks=chunks),
        (*xs, *gs, *hidden, *gates, *ups),
        after,
        grid=(here,),
        in_specs=[rows] * (2 * chunks) + [middle] * (3 * chunks),
        out_specs=[pl.BlockSpec((1, depth, width), lambda e: (e, 0, 0))] * 3,
        out_shape=[jax.ShapeDtypeStruct((here, depth, width), F32)] * 3,
        name="expert_weight_grads",
        flops=4 * here * chunks * sources * slots * width * depth * 2,
    )


def body(
    n_expert,
    n_tensor,
    inputs,
    gain_one,
    w_query,
    w_key,
    w_value,
    w_out,
    rel_table,
    gain_two,
    router,
    w_gate,
    w_up,
    w_down,
    routes,
    buckets,
    grad_out,
):
    rows, width = inputs.shape
    experts = router.shape[1]
    here = w_gate.shape[0]
    tokens = routes.shape[0]
    cap = (5 * rows * TOP + 4 * experts - 1) // (4 * experts)
    slots = experts * cap
    seq = buckets.shape[0]
    share = seq // rows
    count = rel_table.shape[0]
    head_cols = w_query.shape[1]
    at_expert = lax.axis_index("expert")
    at_tensor = lax.axis_index("tensor")
    steps = range(n_tensor)
    far = range(2, n_tensor)
    last = [None]

    def swap(value, step):
        return lax.ppermute(value, "tensor", [(i, i ^ step) for i in range(n_tensor)])

    def exchange(value):
        return lax.all_to_all(value, "expert", split_axis=0, concat_axis=0, tiled=True)

    def ordered(run, *operands, after=()):
        before = last[0] if isinstance(last[0], tuple) else (last[0],)
        result = run(*operands, (*before, *after))
        last[0] = result[0] if isinstance(result, (list, tuple)) else result
        return result

    labels = jnp.arange(experts, dtype=jnp.int32)
    grouped = routes.T.reshape(TOP, n_expert * n_tensor, rows)
    marks = (grouped[:, :, None, :] == labels[:, None]).astype(BF)
    order = jnp.arange(rows, dtype=jnp.int32)
    earlier = (order[:, None] < order[None, :]).astype(BF)
    ahead = jnp.einsum("kges,st->kget", marks, earlier, preferred_element_type=F32)
    first_count = jnp.sum(marks[0].astype(F32), axis=-1, keepdims=True)
    ahead = ahead + jnp.stack([jnp.zeros_like(first_count), first_count])
    places = jnp.sum(ahead * marks.astype(F32), axis=2).astype(jnp.int32)
    slot_ids = jnp.where(places < cap, grouped * cap + places, -1)
    slot_ids = slot_ids.reshape(TOP, n_expert, n_tensor, rows)
    choices = grouped.reshape(TOP, n_expert, n_tensor, rows)

    def relative(value, axis):
        return jnp.stack([lax.dynamic_index_in_dim(value, at_tensor ^ i, axis, keepdims=False) for i in steps])

    own_ids = relative(lax.dynamic_index_in_dim(slot_ids, at_expert, 1, keepdims=False), 1)
    id_rows = [own_ids[i] for i in steps]
    id_cols = jnp.swapaxes(own_ids, 1, 2)
    local = slot_ids - at_expert * (here * cap)
    slot_here = jnp.arange(here * cap, dtype=jnp.int32)[:, None]
    partner = jnp.sum(
        jnp.where(local[0][:, :, None, :] == slot_here, choices[1][:, :, None, :], 0)
        + jnp.where(local[1][:, :, None, :] == slot_here, choices[0][:, :, None, :], 0),
        axis=-1,
    ).reshape(n_expert, n_tensor, here, cap)
    partners = jnp.swapaxes(relative(partner, 1), 1, 2).reshape(n_tensor, here, n_expert * cap, 1)

    def send(step, value, after=()):
        buffer = ordered(to_slots, id_rows[step], value, slots, after=after)
        return exchange(buffer.reshape(n_expert, here, cap, width))

    def home(step, value, more=(), kind=BF, after=()):
        return ordered(to_tokens, id_cols[step], value.reshape(slots, width), more, kind, after=after)

    def gather(value):
        whole = lax.all_gather(value, "tensor", axis=0, tiled=True).reshape(n_tensor, rows, width)
        return [lax.dynamic_index_in_dim(whole, at_tensor ^ i, 0, keepdims=False) for i in steps]

    def everywhere(values):
        total = jnp.concatenate([value.reshape(-1) for value in values])
        for axis, size in (("expert", n_expert), ("tensor", n_tensor)):
            for bit in range(size.bit_length() - 1):
                total = total + lax.ppermute(total, axis, [(i, i ^ (1 << bit)) for i in range(size)])
        totals = []
        for value in values:
            totals.append(total[: value.size].reshape(value.shape))
            total = total[value.size :]
        return totals

    def whole_seq(value):
        if share == 1:
            return value
        groups = [[i * share + j for j in range(share)] for i in range(n_tensor // share)]
        return lax.all_gather(value, "tensor", axis=0, tiled=True, axis_index_groups=groups)

    def own_rows(value):
        if share == 1:
            return value
        return lax.dynamic_slice_in_dim(value, (at_tensor % share) * rows, rows, 0)

    packed = jnp.concatenate([w_query.T, w_key.T, w_value.T, w_out], 0)
    strip = 4 * head_cols // n_expert
    blocks = 4 * head_cols // LANES
    pairs = blocks // 4
    own_w = packed.reshape(4, pairs, 1, LANES, width)
    packed = ordered(hold, lax.dynamic_slice_in_dim(packed, at_expert * strip, strip, 0))
    strips = jnp.stack([swap(packed, i) for i in steps[1:]])
    table_own = jnp.pad(rel_table.T, ((0, 0), (0, LANES - count)))
    table_all = jnp.stack([table_own] + [swap(table_own, i) for i in steps[1:]])
    table_all = table_all.reshape(n_tensor * pairs, 2, LANES)

    inputs_f = inputs.astype(F32)
    normed_one = rms_scale(inputs_f, gain_one).astype(BF)
    attn_in = whole_seq(normed_one)
    grad_far = gather(ordered(hold, grad_out, after=(strips, table_all)))
    own_part = ordered(attend, attn_in, own_w, buckets, table_all[:pairs])

    bits = [1 << i for i in range(1, n_expert.bit_length() - 1)]
    sources = jnp.arange(n_expert, dtype=jnp.int32) ^ at_expert
    halves, places, came = [], [], []
    for half in range(2):
        held, order = strips[None, :, :, half * width // 2 : (half + 1) * width // 2], [0]
        for bit in (bits if half == 0 else bits[::-1]) + [1]:
            came.append(held)
            held = jnp.concatenate([held, lax.ppermute(held, "expert", [(i, i ^ bit) for i in range(n_expert)])], 0)
            order = order + [i ^ bit for i in order]
        halves.append(held)
        where = jnp.asarray([order.index(i) for i in range(n_expert)], jnp.int32)
        places.append(jnp.sum(jnp.where(sources[:, None] == jnp.arange(n_expert), where, 0), 1))
    places = jnp.stack(places).astype(jnp.int32)

    grad_slots = {0: send(0, grad_out, (came[len(bits)], came[-1]))}
    attn_w = ordered(assemble, places, halves)
    attn_w = attn_w.reshape(blocks, n_expert // blocks, n_tensor - 1, strip, width)
    attn_w = jnp.swapaxes(attn_w, 1, 2).reshape(4, pairs, n_tensor - 1, LANES, width)
    rest_part = ordered(attend, attn_in, attn_w, buckets, table_all[pairs:])
    grad_slots[1] = send(1, grad_far[1])
    resid = inputs_f + own_rows(own_part[3] + rest_part[3])
    normed_two = rms_scale(resid, gain_two)
    normed_low = normed_two.astype(BF)

    token_far = gather(normed_low)
    token_slots = {0: send(0, normed_low)}
    for i in far:
        grad_slots[i] = send(i, grad_far[i])

    counts = jnp.sum((routes.T[:, None, :] == labels[:, None]).astype(F32), axis=(0, 2))
    route_share = counts / (tokens * TOP)

    def losses(normed, router_w):
        logits = jnp.dot(normed, router_w, precision=highest)
        router_probs = jax.nn.softmax(logits, axis=-1)
        log_totals = jax.nn.logsumexp(logits, axis=-1)
        balance = experts * jnp.sum(route_share * jnp.sum(router_probs, axis=0)) / tokens
        return balance, jnp.sum(log_totals * log_totals) / tokens

    (balance_part, zloss_part), losses_back = jax.vjp(losses, normed_two, router)
    normed_grad, router_grad = losses_back(
        (jnp.asarray(balance_weight, F32), jnp.asarray(zloss_weight, F32))
    )

    router_high = router.astype(BF)
    router_low = (router - router_high.astype(F32)).astype(BF)
    fill = ((0, 0), (0, LANES - experts))
    router_pair = jnp.concatenate([jnp.pad(router_high, fill), jnp.pad(router_low, fill)], 1)
    base = jnp.full((1,), at_expert * here, jnp.int32)
    gate_w = jnp.swapaxes(w_gate, 1, 2)
    up_w = jnp.swapaxes(w_up, 1, 2)

    def rows_in(value):
        if cap % 8 == 0:
            return value
        return jnp.swapaxes(value, 0, 1).reshape(1, here, n_expert * cap, width)

    def rows_out(value):
        if cap % 8 == 0:
            return value
        return jnp.swapaxes(value.reshape(here, n_expert, cap, width), 0, 1)

    xs, gs, done = {}, {}, {}

    def work(step):
        xs[step], gs[step] = rows_in(token_slots[step]), rows_in(grad_slots[step])
        done[step] = ordered(
            expert_chunk, base, xs[step], gs[step], partners[step], gate_w, up_w, w_down, router_pair
        )

    work(0)
    for i in steps[1:]:
        token_slots[i] = send(i, token_far[i], (*grad_slots.values(),))
    for i in steps[1:]:
        work(i)
    backs = {i: rows_out(done[i][1]) for i in steps}
    outs = {i: rows_out(done[i][0]) for i in steps}
    moe_far, near = [], None
    for i in far:
        moe_far.append(swap(home(i, exchange(backs[i]), after=moe_far[-1:]), i))
        if i == far[0]:
            near = exchange(ordered(add, backs[0], swap(backs[1], 1)))
    gate_grad, up_grad, down_grad = ordered(
        weight_grads,
        *[[v[i] for i in steps] for v in (xs, gs)],
        *[[done[i][j] for i in steps] for j in (2, 3, 4)],
    )
    moe_grad = home(0, near, moe_far, F32)
    router_grad = router_grad + sum(done[i][5] for i in steps)[:experts].T

    grad_f = grad_out.astype(F32)
    resid_norm_grad, gain_two_grad = jax.vjp(rms_scale, resid, gain_two)[1](normed_grad + moe_grad)
    resid_grad = grad_f + resid_norm_grad
    attn_grad = whole_seq(resid_grad.astype(BF))
    out_all = ordered(stack, jnp.arange(n_tensor, dtype=jnp.int32) ^ at_tensor, [outs[i] for i in steps])
    rest_back = ordered(attend_back, attn_in, attn_grad, attn_w, *rest_part[:3])
    own_back = ordered(attend_back, attn_in, attn_grad, own_w, *own_part[:3])
    out_sum = lax.psum_scatter(out_all, "tensor", scatter_dimension=0, tiled=True)
    out_sum = exchange(out_sum.reshape(n_expert, here, cap, width))
    normed_one_grad = own_back[2] + rest_back[2]

    side = at_expert % 2

    def pair_sum(weight_parts):
        groups = weight_parts.shape[2]
        parts = weight_parts.reshape(blocks, groups, n_expert // blocks, strip, width)
        parts = jnp.swapaxes(parts, 1, 2).reshape(n_expert // 2, 2, groups, strip, width)
        kept = lax.dynamic_index_in_dim(parts, side, 1, keepdims=False)
        given = lax.dynamic_index_in_dim(parts, 1 - side, 1, keepdims=False)
        given = lax.ppermute(given, "expert", [(i, i ^ 1) for i in range(n_expert)])
        return (kept.astype(F32) + given.astype(F32)).astype(BF)

    def plane_sum(parts):
        parts = lax.all_to_all(
            parts,
            "expert",
            split_axis=0,
            concat_axis=0,
            tiled=True,
            axis_index_groups=[list(range(i, n_expert, 2)) for i in range(2)],
        )
        return jnp.sum(parts.astype(F32), axis=0).astype(BF)

    parts = [pair_sum(own_back[0]), pair_sum(rest_back[0])]
    parts = [plane_sum(part) for part in parts]
    parts = [part[i] for part in parts for i in range(part.shape[0])]
    table_grad = ordered(table_back, (own_back[1], rest_back[1]), buckets, count)
    input_norm_grad, gain_one_grad = jax.vjp(rms_scale, inputs_f, gain_one)[1](own_rows(normed_one_grad))
    input_grad = resid_grad + input_norm_grad

    table_grad = relative(table_grad.T.reshape(n_tensor, rel_table.shape[1], count), 0) / share
    small = [router_grad.T, gain_one_grad, gain_two_grad, table_grad, jnp.stack([balance_part, zloss_part])]
    router_total, gain_one_total, gain_two_total, table_total, loss_total = everywhere(small)
    strip_grad = ordered(add, parts[0], *[swap(parts[i], i) for i in steps[1:]], after=(gain_one_total,))
    if share > 1:
        strip_grad = (strip_grad.astype(F32) / share).astype(BF)
    output = home(0, out_sum, (resid,), BF)

    attn_w_grad = lax.all_gather(strip_grad, "expert", axis=0, tiled=True).astype(F32)
    table_total = lax.dynamic_index_in_dim(table_total, at_tensor, 0, keepdims=False).T
    return (
        output,
        input_grad,
        gain_one_total,
        attn_w_grad[:head_cols].T,
        attn_w_grad[head_cols : 2 * head_cols].T,
        attn_w_grad[2 * head_cols : 3 * head_cols].T,
        attn_w_grad[3 * head_cols :],
        table_total,
        gain_two_total,
        router_total.T,
        jnp.swapaxes(gate_grad, 1, 2),
        jnp.swapaxes(up_grad, 1, 2),
        down_grad,
        loss_total,
    )


def solution(mesh):
    return jax.shard_map(
        functools.partial(body, mesh.shape["expert"], mesh.shape["tensor"]),
        mesh=mesh,
        in_specs=(
            P(("expert", "tensor"), None),
            P(),
            P(None, "tensor"),
            P(None, "tensor"),
            P(None, "tensor"),
            P("tensor", None),
            P(None, "tensor"),
            P(),
            P(),
            P("expert", None, "tensor"),
            P("expert", None, "tensor"),
            P("expert", "tensor", None),
            P(),
            P(),
            P(("expert", "tensor"), None),
        ),
        out_specs=(
            P(("expert", "tensor"), None),
            P(("expert", "tensor"), None),
            P(),
            P(None, "tensor"),
            P(None, "tensor"),
            P(None, "tensor"),
            P("tensor", None),
            P(None, "tensor"),
            P(),
            P(),
            P("expert", None, "tensor"),
            P("expert", None, "tensor"),
            P("expert", "tensor", None),
            P(),
        ),
        check_vma=False,
    )
```

time: 1150 us -> 886 us (0.77)
  waiting for transfers between devices: 527 us -> 310 us
  Pallas kernels: 196 us -> 317 us
  matrix products: 100 us -> 9.37 us
  blocking collectives: 78 us -> 0 us
  local copies, waits for them, and re-layouts: 85.4 us -> 55.8 us
  other arithmetic: 41.1 us -> 60.8 us
    ppermute x12, waiting for transfers between devices: 330 us -> 97 us  [swap(): lax.ppermute(value, 'tensor', [(i, i ^ step) for i in range(n_tensor)])]
    unnamed x12 -> x4, waiting for transfers between devices: 140 us -> 0.75 us
    all_to_all x12, waiting for transfers between devices: 10.7 us -> 139 us  [exchange(): lax.all_to_all(value, 'expert', split_axis=0, concat_axis=0, tiled=True)]
    pallas_call x14 -> x28, Pallas kernels: 196 us -> 317 us  [the longest x26 300 us: launch(): pl.pallas_call(drop(kernel, len(operands), len(held)), grid=grid, in_spec...]
    dot_general x36 -> x0, matrix products: 87.4 us -> none  [dot(): return lax.dot_general(left, right, dims, preferred_element_type=F32)]
    ppermute x0 -> x13, waiting for transfers between devices: none -> 43.1 us  [the longest x5 26.3 us: everywhere(): lax.ppermute(total, axis, [(i, i ^ 1 << bit) for i in range(size)])]
    psum x1 -> x0, blocking collectives: 39.7 us -> none  [body(): lax.psum((router_grad, gain_one_grad, gain_two_grad, jnp.stack([balance_p...]
    all_gather x1 -> x0, blocking collectives: 38.3 us -> none  [body(): table_all = lax.all_gather(rel_table.T, 'tensor', axis=0, tiled=True)]
  transfers between devices with their start and end apart: 32 -> 43, of which waited for: 16 -> 20; matrix products, arithmetic and copies ran while one was open for 16% -> 12% of each run, Pallas kernels for 17% -> 33%
where the time goes in v2:
time: 886 us; the launch traced here: 872 us
  Pallas kernels  317 us (36%)
  waiting for transfers between devices  310 us (35%)
  starting transfers between devices  103 us (12%)
  other arithmetic  60.8 us (7%)
  local copies, waits for them, and re-layouts  55.8 us (6%)
  between operations  16.4 us (2%)
  matrix products  9.37 us (1%)
    pallas_call x26, Pallas kernels, launch(): pl.pallas_call(drop(kernel, len(operands), len(held)), grid=grid, in_spec...  300 us
    all_to_all x12, waiting for transfers between devices, exchange(): lax.all_to_all(value, 'expert', split_axis=0, concat_axis=0, tiled=True)  139 us
    ppermute x12, waiting for transfers between devices, swap(): lax.ppermute(value, 'tensor', [(i, i ^ step) for i in range(n_tensor)])  97 us
    all_to_all x12, starting transfers between devices, exchange(): lax.all_to_all(value, 'expert', split_axis=0, concat_axis=0, tiled=True)  49.4 us
    all_gather x1, waiting for transfers between devices, body(): lax.all_gather(strip_grad, 'expert', axis=0, tiled=True).astype(F32)  29.6 us
    ppermute x5, waiting for transfers between devices, everywhere(): lax.ppermute(total, axis, [(i, i ^ 1 << bit) for i in range(size)])  26.3 us
    unnamed x103, local copies, waits for them, and re-layouts  22.1 us
    ppermute x12, starting transfers between devices, swap(): lax.ppermute(value, 'tensor', [(i, i ^ step) for i in range(n_tensor)])  19.3 us
  transfers between devices with their start and end apart: 43, of which 20 were waited for; matrix products, arithmetic and copies ran while one was open for 12% of the time, Pallas kernels for 33%

profile of v2, /device:TPU:0, one launch (start us, length us, event | category | flops | bytes accessed | tf_op | source)
XLA Modules:
  0.0 872.3 jit_solution(14062498165821595805)
XLA Ops:
  14.7 5.0 collective-permute-start.2
  24.7 17.6 %collective-permute-done.4 = f32[4,128]{1,0:T(4,128)S(1)} collective-permute-done((f32[4,128]{1,0:T(4,128)S(1)}, f32[4,128]{1,0:T(4,128)S(1)}, u32[]{:S(2)}, u32[]{:S(2)}) %collective-permute-start.4) | collective-permute-done | bytes 2080 | tf_op jit(solution)/shard_map/ppermute | solution.py:565
  68.3 12.3 %collective-permute-done.10 = bf16[2,3,128,512]{3,2,1,0:T(8,128)(2,1)S(1)} collective-permute-done((bf16[2,3,128,512]{3,2,1,0:T(8,128)(2,1)S(1)}, bf16[2,3,128,512]{3,2,1,0:T(8,128)(2,1)S(1)}, u32[]{:S(2)}, u32[]{:S(2)}) %collective-permute-start.10) | collective-permute-done | bytes 786464 | tf_op jit(solution)/shard_map/ppermute | solution.py:661
  86.4 13.2 %attend.2 = (bf16[3,512,256]{2,1,0:T(8,128)(2,1)}, bf16[512,256]{1,0:T(8,128)(2,1)}, bf16[4,512,512]{2,1,0:T(8,128)(2,1)}, f32[512,1024]{1,0:T(8,128)}) custom-call(bf16[512,1024]{1,0:T(8,128)(2,1)} %fusion.5.refs_0_, bf16[4,2,1,128,1024]{4,3,2,1,0:T(8,128)(2,1)} %bitcast.166, s32[512,512]{1,0:T(8,128)} %refs_2_.5, f32[2,2,128]{2,1,0:T(2,128)} %bitcast.212, ...), custom_call_target="tpu_custom_call" | custom-call | flops 1610612736 | bytes 9439232 | tf_op jit(solution)/shard_map/attend/pallas_call | solution.py:47
  116.4 8.6 assemble.1.refs_4_
  125.0 32.6 %attend.3 = (bf16[3,512,768]{2,1,0:T(8,128)(2,1)}, bf16[512,768]{1,0:T(8,128)(2,1)}, bf16[12,512,512]{2,1,0:T(8,128)(2,1)}, f32[512,1024]{1,0:T(8,128)}) custom-call(bf16[512,1024]{1,0:T(8,128)(2,1)} %fusion.5.refs_0_, bf16[4,2,3,128,1024]{4,3,2,1,0:T(8,128)(2,1)} %bitcast.168, s32[512,512]{1,0:T(8,128)} %refs_2_.5, f32[6,2,128]{2,1,0:T(2,128)} %bitcast.210, ...), custom_call_target="tpu_custom_call" | custom-call | flops 4831838208 | bytes 19929088 | tf_op jit(solution)/shard_map/attend/pallas_call | solution.py:47
  181.6 22.3 %all-to-all-done.2.refs_4_.refs_2_.refs_5_ = bf16[8,4,40,1024]{3,2,1,0:T(8,128)(2,1)} async-done(((bf16[8,4,40,1024]{3,2,1,0:T(8,128)(2,1)}), bf16[8,4,40,1024]{3,2,1,0:T(8,128)(2,1)}, u32[]{:S(2)}, u32[]{:S(2)}) %all-to-all-start.2) | async-done | bytes 2621472 | tf_op jit(solution)/shard_map/all_to_all | solution.py:568
  212.7 26.9 %all-to-all-done.refs_1_.refs_0_ = bf16[8,4,40,1024]{3,2,1,0:T(8,128)(2,1)S(1)} async-done(((bf16[8,4,40,1024]{3,2,1,0:T(8,128)(2,1)}), bf16[8,4,40,1024]{3,2,1,0:T(8,128)(2,1)S(1)}, u32[]{:S(2)}, u32[]{:S(2)}) %all-to-all-start) | async-done | bytes 2621472 | tf_op jit(solution)/shard_map/all_to_all | solution.py:568
  256.3 20.6 %all-to-all-done.3.refs_5_.refs_2_.refs_6_ = bf16[8,4,40,1024]{3,2,1,0:T(8,128)(2,1)S(1)} async-done(((bf16[8,4,40,1024]{3,2,1,0:T(8,128)(2,1)}), bf16[8,4,40,1024]{3,2,1,0:T(8,128)(2,1)S(1)}, u32[]{:S(2)}, u32[]{:S(2)}) %all-to-all-start.3) | async-done | bytes 2621472 | tf_op jit(solution)/shard_map/all_to_all | solution.py:568
  285.1 20.9 %experts.4 = (bf16[8,4,40,1024]{3,2,1,0:T(8,128)(2,1)}, bf16[8,4,40,1024]{3,2,1,0:T(8,128)(2,1)}, bf16[4,320,704]{2,1,0:T(8,128)(2,1)}, bf16[4,320,704]{2,1,0:T(...) custom-call(s32[1]{0:T(128)} %bitcast.9.refs_0_, bf16[8,4,40,1024]{3,2,1,0:T(8,128)(2,1)} %copy-done.18, ...), custom_call_target="tpu_custom_call" | custom-call | flops 22145925120 | bytes 34247684 | tf_op jit(solution)/shard_map/experts/pallas_call | solution.py:47
  309.6 5.8 all-to-all-done.4.refs_6_.refs_2_.refs_7_
  328.0 27.7 %all-to-all-done.5.refs_1_ = bf16[8,4,40,1024]{3,2,1,0:T(8,128)(2,1)S(1)} async-done(((bf16[8,4,40,1024]{3,2,1,0:T(8,128)(2,1)}), bf16[8,4,40,1024]{3,2,1,0:T(8,128)(2,1)S(1)}, u32[]{:S(2)}, u32[]{:S(2)}) %all-to-all-start.5) | async-done | bytes 2621472 | tf_op jit(solution)/shard_map/all_to_all | solution.py:568
  368.2 25.6 %all-to-all-done.6.refs_1_.refs_2_ = bf16[8,4,40,1024]{3,2,1,0:T(8,128)(2,1)} async-done(((bf16[8,4,40,1024]{3,2,1,0:T(8,128)(2,1)}), bf16[8,4,40,1024]{3,2,1,0:T(8,128)(2,1)}, u32[]{:S(2)}, u32[]{:S(2)}) %all-to-all-start.6) | async-done | bytes 2621472 | tf_op jit(solution)/shard_map/all_to_all | solution.py:568
  397.7 20.9 %experts.5 = (bf16[8,4,40,1024]{3,2,1,0:T(8,128)(2,1)}, bf16[8,4,40,1024]{3,2,1,0:T(8,128)(2,1)}, bf16[4,320,704]{2,1,0:T(8,128)(2,1)}, bf16[4,320,704]{2,1,0:T(...) custom-call(s32[1]{0:T(128)} %bitcast.9.refs_0_, bf16[8,4,40,1024]{3,2,1,0:T(8,128)(2,1)} %copy-done.19, ...), custom_call_target="tpu_custom_call" | custom-call | flops 22145925120 | bytes 34247684 | tf_op jit(solution)/shard_map/experts/pallas_call | solution.py:47
  418.6 21.0 %experts.6 = (bf16[8,4,40,1024]{3,2,1,0:T(8,128)(2,1)}, bf16[8,4,40,1024]{3,2,1,0:T(8,128)(2,1)}, bf16[4,320,704]{2,1,0:T(8,128)(2,1)}, bf16[4,320,704]{2,1,0:T(...) custom-call(s32[1]{0:T(128)} %bitcast.9.refs_0_, ...), custom_call_target="tpu_custom_call" | custom-call | flops 22145925120 | bytes 34247684 | tf_op jit(solution)/shard_map/experts/pallas_call | solution.py:47
  446.8 20.9 %experts.7 = (bf16[8,4,40,1024]{3,2,1,0:T(8,128)(2,1)}, bf16[8,4,40,1024]{3,2,1,0:T(8,128)(2,1)}, bf16[4,320,704]{2,1,0:T(8,128)(2,1)}, bf16[4,320,704]{2,1,0:T(...) custom-call(s32[1]{0:T(128)} %bitcast.9.refs_0_, bf16[8,4,40,1024]{3,2,1,0:T(8,128)(2,1)} %copy-done.20, ...), custom_call_target="tpu_custom_call" | custom-call | flops 22145925120 | bytes 34247684 | tf_op jit(solution)/shard_map/experts/pallas_call | solution.py:47
  467.7 10.3 %all-to-all-done.8 = bf16[8,4,40,1024]{3,2,1,0:T(8,128)(2,1)S(1)} async-done(((bf16[8,4,40,1024]{3,2,1,0:T(8,128)(2,1)}), bf16[8,4,40,1024]{3,2,1,0:T(8,128)(2,1)S(1)}, u32[]{:S(2)}, u32[]{:S(2)}) %all-to-all-start.8) | async-done | bytes 2621472 | tf_op jit(solution)/shard_map/all_to_all | solution.py:568
  490.4 29.1 %collective-permute-done.12.refs_1_ = bf16[8,4,40,1024]{3,2,1,0:T(8,128)(2,1)} collective-permute-done((bf16[8,4,40,1024]{3,2,1,0:T(8,128)(2,1)}, bf16[8,4,40,1024]{3,2,1,0:T(8,128)(2,1)}, u32[]{:S(2)}, u32[]{:S(2)}) %collective-permute-start.12) | collective-permute-done | bytes 2621472 | tf_op jit(solution)/shard_map/ppermute | solution.py:565
  519.5 6.6 add.292.refs_2_
  530.1 8.9 %collective-permute-done.13.refs_3_.refs_2_ = bf16[512,1024]{1,0:T(8,128)(2,1)} collective-permute-done((bf16[512,1024]{1,0:T(8,128)(2,1)}, bf16[512,1024]{1,0:T(8,128)(2,1)}, u32[]{:S(2)}, u32[]{:S(2)}) %collective-permute-start.13) | collective-permute-done | bytes 1048608 | tf_op jit(solution)/shard_map/ppermute | solution.py:565
  545.8 30.9 %expert_weight_grads.1 = (f32[4,704,1024]{2,1,0:T(8,128)}, f32[4,704,1024]{2,1,0:T(8,128)}, f32[4,704,1024]{2,1,0:T(8,128)}) custom-call(bf16[8,4,40,1024]{3,2,1,0:T(8,128)(2,1)} %copy-done.18, bf16[8,4,40,1024]{3,2,1,0:T(8,128)(2,1)} %copy-done.19, bf16[8,4,40,1024]{3,2,1,0:T(8,128)(2,1)} %all-to-all-done.6.refs_1_.refs_2_, ...), custom_call_target="tpu_custom_call" | custom-call | flops 29527900160 | bytes 77201408 | tf_op jit(solution)/shard_map/expert_weight_grads/pallas_call | solution.py:47
  578.2 5.2 to_tokens.6.refs_4_
  583.4 8.9 %stack.113.refs_6_ = bf16[32,4,40,1024]{3,2,1,0:T(8,128)(2,1)} custom-call(s32[4]{0:T(128)} %iota_xor_fusion.1.place_ref, bf16[8,4,40,1024]{3,2,1,0:T(8,128)(2,1)} %get-tuple-element.59.refs_2_.refs_0_, bf16[8,4,40,1024]{3,2,1,0:T(8,128)(2,1)} %get-tuple-element.60.refs_8_.refs_1_, bf16[8,4,40,1024]{3,2,1,0:T(8,128)(2,1)} %get-tuple-element.61.refs_8_.refs_2_, ...), custom_call_target="tpu_custom_call" | custom-call | tf_op jit(solution)/shard_map/stack/pallas_call | solution.py:307
  601.2 34.3 %attend_back.2 = (bf16[4,2,3,128,1024]{4,3,2,1,0:T(8,128)(2,1)}, bf16[12,512,512]{2,1,0:T(8,128)(2,1)}, f32[512,1024]{1,0:T(8,128)}) custom-call(bf16[512,1024]{1,0:T(8,128)(2,1)} %fusion.5.refs_0_, bf16[512,1024]{1,0:T(8,128)(2,1)} %fusion.38.refs_1_, bf16[4,2,3,128,1024]{4,3,2,1,0:T(8,128)(2,1)} %bitcast.169, ...), custom_call_target="tpu_custom_call" | custom-call | flops 9663676416 | bytes 32505856 | tf_op jit(solution)/shard_map/attend_back/pallas_call | solution.py:47
  643.9 14.2 %attend_back.3 = (bf16[4,2,1,128,1024]{4,3,2,1,0:T(8,128)(2,1)}, bf16[4,512,512]{2,1,0:T(8,128)(2,1)}, f32[512,1024]{1,0:T(8,128)}) custom-call(bf16[512,1024]{1,0:T(8,128)(2,1)} %fusion.5.refs_0_, bf16[512,1024]{1,0:T(8,128)(2,1)} %fusion.38.refs_1_, bf16[4,2,1,128,1024]{4,3,2,1,0:T(8,128)(2,1)} %bitcast.167, ...), custom_call_target="tpu_custom_call" | custom-call | flops 3221225472 | bytes 13631488 | tf_op jit(solution)/shard_map/attend_back/pallas_call | solution.py:47
  661.0 6.1 fusion
  671.9 23.6 %table_back.1 = f32[256,512]{1,0:T(8,128)} custom-call(bf16[4,512,512]{2,1,0:T(8,128)(2,1)} %get-tuple-element.86.refs_0_, bf16[12,512,512]{2,1,0:T(8,128)(2,1)} %get-tuple-element.87.refs_1_, s32[512,512]{1,0:T(8,128)} %refs_2_.5, bf16[4,2,1,128,1024]{4,3,2,1,0:T(8,128)(2,1)} %get-tuple-element.85.refs_3_), custom_call_target="tpu_custom_call" | custom-call | flops 17179869184 | bytes 9961472 | tf_op jit(solution)/shard_map/table_back/pallas_call | solution.py:47
  720.3 13.6 %collective-permute-start.23 = (f32[35330]{0:T(1024)S(1)}, f32[35330]{0:T(1024)S(1)}, u32[]{:S(2)}, u32[]{:S(2)}) collective-permute-start(f32[35330]{0:T(1024)S(1)} %add.205), channel_id=1, source_target_pairs={{0,1},{1,0},{2,3},{3,2},{4,5},{5,4},{6,7},{7,6},{8,9},{9,8},{10,11... | collective-permute-start | bytes 423968 | tf_op jit(solution)/shard_map/ppermute | solution.py:619
  734.0 9.6 %collective-permute-done.23 = f32[35330]{0:T(1024)S(1)} collective-permute-done((f32[35330]{0:T(1024)S(1)}, f32[35330]{0:T(1024)S(1)}, u32[]{:S(2)}, u32[]{:S(2)}) %collective-permute-start.23) | collective-permute-done | bytes 141352 | tf_op jit(solution)/shard_map/ppermute | solution.py:619
  755.2 10.7 %collective-permute-done.24 = f32[35330]{0:T(1024)} collective-permute-done((f32[35330]{0:T(1024)S(1)}, f32[35330]{0:T(1024)}, u32[]{:S(2)}, u32[]{:S(2)}) %collective-permute-start.24) | collective-permute-done | bytes 141352 | tf_op jit(solution)/shard_map/ppermute | solution.py:619
  769.7 38.5 %collective-permute-done.18.refs_2_ = bf16[128,1024]{1,0:T(8,128)(2,1)} collective-permute-done((bf16[128,1024]{1,0:T(8,128)(2,1)}, bf16[128,1024]{1,0:T(8,128)(2,1)}, u32[]{:S(2)}, u32[]{:S(2)}) %collective-permute-start.18) | collective-permute-done | bytes 262176 | tf_op jit(solution)/shard_map/ppermute | solution.py:565
  821.4 29.6 %all-gather.8.cloned.1.call-done = bf16[1024,1024]{1,0:T(8,128)(2,1)} async-done(((bf16[128,1024]{1,0:T(8,128)(2,1)}), bf16[1024,1024]{1,0:T(8,128)(2,1)}) %all-gather.8.cloned.1.call-update) | async-done | bytes 2097168 | tf_op jit(solution)/shard_map/all_gather | solution.py:792
  (302 shorter events, 273.9 us)
Async XLA Ops:
  7.2 150.4 %all-gather.4.cloned.1.call-start = ((), (), s32[]{:S(2)}) async-start(), calls=%async_computation.15 | async-start | bytes 5242880 | tf_op jit(solution)/shard_map/all_gather | solution.py:612
  14.7 33.6 %collective-permute-start.2 = (bf16[128,1024]{1,0:T(8,128)(2,1)}, bf16[128,1024]{1,0:T(8,128)(2,1)S(1)}, u32[]{:S(2)}, u32[]{:S(2)}) collective-permute-start(bf16[128,1024]{1,0:T(8,128)(2,1)} %hold.2.refs_1_), channel_id=1, source_target_pairs={{0,3},{1,2},{2,1},{3,0},{4,7},{5,6},{6,5},{7,4},{8,11},{9,10},{10,... | collective-permute-start | bytes 786440 | tf_op jit(solution)/shard_map/ppermute | solution.py:565
  19.7 28.6 %collective-permute-start.1 = (bf16[128,1024]{1,0:T(8,128)(2,1)}, bf16[128,1024]{1,0:T(8,128)(2,1)S(1)}, u32[]{:S(2)}, u32[]{:S(2)}) collective-permute-start(bf16[128,1024]{1,0:T(8,128)(2,1)} %hold.2.refs_1_), channel_id=1, source_target_pairs={{0,2},{1,3},{2,0},{3,1},{4,6},{5,7},{6,4},{7,5},{8,10},{9,11},{10,... | collective-permute-start | bytes 786440 | tf_op jit(solution)/shard_map/ppermute | solution.py:565
  19.7 28.6 %collective-permute-start = (bf16[128,1024]{1,0:T(8,128)(2,1)}, bf16[128,1024]{1,0:T(8,128)(2,1)S(1)}, u32[]{:S(2)}, u32[]{:S(2)}) collective-permute-start(bf16[128,1024]{1,0:T(8,128)(2,1)} %hold.2.refs_1_), channel_id=1, source_target_pairs={{0,1},{1,0},{2,3},{3,2},{4,5},{5,4},{6,7},{7,6},{8,9},{9,8},{10,11... | collective-permute-start | bytes 786440 | tf_op jit(solution)/shard_map/ppermute | solution.py:565
  22.7 22.1 %collective-permute-start.3 = (f32[4,128]{1,0:T(4,128)S(1)}, f32[4,128]{1,0:T(4,128)S(1)}, u32[]{:S(2)}, u32[]{:S(2)}) collective-permute-start(f32[4,128]{1,0:T(4,128)S(1)} %get-tuple-element.235), channel_id=1, source_target_pairs={{0,1},{1,0},{2,3},{3,2},{4,5},{5,4},{6,7},{7,6},{8,9},{9,8},{10,11... | collective-permute-start | bytes 6152 | tf_op jit(solution)/shard_map/ppermute | solution.py:565
  82.0 28.2 %collective-permute-start.11 = (bf16[4,3,128,512]{3,2,1,0:T(8,128)(2,1)}, bf16[4,3,128,512]{3,2,1,0:T(8,128)(2,1)}, u32[]{:S(2)}, u32[]{:S(2)}) collective-permute-start(bf16[4,3,128,512]{3,2,1,0:T(8,128)(2,1)} %pad_maximum_fusion.4.refs_4_), channel_id=1, source_target_pairs={{0,4},{4,0},{8,12},{12,8},{16,20},{20,16},{24,28},{28,24},{1,5},{5... | collective-permute-start | bytes 4718600 | tf_op jit(solution)/shard_map/ppermute | solution.py:661
  85.3 28.1 %collective-permute-start.8 = (bf16[4,3,128,512]{3,2,1,0:T(8,128)(2,1)}, bf16[4,3,128,512]{3,2,1,0:T(8,128)(2,1)}, u32[]{:S(2)}, u32[]{:S(2)}) collective-permute-start(bf16[4,3,128,512]{3,2,1,0:T(8,128)(2,1)} %pad_maximum_fusion.3.refs_3_), channel_id=1, source_target_pairs={{0,4},{4,0},{8,12},{12,8},{16,20},{20,16},{24,28},{28,24},{1,5},{5... | collective-permute-start | bytes 4718600 | tf_op jit(solution)/shard_map/ppermute | solution.py:661
  104.2 61.5 %all-to-all-start.1 = ((bf16[8,4,40,1024]{3,2,1,0:T(8,128)(2,1)}), bf16[8,4,40,1024]{3,2,1,0:T(8,128)(2,1)S(1)}, u32[]{:S(2)}, u32[]{:S(2)}) async-start(bf16[8,4,40,1024]{3,2,1,0:T(8,128)(2,1)} %bitcast.160), calls=%async_computation.1 | async-start | bytes 5242880 | tf_op jit(solution)/shard_map/all_to_all | solution.py:568
  167.2 36.7 %all-to-all-start.2 = ((bf16[8,4,40,1024]{3,2,1,0:T(8,128)(2,1)}), bf16[8,4,40,1024]{3,2,1,0:T(8,128)(2,1)}, u32[]{:S(2)}, u32[]{:S(2)}) async-start(bf16[8,4,40,1024]{3,2,1,0:T(8,128)(2,1)} %bitcast.157), calls=%async_computation.2 | async-start | bytes 5242880 | tf_op jit(solution)/shard_map/all_to_all | solution.py:568
  203.8 35.8 %all-to-all-start = ((bf16[8,4,40,1024]{3,2,1,0:T(8,128)(2,1)}), bf16[8,4,40,1024]{3,2,1,0:T(8,128)(2,1)S(1)}, u32[]{:S(2)}, u32[]{:S(2)}) async-start(bf16[8,4,40,1024]{3,2,1,0:T(8,128)(2,1)} %bitcast.159), calls=%async_computation | async-start | bytes 5242880 | tf_op jit(solution)/shard_map/all_to_all | solution.py:568
  207.5 98.5 %all-gather.6.cloned.1.call-start = ((), (), s32[]{:S(2)}) async-start(), calls=%async_computation.16 | async-start | bytes 5242880 | tf_op jit(solution)/shard_map/all_gather | solution.py:612
  241.1 35.8 %all-to-all-start.3 = ((bf16[8,4,40,1024]{3,2,1,0:T(8,128)(2,1)}), bf16[8,4,40,1024]{3,2,1,0:T(8,128)(2,1)S(1)}, u32[]{:S(2)}, u32[]{:S(2)}) async-start(bf16[8,4,40,1024]{3,2,1,0:T(8,128)(2,1)} %bitcast.158), calls=%async_computation.3 | async-start | bytes 5242880 | tf_op jit(solution)/shard_map/all_to_all | solution.py:568
  278.4 36.9 %all-to-all-start.4 = ((bf16[8,4,40,1024]{3,2,1,0:T(8,128)(2,1)}), bf16[8,4,40,1024]{3,2,1,0:T(8,128)(2,1)}, u32[]{:S(2)}, u32[]{:S(2)}) async-start(bf16[8,4,40,1024]{3,2,1,0:T(8,128)(2,1)} %bitcast.165), calls=%async_computation.4 | async-start | bytes 5242880 | tf_op jit(solution)/shard_map/all_to_all | solution.py:568
  319.8 35.8 %all-to-all-start.5 = ((bf16[8,4,40,1024]{3,2,1,0:T(8,128)(2,1)}), bf16[8,4,40,1024]{3,2,1,0:T(8,128)(2,1)S(1)}, u32[]{:S(2)}, u32[]{:S(2)}) async-start(bf16[8,4,40,1024]{3,2,1,0:T(8,128)(2,1)} %bitcast.156), calls=%async_computation.5 | async-start | bytes 5242880 | tf_op jit(solution)/shard_map/all_to_all | solution.py:568
  357.2 36.7 %all-to-all-start.6 = ((bf16[8,4,40,1024]{3,2,1,0:T(8,128)(2,1)}), bf16[8,4,40,1024]{3,2,1,0:T(8,128)(2,1)}, u32[]{:S(2)}, u32[]{:S(2)}) async-start(bf16[8,4,40,1024]{3,2,1,0:T(8,128)(2,1)} %bitcast.155), calls=%async_computation.6 | async-start | bytes 5242880 | tf_op jit(solution)/shard_map/all_to_all | solution.py:568
  393.8 45.7 %all-to-all-start.7 = ((bf16[8,4,40,1024]{3,2,1,0:T(8,128)(2,1)}), bf16[8,4,40,1024]{3,2,1,0:T(8,128)(2,1)S(1)}, u32[]{:S(2)}, u32[]{:S(2)}) async-start(bf16[8,4,40,1024]{3,2,1,0:T(8,128)(2,1)} %bitcast.164), calls=%async_computation.7 | async-start | bytes 5242880 | tf_op jit(solution)/shard_map/all_to_all | solution.py:568
  441.1 36.9 %all-to-all-start.8 = ((bf16[8,4,40,1024]{3,2,1,0:T(8,128)(2,1)}), bf16[8,4,40,1024]{3,2,1,0:T(8,128)(2,1)S(1)}, u32[]{:S(2)}, u32[]{:S(2)}) async-start(bf16[8,4,40,1024]{3,2,1,0:T(8,128)(2,1)} %get-tuple-element.65), calls=%async_computation.8 | async-start | bytes 5242880 | tf_op jit(solution)/shard_map/all_to_all | solution.py:568
  446.8 72.6 %collective-permute-start.12 = (bf16[8,4,40,1024]{3,2,1,0:T(8,128)(2,1)}, bf16[8,4,40,1024]{3,2,1,0:T(8,128)(2,1)}, u32[]{:S(2)}, u32[]{:S(2)}) collective-permute-start(bf16[8,4,40,1024]{3,2,1,0:T(8,128)(2,1)} %get-tuple-element.64), channel_id=1, source_target_pairs={{0,1},{1,0},{2,3},{3,2},{4,5},{5,4},{6,7},{7,6},{8,9},{9,8},{10,11... | collective-permute-start | bytes 7864328 | tf_op jit(solution)/shard_map/ppermute | solution.py:565
  479.6 46.5 %all-to-all-start.10 = ((bf16[8,4,40,1024]{3,2,1,0:T(8,128)(2,1)}), bf16[8,4,40,1024]{3,2,1,0:T(8,128)(2,1)}, u32[]{:S(2)}, u32[]{:S(2)}) async-start(bf16[8,4,40,1024]{3,2,1,0:T(8,128)(2,1)} %get-tuple-element.66), calls=%async_computation.10 | async-start | bytes 5242880 | tf_op jit(solution)/shard_map/all_to_all | solution.py:568
  489.8 49.2 %collective-permute-start.13 = (bf16[512,1024]{1,0:T(8,128)(2,1)}, bf16[512,1024]{1,0:T(8,128)(2,1)}, u32[]{:S(2)}, u32[]{:S(2)}) collective-permute-start(bf16[512,1024]{1,0:T(8,128)(2,1)} %to_tokens.4.refs_2_), channel_id=1, source_target_pairs={{0,2},{1,3},{2,0},{3,1},{4,6},{5,7},{6,4},{7,5},{8,10},{9,11},{10,... | collective-permute-start | bytes 3145736 | tf_op jit(solution)/shard_map/ppermute | solution.py:565
  526.1 50.6 %all-to-all-start.9 = ((bf16[8,4,40,1024]{3,2,1,0:T(8,128)(2,1)}), bf16[8,4,40,1024]{3,2,1,0:T(8,128)(2,1)S(1)}, u32[]{:S(2)}, u32[]{:S(2)}) async-start(bf16[8,4,40,1024]{3,2,1,0:T(8,128)(2,1)} %add.292.refs_2_), calls=%async_computation.9 | async-start | bytes 5242880 | tf_op jit(solution)/shard_map/all_to_all | solution.py:568
  529.9 280.4 %reduce-scatter.2.cloned.1.call-start = ((), (), s32[]{:S(2)}) async-start(), calls=%async_computation.17 | async-start | bytes 13107200 | tf_op jit(solution)/shard_map/reduce_scatter | solution.py:751
  543.4 33.2 %collective-permute-start.14 = (bf16[512,1024]{1,0:T(8,128)(2,1)}, bf16[512,1024]{1,0:T(8,128)(2,1)}, u32[]{:S(2)}, u32[]{:S(2)}) collective-permute-start(bf16[512,1024]{1,0:T(8,128)(2,1)} %to_tokens.5.refs_20_), channel_id=1, source_target_pairs={{0,3},{1,2},{2,1},{3,0},{4,7},{5,6},{6,5},{7,4},{8,11},{9,10},{10,... | collective-permute-start | bytes 3145736 | tf_op jit(solution)/shard_map/ppermute | solution.py:565
  660.4 52.6 %collective-permute-start.15 = (bf16[4,1,128,1024]{3,2,0,1:T(8,128)(2,1)}, bf16[4,1,128,1024]{3,2,0,1:T(8,128)(2,1)}, u32[]{:S(2)}, u32[]{:S(2)}) collective-permute-start(bf16[4,1,128,1024]{3,2,0,1:T(8,128)(2,1)} %dynamic-slice_bitcast_fusion.1), channel_id=1, source_target_pairs={{0,4},{4,0},{8,12},{12,8},{16,20},{20,16},{24,28},{28,24},{1,5},{5... | collective-permute-start | bytes 3145736 | tf_op jit(solution)/shard_map/ppermute | solution.py:763
  667.0 48.9 %all-to-all-start.13 = ((bf16[4,3,128,1024]{3,2,1,0:T(8,128)(2,1)}), bf16[4,3,128,1024]{3,2,1,0:T(8,128)(2,1)}, u32[]{:S(2)}, u32[]{:S(2)}) async-start(bf16[4,3,128,1024]{3,2,1,0:T(8,128)(2,1)} %fusion), calls=%async_computation.14 | async-start | bytes 6291456 | tf_op jit(solution)/shard_map/all_to_all | solution.py:767
  716.0 51.5 %all-to-all-start.12 = ((bf16[4,1,128,1024]{3,2,1,0:T(8,128)(2,1)}), bf16[4,1,128,1024]{3,2,1,0:T(8,128)(2,1)}, u32[]{:S(2)}, u32[]{:S(2)}) async-start(bf16[4,1,128,1024]{3,2,1,0:T(8,128)(2,1)} %fusion.18), calls=%async_computation.13 | async-start | bytes 2097152 | tf_op jit(solution)/shard_map/all_to_all | solution.py:767
  720.2 130.7 %all-gather.8.cloned.1.call-start = ((), (), s32[]{:S(2)}) async-start(), calls=%async_computation.18 | async-start | bytes 2359296 | tf_op jit(solution)/shard_map/all_gather | solution.py:792
  720.3 23.3 %collective-permute-start.23 = (f32[35330]{0:T(1024)S(1)}, f32[35330]{0:T(1024)S(1)}, u32[]{:S(2)}, u32[]{:S(2)}) collective-permute-start(f32[35330]{0:T(1024)S(1)} %add.205), channel_id=1, source_target_pairs={{0,1},{1,0},{2,3},{3,2},{4,5},{5,4},{6,7},{7,6},{8,9},{9,8},{10,11... | collective-permute-start | bytes 423968 | tf_op jit(solution)/shard_map/ppermute | solution.py:619
  743.6 22.3 %collective-permute-start.24 = (f32[35330]{0:T(1024)S(1)}, f32[35330]{0:T(1024)}, u32[]{:S(2)}, u32[]{:S(2)}) collective-permute-start(f32[35330]{0:T(1024)S(1)} %add.206), channel_id=1, source_target_pairs={{0,2},{1,3},{2,0},{3,1},{4,6},{5,7},{6,4},{7,5},{8,10},{9,11},{10,... | collective-permute-start | bytes 423968 | tf_op jit(solution)/shard_map/ppermute | solution.py:619
  752.1 56.1 %collective-permute-start.18 = (bf16[128,1024]{1,0:T(8,128)(2,1)}, bf16[128,1024]{1,0:T(8,128)(2,1)}, u32[]{:S(2)}, u32[]{:S(2)}) collective-permute-start(bf16[128,1024]{1,0:T(8,128)(2,1)} %get-tuple-element.208), channel_id=1, source_target_pairs={{0,2},{1,3},{2,0},{3,1},{4,6},{5,7},{6,4},{7,5},{8,10},{9,11},{10,... | collective-permute-start | bytes 786440 | tf_op jit(solution)/shard_map/ppermute | solution.py:565
  754.1 54.1 %collective-permute-start.17 = (bf16[128,1024]{1,0:T(8,128)(2,1)}, bf16[128,1024]{1,0:T(8,128)(2,1)}, u32[]{:S(2)}, u32[]{:S(2)}) collective-permute-start(bf16[128,1024]{1,0:T(8,128)(2,1)} %get-tuple-element.209), channel_id=1, source_target_pairs={{0,1},{1,0},{2,3},{3,2},{4,5},{5,4},{6,7},{7,6},{8,9},{9,8},{10,11... | collective-permute-start | bytes 786440 | tf_op jit(solution)/shard_map/ppermute | solution.py:565
  810.3 50.2 %all-to-all-start.11 = ((bf16[8,4,40,1024]{3,2,1,0:T(8,128)(2,1)}), bf16[8,4,40,1024]{3,2,1,0:T(8,128)(2,1)}, u32[]{:S(2)}, u32[]{:S(2)}) async-start(bf16[8,4,40,1024]{3,2,1,0:T(8,128)(2,1)} %reduce-scatter.2.cloned.1.call-done), calls=%async_computation.12 | async-start | bytes 5242880 | tf_op jit(solution)/shard_map/all_to_all | solution.py:568
  (58 other events, 400.4 us)
Sparse Core Ops, SparseCore 0:
  51.7 80.8 all-gather.3
  210.5 81.1 all-gather.5
  592.5 211.7 reduce-scatter.1
  810.4 40.4 all-gather.7

commit v3 on v2

--- a/solution.py
+++ b/solution.py
@@ -272,6 +272,31 @@
     )(place, *halves, *held)
 
 
+def split_kernel(in_ref, *out_refs):
+    cols = in_ref.shape[0] // 4
+    for part, ref in enumerate(out_refs):
+        rows = in_ref[part * cols : (part + 1) * cols, :].astype(F32)
+        ref[...] = rows if part == 3 else rows.T
+
+
+def split(value, after):
+    rows, width = value.shape
+    cols = rows // 4
+    tile = min(width, 256)
+    wide = pl.BlockSpec((tile, cols), lambda i: (i, 0))
+    return launch(
+        split_kernel,
+        (value,),
+        after,
+        grid=(width // tile,),
+        in_specs=[pl.BlockSpec((rows, tile), lambda i: (0, i))],
+        out_specs=[wide, wide, wide, pl.BlockSpec((cols, tile), lambda i: (0, i))],
+        out_shape=[jax.ShapeDtypeStruct((width, cols), F32)] * 3 + [jax.ShapeDtypeStruct((cols, width), F32)],
+        name="split",
+        flops=value.size,
+    )
+
+
 def copy_kernel(from_ref, to_ref):
     to_ref[...] = from_ref[...]
 
@@ -370,6 +395,43 @@
         name="to_slots",
         flops=slots * rows * width * 2,
     )
+
+
+def to_many_slots(place, ids, values, here, after):
+    chunks = place.shape[0]
+    _, rows, width = values.shape
+    count = here[0] * here[1]
+    held = [value for value in after if value is not None]
+    steps = 4
+    part = here[0] // steps
+
+    def kernel(place_ref, id_ref, x_ref, *refs):
+        out_ref = refs[-1]
+        total = part * here[1]
+        slot = lax.broadcasted_iota(jnp.int32, (total, rows), 0) + pl.program_id(1) * total
+        onehot = (slot == id_ref[0, 0:1, :]) | (slot == id_ref[0, 1:2, :])
+        out = dot(onehot.astype(F32).astype(BF), x_ref[0])
+        out_ref[...] = out.reshape(out_ref.shape).astype(BF)
+
+    return pl.pallas_call(
+        kernel,
+        grid_spec=pltpu.PrefetchScalarGridSpec(
+            num_scalar_prefetch=1,
+            grid=(chunks, steps),
+            in_specs=[
+                pl.BlockSpec((1, TOP, rows), lambda c, j, at: (c, 0, 0)),
+                pl.BlockSpec((1, rows, width), lambda c, j, at: (at[c], 0, 0)),
+            ]
+            + [pl.BlockSpec(memory_space=pl.ANY)] * len(held),
+            out_specs=pl.BlockSpec((part, 1, here[1], width), lambda c, j, at: (j, c, 0, 0)),
+        ),
+        out_shape=jax.ShapeDtypeStruct((here[0], chunks, here[1], width), BF),
+        compiler_params=pltpu.CompilerParams(vmem_limit_bytes=40 * MIB),
+        cost_estimate=pl.CostEstimate(
+            flops=2 * chunks * count * rows * width, bytes_accessed=4 * chunks * count * width, transcendentals=0
+        ),
+        name="to_many_slots",
+    )(place, ids, values, *held)
 
 
 def collect_kernel(id_ref, slot_ref, *refs):
@@ -466,8 +528,14 @@
     route_ref[...] += part
 
 
-def expert_chunk(base, x, g, other, gate_w, up_w, down_w, router_pair, after):
-    sources, here, slots, width = x.shape
+def chunk_spec(array, chunk):
+    sources, _, _, slots, width = array.shape
+    return pl.BlockSpec((sources, 1, 1, slots, width), lambda e: (0, chunk, e, 0, 0))
+
+
+def expert_chunk(base, x_at, g_at, other, gate_w, up_w, down_w, router_pair, after):
+    (x, x_chunk), (g, g_chunk) = x_at, g_at
+    sources, _, here, slots, width = x.shape
     hidden = down_w.shape[1]
     count = sources * slots
     rows = pl.BlockSpec((sources, 1, slots, width), lambda e: (0, e, 0, 0))
@@ -480,8 +548,8 @@
         grid=(here,),
         in_specs=[
             pl.BlockSpec(memory_space=pltpu.SMEM),
-            rows,
-            rows,
+            chunk_spec(x, x_chunk),
+            chunk_spec(g, g_chunk),
             pl.BlockSpec((1, count, 1), lambda e: (e, 0, 0)),
             weights,
             weights,
@@ -489,7 +557,7 @@
             pl.BlockSpec((width, 2 * LANES), lambda e: (0, 0)),
         ],
         out_specs=[rows, rows, middle, middle, middle, pl.BlockSpec((LANES, width), lambda e: (0, 0))],
-        out_shape=[jax.ShapeDtypeStruct(x.shape, BF)] * 2
+        out_shape=[jax.ShapeDtypeStruct((sources, here, slots, width), BF)] * 2
         + [jax.ShapeDtypeStruct((here, count, hidden), BF)] * 3
         + [jax.ShapeDtypeStruct((LANES, width), F32)],
         name="experts",
@@ -508,17 +576,16 @@
 
 
 def weight_grads(xs, gs, hidden, gates, ups, after):
-    sources, here, slots, width = xs[0].shape
+    sources, _, here, slots, width = xs[0][0].shape
     depth = hidden[0].shape[2]
-    rows = pl.BlockSpec((sources, 1, slots, width), lambda e: (0, e, 0, 0))
     middle = pl.BlockSpec((1, sources * slots, depth), lambda e: (e, 0, 0))
     chunks = len(xs)
     return launch(
         functools.partial(weight_kernel, chunks=chunks),
-        (*xs, *gs, *hidden, *gates, *ups),
+        (*[v for v, _ in xs], *[v for v, _ in gs], *hidden, *gates, *ups),
         after,
         grid=(here,),
-        in_specs=[rows] * (2 * chunks) + [middle] * (3 * chunks),
+        in_specs=[chunk_spec(*v) for v in (*xs, *gs)] + [middle] * (3 * chunks),
         out_specs=[pl.BlockSpec((1, depth, width), lambda e: (e, 0, 0))] * 3,
         out_shape=[jax.ShapeDtypeStruct((here, depth, width), F32)] * 3,
         name="expert_weight_grads",
@@ -648,7 +715,8 @@
     inputs_f = inputs.astype(F32)
     normed_one = rms_scale(inputs_f, gain_one).astype(BF)
     attn_in = whole_seq(normed_one)
-    grad_far = gather(ordered(hold, grad_out, after=(strips, table_all)))
+    grad_low = ordered(hold, grad_out, after=(strips, table_all))
+    grad_all = lax.all_gather(grad_low, "tensor", axis=0, tiled=True).reshape(n_tensor, rows, width)
     own_part = ordered(attend, attn_in, own_w, buckets, table_all[:pairs])
 
     bits = [1 << i for i in range(1, n_expert.bit_length() - 1)]
@@ -665,20 +733,22 @@
         places.append(jnp.sum(jnp.where(sources[:, None] == jnp.arange(n_expert), where, 0), 1))
     places = jnp.stack(places).astype(jnp.int32)
 
-    grad_slots = {0: send(0, grad_out, (came[len(bits)], came[-1]))}
+    grad_own = send(0, grad_out, (came[len(bits)], came[-1]))
     attn_w = ordered(assemble, places, halves)
+    others = jnp.arange(1, n_tensor, dtype=jnp.int32) ^ at_tensor
+    grad_rest = exchange(
+        ordered(to_many_slots, others, own_ids[1:], grad_all, (n_expert, here * cap), after=(grad_own,))
+    )
+    grad_slots = {0: (grad_own, 0)} | {i: (grad_rest, i - 1) for i in steps[1:]}
     attn_w = attn_w.reshape(blocks, n_expert // blocks, n_tensor - 1, strip, width)
     attn_w = jnp.swapaxes(attn_w, 1, 2).reshape(4, pairs, n_tensor - 1, LANES, width)
     rest_part = ordered(attend, attn_in, attn_w, buckets, table_all[pairs:])
-    grad_slots[1] = send(1, grad_far[1])
     resid = inputs_f + own_rows(own_part[3] + rest_part[3])
     normed_two = rms_scale(resid, gain_two)
     normed_low = normed_two.astype(BF)
 
     token_far = gather(normed_low)
-    token_slots = {0: send(0, normed_low)}
-    for i in far:
-        grad_slots[i] = send(i, grad_far[i])
+    token_slots = {0: send(0, normed_low, (grad_rest,))}
 
     counts = jnp.sum((routes.T[:, None, :] == labels[:, None]).astype(F32), axis=(0, 2))
     route_share = counts / (tokens * TOP)
@@ -704,9 +774,11 @@
     up_w = jnp.swapaxes(w_up, 1, 2)
 
     def rows_in(value):
+        value, chunk = value
         if cap % 8 == 0:
-            return value
-        return jnp.swapaxes(value, 0, 1).reshape(1, here, n_expert * cap, width)
+            return value.reshape(n_expert, -1, here, cap, width), chunk
+        value = value.reshape(n_expert, -1, here, cap, width)[:, chunk]
+        return jnp.swapaxes(value, 0, 1).reshape(1, 1, here, n_expert * cap, width), 0
 
     def rows_out(value):
         if cap % 8 == 0:
@@ -716,16 +788,17 @@
     xs, gs, done = {}, {}, {}
 
     def work(step):
-        xs[step], gs[step] = rows_in(token_slots[step]), rows_in(grad_slots[step])
+        xs[step], gs[step] = rows_in((token_slots[step], 0)), rows_in(grad_slots[step])
         done[step] = ordered(
             expert_chunk, base, xs[step], gs[step], partners[step], gate_w, up_w, w_down, router_pair
         )
 
+    token_slots[1] = send(1, token_far[1])
     work(0)
-    for i in steps[1:]:
-        token_slots[i] = send(i, token_far[i], (*grad_slots.values(),))
-    for i in steps[1:]:
-        work(i)
+    for i in far:
+        token_slots[i] = send(i, token_far[i])
+        work(i - 1)
+    work(n_tensor - 1)
     backs = {i: rows_out(done[i][1]) for i in steps}
     outs = {i: rows_out(done[i][0]) for i in steps}
     moe_far, near = [], None
@@ -789,16 +862,17 @@
         strip_grad = (strip_grad.astype(F32) / share).astype(BF)
     output = home(0, out_sum, (resid,), BF)
 
-    attn_w_grad = lax.all_gather(strip_grad, "expert", axis=0, tiled=True).astype(F32)
+    attn_w_grad = lax.all_gather(strip_grad, "expert", axis=0, tiled=True)
+    query_grad, key_grad, value_grad, out_proj_grad = ordered(split, attn_w_grad)
     table_total = lax.dynamic_index_in_dim(table_total, at_tensor, 0, keepdims=False).T
     return (
         output,
         input_grad,
         gain_one_total,
-        attn_w_grad[:head_cols].T,
-        attn_w_grad[head_cols : 2 * head_cols].T,
-        attn_w_grad[2 * head_cols : 3 * head_cols].T,
-        attn_w_grad[3 * head_cols :],
+        query_grad,
+        key_grad,
+        value_grad,
+        out_proj_grad,
         table_total,
         gain_two_total,
         router_total.T,

time: 886 us -> 831 us (0.938)
  waiting for transfers between devices: 310 us -> 282 us
  starting transfers between devices: 103 us -> 92.4 us
  local copies, waits for them, and re-layouts: 55.8 us -> 46.3 us
    all_gather x1 -> x2, waiting for transfers between devices: 29.6 us -> 8.76 us  [the longest x1 8.75 us: body(): lax.all_gather(grad_low, 'tensor', axis=0, tiled=True)]
    all_gather x2 -> x1, waiting for transfers between devices: 0.04 us -> 13.7 us  [gather(): lax.all_gather(value, 'tensor', axis=0, tiled=True)]
    pallas_call x0 -> x1, Pallas kernels: none -> 9.27 us  [to_many_slots(): pl.pallas_call(kernel, grid_spec=pltpu.PrefetchScalarGridSpec(num_scalar_...]
    pallas_call x26 -> x24, Pallas kernels: 300 us -> 291 us  [launch(): pl.pallas_call(drop(kernel, len(operands), len(held)), grid=grid, in_spec...]
    all_to_all x12 -> x10, starting transfers between devices: 49.4 us -> 42.5 us  [exchange(): lax.all_to_all(value, 'expert', split_axis=0, concat_axis=0, tiled=True)]
    all_to_all x12 -> x10, waiting for transfers between devices: 139 us -> 133 us  [exchange(): lax.all_to_all(value, 'expert', split_axis=0, concat_axis=0, tiled=True)]
    unnamed x103 -> x104, local copies, waits for them, and re-layouts: 22.1 us -> 17.2 us
  transfers between devices with their start and end apart: 43 -> 41, of which waited for: 20 -> 23; matrix products, arithmetic and copies ran while one was open for 12% -> 12% of each run, Pallas kernels for 33% -> 35%
where the time goes in v3:
time: 831 us; the launch traced here: 821 us
  Pallas kernels  318 us (38%)
  waiting for transfers between devices  282 us (34%)
  starting transfers between devices  92.4 us (11%)
  other arithmetic  56.2 us (7%)
  local copies, waits for them, and re-layouts  46.3 us (6%)
  between operations  16.5 us (2%)
  matrix products  9.38 us (1%)
    pallas_call x24, Pallas kernels, launch(): pl.pallas_call(drop(kernel, len(operands), len(held)), grid=grid, in_spec...  291 us
    all_to_all x10, waiting for transfers between devices, exchange(): lax.all_to_all(value, 'expert', split_axis=0, concat_axis=0, tiled=True)  133 us
    ppermute x12, waiting for transfers between devices, swap(): lax.ppermute(value, 'tensor', [(i, i ^ step) for i in range(n_tensor)])  90.6 us
    all_to_all x10, starting transfers between devices, exchange(): lax.all_to_all(value, 'expert', split_axis=0, concat_axis=0, tiled=True)  42.5 us
    ppermute x5, waiting for transfers between devices, everywhere(): lax.ppermute(total, axis, [(i, i ^ 1 << bit) for i in range(size)])  27.5 us
    ppermute x5, starting transfers between devices, everywhere(): lax.ppermute(total, axis, [(i, i ^ 1 << bit) for i in range(size)])  18.5 us
    unnamed x104, local copies, waits for them, and re-layouts  17.2 us
  transfers between devices with their start and end apart: 41, of which 23 were waited for; matrix products, arithmetic and copies ran while one was open for 12% of the time, Pallas kernels for 35%

profile of v3, /device:TPU:0, one launch (start us, length us, event | category | flops | bytes accessed | tf_op | source)
XLA Modules:
  0.0 820.7 jit_solution(5214084835868171646)
XLA Ops:
  33.0 13.2 %collective-permute-done.1 = bf16[128,1024]{1,0:T(8,128)(2,1)S(1)} collective-permute-done((bf16[128,1024]{1,0:T(8,128)(2,1)}, bf16[128,1024]{1,0:T(8,128)(2,1)S(1)}, u32[]{:S(2)}, u32[]{:S(2)}) %collective-permute-start.1) | collective-permute-done | bytes 262176 | tf_op jit(solution)/shard_map/ppermute | solution.py:632
  64.4 13.3 %attend.2 = (bf16[3,512,256]{2,1,0:T(8,128)(2,1)}, bf16[512,256]{1,0:T(8,128)(2,1)}, bf16[4,512,512]{2,1,0:T(8,128)(2,1)}, f32[512,1024]{1,0:T(8,128)}) custom-call(bf16[512,1024]{1,0:T(8,128)(2,1)} %fusion.5.refs_0_, bf16[4,2,1,128,1024]{4,3,2,1,0:T(8,128)(2,1)} %bitcast.162, s32[512,512]{1,0:T(8,128)} %refs_2_.5, f32[2,2,128]{2,1,0:T(2,128)} %bitcast.16.refs_3_, ...), custom_call_target="tpu_custom_call" | custom-call | flops 1610612736 | bytes 9439232 | tf_op jit(solution)/shard_map/attend/pallas_call | solution.py:47
  98.3 8.5 %assemble.1.refs_0_ = bf16[8,3,128,1024]{3,2,1,0:T(8,128)(2,1)} custom-call(s32[2,8]{1,0:T(2,128)} %pad_add_fusion.2.place_ref, bf16[8,3,128,512]{3,2,1,0:T(8,128)(2,1)} %pad_maximum_fusion.refs_0_, bf16[8,3,128,512]{3,2,1,0:T(8,128)(2,1)} %pad_maximum_fusion.1.refs_1_, bf16[1280,1024]{1,0:T(8,128)(2,1)} %to_slots.5.refs_2_), custom_call_target="tpu_custom_call" | custom-call | bytes 12582912 | tf_op jit(solution)/shard_map/assemble/pallas_call | solution.py:257
  106.8 15.0 %all-to-all-done.refs_1_ = bf16[8,4,40,1024]{3,2,1,0:T(8,128)(2,1)S(1)} async-done(((bf16[8,4,40,1024]{3,2,1,0:T(8,128)(2,1)}), bf16[8,4,40,1024]{3,2,1,0:T(8,128)(2,1)S(1)}, u32[]{:S(2)}, u32[]{:S(2)}) %all-to-all-start) | async-done | bytes 2621472 | tf_op jit(solution)/shard_map/all_to_all | solution.py:635
  121.8 8.8 %all-gather.4.cloned.1.call-done = bf16[2048,1024]{1,0:T(8,128)(2,1)} async-done(((bf16[512,1024]{1,0:T(8,128)(2,1)}), bf16[2048,1024]{1,0:T(8,128)(2,1)}) %all-gather.4.cloned.1.call-update) | async-done | bytes 4194320 | tf_op jit(solution)/shard_map/all_gather | solution.py:719
  135.5 9.3 %to_many_slots.1.refs_4_ = bf16[8,3,160,1024]{3,2,1,0:T(8,128)(2,1)} custom-call(s32[3]{0:T(128)S(1)} %add_xor_fusion.place_ref, s32[3,2,512]{2,1,0:T(2,128)S(1)} %pad_add_fusion.1.id_ref, bf16[4,512,1024]{2,1,0:T(8,128)(2,1)S(1)} %bitcast.153, bf16[8,3,128,1024]{3,2,1,0:T(8,128)(2,1)S(1)} %copy-done, bf16[8,4,40,1024]{3,2,1,0:T(8,128)(2,1)S(1)} %all-to-all-done.refs_1_), custom_call_target="tpu_custom_call" | custom-call | flops 4026531840 | bytes 15728640 | tf_op jit(solution)/shard_map/to_many_slots/pallas_call | solution.py:416
  151.1 32.7 %attend.3 = (bf16[3,512,768]{2,1,0:T(8,128)(2,1)}, bf16[512,768]{1,0:T(8,128)(2,1)}, bf16[12,512,512]{2,1,0:T(8,128)(2,1)}, f32[512,1024]{1,0:T(8,128)}) custom-call(bf16[512,1024]{1,0:T(8,128)(2,1)} %fusion.5.refs_0_, bf16[4,2,3,128,1024]{4,3,2,1,0:T(8,128)(2,1)} %bitcast.149, s32[512,512]{1,0:T(8,128)} %refs_2_.5, f32[6,2,128]{2,1,0:T(2,128)} %bitcast.201, ...), custom_call_target="tpu_custom_call" | custom-call | flops 4831838208 | bytes 19929088 | tf_op jit(solution)/shard_map/attend/pallas_call | solution.py:47
  188.5 49.8 %all-to-all-done.1.refs_3_ = bf16[8,3,160,1024]{3,2,1,0:T(8,128)(2,1)} async-done(((bf16[8,3,160,1024]{3,2,1,0:T(8,128)(2,1)}), bf16[8,3,160,1024]{3,2,1,0:T(8,128)(2,1)}, u32[]{:S(2)}, u32[]{:S(2)}) %all-to-all-start.1) | async-done | bytes 7864352 | tf_op jit(solution)/shard_map/all_to_all | solution.py:635
  254.6 13.7 %all-gather.6.cloned.1.call-done = bf16[2048,1024]{1,0:T(8,128)(2,1)} async-done(((bf16[512,1024]{1,0:T(8,128)(2,1)}), bf16[2048,1024]{1,0:T(8,128)(2,1)}) %all-gather.6.cloned.1.call-update) | async-done | bytes 4194320 | tf_op jit(solution)/shard_map/all_gather | solution.py:679
  285.7 20.9 %experts.4 = (bf16[8,4,40,1024]{3,2,1,0:T(8,128)(2,1)}, bf16[8,4,40,1024]{3,2,1,0:T(8,128)(2,1)}, bf16[4,320,704]{2,1,0:T(8,128)(2,1)}, bf16[4,320,704]{2,1,0:T(...) custom-call(s32[1]{0:T(128)} %bitcast.9.refs_0_, bf16[8,1,4,40,1024]{4,3,2,1,0:T(8,128)(2,1)} %bitcast.165, ...), custom_call_target="tpu_custom_call" | custom-call | flops 22145925120 | bytes 34247684 | tf_op jit(solution)/shard_map/experts/pallas_call | solution.py:47
  311.1 6.0 all-to-all-done.3
  321.8 20.9 %experts.5 = (bf16[8,4,40,1024]{3,2,1,0:T(8,128)(2,1)}, bf16[8,4,40,1024]{3,2,1,0:T(8,128)(2,1)}, bf16[4,320,704]{2,1,0:T(8,128)(2,1)}, bf16[4,320,704]{2,1,0:T(...) custom-call(s32[1]{0:T(128)} %bitcast.9.refs_0_, bf16[8,1,4,40,1024]{4,3,2,1,0:T(8,128)(2,1)} %bitcast.52.refs_1_, ...), custom_call_target="tpu_custom_call" | custom-call | flops 22145925120 | bytes 39490564 | tf_op jit(solution)/shard_map/experts/pallas_call | solution.py:47
  347.2 5.7 all-to-all-done.4
  360.3 20.9 %experts.6 = (bf16[8,4,40,1024]{3,2,1,0:T(8,128)(2,1)}, bf16[8,4,40,1024]{3,2,1,0:T(8,128)(2,1)}, bf16[4,320,704]{2,1,0:T(8,128)(2,1)}, bf16[4,320,704]{2,1,0:T(...) custom-call(s32[1]{0:T(128)} %bitcast.9.refs_0_, bf16[8,1,4,40,1024]{4,3,2,1,0:T(8,128)(2,1)} %bitcast.167, ...), custom_call_target="tpu_custom_call" | custom-call | flops 22145925120 | bytes 39490564 | tf_op jit(solution)/shard_map/experts/pallas_call | solution.py:47
  381.2 10.3 %all-to-all-done.5 = bf16[8,4,40,1024]{3,2,1,0:T(8,128)(2,1)} async-done(((bf16[8,4,40,1024]{3,2,1,0:T(8,128)(2,1)}), bf16[8,4,40,1024]{3,2,1,0:T(8,128)(2,1)}, u32[]{:S(2)}, u32[]{:S(2)}) %all-to-all-start.5) | async-done | bytes 2621472 | tf_op jit(solution)/shard_map/all_to_all | solution.py:635
  396.2 20.9 %experts.7 = (bf16[8,4,40,1024]{3,2,1,0:T(8,128)(2,1)}, bf16[8,4,40,1024]{3,2,1,0:T(8,128)(2,1)}, bf16[4,320,704]{2,1,0:T(8,128)(2,1)}, bf16[4,320,704]{2,1,0:T(...) custom-call(s32[1]{0:T(128)} %bitcast.9.refs_0_, bf16[8,1,4,40,1024]{4,3,2,1,0:T(8,128)(2,1)} %bitcast.61.refs_1_.refs_3_, ...), custom_call_target="tpu_custom_call" | custom-call | flops 22145925120 | bytes 39490564 | tf_op jit(solution)/shard_map/experts/pallas_call | solution.py:47
  417.2 10.2 %all-to-all-done.6 = bf16[8,4,40,1024]{3,2,1,0:T(8,128)(2,1)S(1)} async-done(((bf16[8,4,40,1024]{3,2,1,0:T(8,128)(2,1)}), bf16[8,4,40,1024]{3,2,1,0:T(8,128)(2,1)S(1)}, u32[]{:S(2)}, u32[]{:S(2)}) %all-to-all-start.6) | async-done | bytes 2621472 | tf_op jit(solution)/shard_map/all_to_all | solution.py:635
  440.6 28.1 %collective-permute-done.12.refs_1_ = bf16[8,4,40,1024]{3,2,1,0:T(8,128)(2,1)} collective-permute-done((bf16[8,4,40,1024]{3,2,1,0:T(8,128)(2,1)}, bf16[8,4,40,1024]{3,2,1,0:T(8,128)(2,1)}, u32[]{:S(2)}, u32[]{:S(2)}) %collective-permute-start.12) | collective-permute-done | bytes 2621472 | tf_op jit(solution)/shard_map/ppermute | solution.py:632
  468.6 6.5 add.298.refs_2_
  479.2 9.0 %collective-permute-done.13.refs_3_.refs_2_ = bf16[512,1024]{1,0:T(8,128)(2,1)} collective-permute-done((bf16[512,1024]{1,0:T(8,128)(2,1)}, bf16[512,1024]{1,0:T(8,128)(2,1)}, u32[]{:S(2)}, u32[]{:S(2)}) %collective-permute-start.13) | collective-permute-done | bytes 1048608 | tf_op jit(solution)/shard_map/ppermute | solution.py:632
  493.3 31.3 %expert_weight_grads.1 = (f32[4,704,1024]{2,1,0:T(8,128)}, f32[4,704,1024]{2,1,0:T(8,128)}, f32[4,704,1024]{2,1,0:T(8,128)}) custom-call(bf16[8,1,4,40,1024]{4,3,2,1,0:T(8,128)(2,1)} %bitcast.166, bf16[8,1,4,40,1024]{4,3,2,1,0:T(8,128)(2,1)} %bitcast.52.refs_1_, bf16[8,1,4,40,1024]{4,3,2,1,0:T(8,128)(2,1)} %bitcast.168, ...), custom_call_target="tpu_custom_call" | custom-call | flops 29527900160 | bytes 92930048 | tf_op jit(solution)/shard_map/expert_weight_grads/pallas_call | solution.py:47
  526.1 5.1 to_tokens.6.refs_4_
  531.2 9.0 %stack.116.refs_6_ = bf16[32,4,40,1024]{3,2,1,0:T(8,128)(2,1)} custom-call(s32[4]{0:T(128)} %iota_xor_fusion.1.place_ref, bf16[8,4,40,1024]{3,2,1,0:T(8,128)(2,1)} %get-tuple-element.63.refs_2_.refs_0_, bf16[8,4,40,1024]{3,2,1,0:T(8,128)(2,1)} %get-tuple-element.64.refs_2_.refs_1_, bf16[8,4,40,1024]{3,2,1,0:T(8,128)(2,1)} %get-tuple-element.65.refs_8_.refs_2_, ...), custom_call_target="tpu_custom_call" | custom-call | tf_op jit(solution)/shard_map/stack/pallas_call | solution.py:332
  549.2 34.3 %attend_back.2 = (bf16[4,2,3,128,1024]{4,3,2,1,0:T(8,128)(2,1)}, bf16[12,512,512]{2,1,0:T(8,128)(2,1)}, f32[512,1024]{1,0:T(8,128)}) custom-call(bf16[512,1024]{1,0:T(8,128)(2,1)} %fusion.5.refs_0_, bf16[512,1024]{1,0:T(8,128)(2,1)} %fusion.38.refs_1_, bf16[4,2,3,128,1024]{4,3,2,1,0:T(8,128)(2,1)} %bitcast.150, ...), custom_call_target="tpu_custom_call" | custom-call | flops 9663676416 | bytes 32505856 | tf_op jit(solution)/shard_map/attend_back/pallas_call | solution.py:47
  591.9 14.1 %attend_back.3 = (bf16[4,2,1,128,1024]{4,3,2,1,0:T(8,128)(2,1)}, bf16[4,512,512]{2,1,0:T(8,128)(2,1)}, f32[512,1024]{1,0:T(8,128)}) custom-call(bf16[512,1024]{1,0:T(8,128)(2,1)} %fusion.5.refs_0_, bf16[512,1024]{1,0:T(8,128)(2,1)} %fusion.38.refs_1_, bf16[4,2,1,128,1024]{4,3,2,1,0:T(8,128)(2,1)} %bitcast.163, ...), custom_call_target="tpu_custom_call" | custom-call | flops 3221225472 | bytes 13631488 | tf_op jit(solution)/shard_map/attend_back/pallas_call | solution.py:47
  608.8 6.1 fusion
  619.8 23.6 %table_back.1 = f32[256,512]{1,0:T(8,128)} custom-call(bf16[4,512,512]{2,1,0:T(8,128)(2,1)} %get-tuple-element.90.refs_0_, bf16[12,512,512]{2,1,0:T(8,128)(2,1)} %get-tuple-element.91.refs_1_, s32[512,512]{1,0:T(8,128)} %refs_2_.5, bf16[4,2,1,128,1024]{4,3,2,1,0:T(8,128)(2,1)} %get-tuple-element.89.refs_3_), custom_call_target="tpu_custom_call" | custom-call | flops 17179869184 | bytes 9961472 | tf_op jit(solution)/shard_map/table_back/pallas_call | solution.py:47
  668.3 13.8 %collective-permute-start.23 = (f32[35330]{0:T(1024)S(1)}, f32[35330]{0:T(1024)S(1)}, u32[]{:S(2)}, u32[]{:S(2)}) collective-permute-start(f32[35330]{0:T(1024)S(1)} %add.206), channel_id=1, source_target_pairs={{0,1},{1,0},{2,3},{3,2},{4,5},{5,4},{6,7},{7,6},{8,9},{9,8},{10,11... | collective-permute-start | bytes 423968 | tf_op jit(solution)/shard_map/ppermute | solution.py:686
  682.1 10.4 %collective-permute-done.23 = f32[35330]{0:T(1024)S(1)} collective-permute-done((f32[35330]{0:T(1024)S(1)}, f32[35330]{0:T(1024)S(1)}, u32[]{:S(2)}, u32[]{:S(2)}) %collective-permute-start.23) | collective-permute-done | bytes 141352 | tf_op jit(solution)/shard_map/ppermute | solution.py:686
  704.5 11.3 %collective-permute-done.24 = f32[35330]{0:T(1024)} collective-permute-done((f32[35330]{0:T(1024)S(1)}, f32[35330]{0:T(1024)}, u32[]{:S(2)}, u32[]{:S(2)}) %collective-permute-start.24) | collective-permute-done | bytes 141352 | tf_op jit(solution)/shard_map/ppermute | solution.py:686
  719.5 38.0 %collective-permute-done.18.refs_2_ = bf16[128,1024]{1,0:T(8,128)(2,1)} collective-permute-done((bf16[128,1024]{1,0:T(8,128)(2,1)}, bf16[128,1024]{1,0:T(8,128)(2,1)}, u32[]{:S(2)}, u32[]{:S(2)}) %collective-permute-start.18) | collective-permute-done | bytes 262176 | tf_op jit(solution)/shard_map/ppermute | solution.py:632
  770.6 34.1 %all-to-all-done.9 = bf16[8,4,40,1024]{3,2,1,0:T(8,128)(2,1)} async-done(((bf16[8,4,40,1024]{3,2,1,0:T(8,128)(2,1)}), bf16[8,4,40,1024]{3,2,1,0:T(8,128)(2,1)}, u32[]{:S(2)}, u32[]{:S(2)}) %all-to-all-start.9) | async-done | bytes 2621472 | tf_op jit(solution)/shard_map/all_to_all | solution.py:635
  (296 shorter events, 249.6 us)
Async XLA Ops:
  7.2 123.4 %all-gather.4.cloned.1.call-start = ((), (), s32[]{:S(2)}) async-start(), calls=%async_computation.13 | async-start | bytes 5242880 | tf_op jit(solution)/shard_map/all_gather | solution.py:719
  8.6 17.9 %collective-permute-start.4 = (f32[4,128]{1,0:T(4,128)}, f32[4,128]{1,0:T(4,128)}, u32[]{:S(2)}, u32[]{:S(2)}) collective-permute-start(f32[4,128]{1,0:T(4,128)} %get-tuple-element.153), channel_id=1, source_target_pairs={{0,2},{1,3},{2,0},{3,1},{4,6},{5,7},{6,4},{7,5},{8,10},{9,11},{10,... | collective-permute-start | bytes 6152 | tf_op jit(solution)/shard_map/ppermute | solution.py:632
  12.6 16.7 %collective-permute-start.3 = (f32[4,128]{1,0:T(4,128)}, f32[4,128]{1,0:T(4,128)}, u32[]{:S(2)}, u32[]{:S(2)}) collective-permute-start(f32[4,128]{1,0:T(4,128)} %get-tuple-element.153), channel_id=1, source_target_pairs={{0,1},{1,0},{2,3},{3,2},{4,5},{5,4},{6,7},{7,6},{8,9},{9,8},{10,11... | collective-permute-start | bytes 6152 | tf_op jit(solution)/shard_map/ppermute | solution.py:632
  25.4 20.8 %collective-permute-start.1 = (bf16[128,1024]{1,0:T(8,128)(2,1)}, bf16[128,1024]{1,0:T(8,128)(2,1)S(1)}, u32[]{:S(2)}, u32[]{:S(2)}) collective-permute-start(bf16[128,1024]{1,0:T(8,128)(2,1)} %hold.2.refs_1_), channel_id=1, source_target_pairs={{0,2},{1,3},{2,0},{3,1},{4,6},{5,7},{6,4},{7,5},{8,10},{9,11},{10,... | collective-permute-start | bytes 786440 | tf_op jit(solution)/shard_map/ppermute | solution.py:632
  26.5 19.7 %collective-permute-start = (bf16[128,1024]{1,0:T(8,128)(2,1)S(1)}, bf16[128,1024]{1,0:T(8,128)(2,1)S(1)}, u32[]{:S(2)}, u32[]{:S(2)}) collective-permute-start(bf16[128,1024]{1,0:T(8,128)(2,1)S(1)} %copy-done.28), channel_id=1, source_target_pairs={{0,1},{1,0},{2,3},{3,2},{4,5},{5,4},{6,7},{7,6},{8,9},{9,8},{10,11... | collective-permute-start | bytes 786440 | tf_op jit(solution)/shard_map/ppermute | solution.py:632
  59.0 18.8 %collective-permute-start.7 = (bf16[2,3,128,512]{3,2,1,0:T(8,128)(2,1)S(1)}, bf16[2,3,128,512]{3,2,1,0:T(8,128)(2,1)S(1)}, u32[]{:S(2)}, u32[]{:S(2)}) collective-permute-start(bf16[2,3,128,512]{3,2,1,0:T(8,128)(2,1)S(1)} %pad_maximum_fusion.6), channel_id=1, source_target_pairs={{0,16},{4,20},{8,24},{12,28},{16,0},{20,4},{24,8},{28,12},{1,17},{... | collective-permute-start | bytes 2359304 | tf_op jit(solution)/shard_map/ppermute | solution.py:729
  63.0 16.2 %collective-permute-start.10 = (bf16[2,3,128,512]{3,2,1,0:T(8,128)(2,1)S(1)}, bf16[2,3,128,512]{3,2,1,0:T(8,128)(2,1)S(1)}, u32[]{:S(2)}, u32[]{:S(2)}) collective-permute-start(bf16[2,3,128,512]{3,2,1,0:T(8,128)(2,1)S(1)} %pad_maximum_fusion.7), channel_id=1, source_target_pairs={{0,8},{4,12},{8,0},{12,4},{16,24},{20,28},{24,16},{28,20},{1,9},{5... | collective-permute-start | bytes 2359304 | tf_op jit(solution)/shard_map/ppermute | solution.py:729
  85.1 36.7 %all-to-all-start = ((bf16[8,4,40,1024]{3,2,1,0:T(8,128)(2,1)}), bf16[8,4,40,1024]{3,2,1,0:T(8,128)(2,1)S(1)}, u32[]{:S(2)}, u32[]{:S(2)}) async-start(bf16[8,4,40,1024]{3,2,1,0:T(8,128)(2,1)} %bitcast.155), calls=%async_computation | async-start | bytes 5242880 | tf_op jit(solution)/shard_map/all_to_all | solution.py:635
  144.8 93.4 %all-to-all-start.1 = ((bf16[8,3,160,1024]{3,2,1,0:T(8,128)(2,1)}), bf16[8,3,160,1024]{3,2,1,0:T(8,128)(2,1)}, u32[]{:S(2)}, u32[]{:S(2)}) async-start(bf16[8,3,160,1024]{3,2,1,0:T(8,128)(2,1)} %to_many_slots.1.refs_4_), calls=%async_computation.1 | async-start | bytes 15728640 | tf_op jit(solution)/shard_map/all_to_all | solution.py:635
  149.8 118.5 %all-gather.6.cloned.1.call-start = ((), (), s32[]{:S(2)}) async-start(), calls=%async_computation.14 | async-start | bytes 5242880 | tf_op jit(solution)/shard_map/all_gather | solution.py:679
  242.7 36.0 %all-to-all-start.2 = ((bf16[8,4,40,1024]{3,2,1,0:T(8,128)(2,1)}), bf16[8,4,40,1024]{3,2,1,0:T(8,128)(2,1)S(1)}, u32[]{:S(2)}, u32[]{:S(2)}) async-start(bf16[8,4,40,1024]{3,2,1,0:T(8,128)(2,1)} %bitcast.154), calls=%async_computation.2 | async-start | bytes 5242880 | tf_op jit(solution)/shard_map/all_to_all | solution.py:635
  280.2 36.9 %all-to-all-start.3 = ((bf16[8,4,40,1024]{3,2,1,0:T(8,128)(2,1)}), bf16[8,4,40,1024]{3,2,1,0:T(8,128)(2,1)}, u32[]{:S(2)}, u32[]{:S(2)}) async-start(bf16[8,4,40,1024]{3,2,1,0:T(8,128)(2,1)} %bitcast.159), calls=%async_computation.3 | async-start | bytes 5242880 | tf_op jit(solution)/shard_map/all_to_all | solution.py:635
  317.1 35.8 %all-to-all-start.4 = ((bf16[8,4,40,1024]{3,2,1,0:T(8,128)(2,1)}), bf16[8,4,40,1024]{3,2,1,0:T(8,128)(2,1)S(1)}, u32[]{:S(2)}, u32[]{:S(2)}) async-start(bf16[8,4,40,1024]{3,2,1,0:T(8,128)(2,1)} %bitcast.160), calls=%async_computation.4 | async-start | bytes 5242880 | tf_op jit(solution)/shard_map/all_to_all | solution.py:635
  354.4 37.1 %all-to-all-start.5 = ((bf16[8,4,40,1024]{3,2,1,0:T(8,128)(2,1)}), bf16[8,4,40,1024]{3,2,1,0:T(8,128)(2,1)}, u32[]{:S(2)}, u32[]{:S(2)}) async-start(bf16[8,4,40,1024]{3,2,1,0:T(8,128)(2,1)} %bitcast.161), calls=%async_computation.5 | async-start | bytes 5242880 | tf_op jit(solution)/shard_map/all_to_all | solution.py:635
  391.5 35.8 %all-to-all-start.6 = ((bf16[8,4,40,1024]{3,2,1,0:T(8,128)(2,1)}), bf16[8,4,40,1024]{3,2,1,0:T(8,128)(2,1)S(1)}, u32[]{:S(2)}, u32[]{:S(2)}) async-start(bf16[8,4,40,1024]{3,2,1,0:T(8,128)(2,1)} %get-tuple-element.69), calls=%async_computation.6 | async-start | bytes 5242880 | tf_op jit(solution)/shard_map/all_to_all | solution.py:635
  396.2 72.4 %collective-permute-start.12 = (bf16[8,4,40,1024]{3,2,1,0:T(8,128)(2,1)}, bf16[8,4,40,1024]{3,2,1,0:T(8,128)(2,1)}, u32[]{:S(2)}, u32[]{:S(2)}) collective-permute-start(bf16[8,4,40,1024]{3,2,1,0:T(8,128)(2,1)} %get-tuple-element.68), channel_id=1, source_target_pairs={{0,1},{1,0},{2,3},{3,2},{4,5},{5,4},{6,7},{7,6},{8,9},{9,8},{10,11... | collective-permute-start | bytes 7864328 | tf_op jit(solution)/shard_map/ppermute | solution.py:632
  428.8 46.4 %all-to-all-start.8 = ((bf16[8,4,40,1024]{3,2,1,0:T(8,128)(2,1)}), bf16[8,4,40,1024]{3,2,1,0:T(8,128)(2,1)}, u32[]{:S(2)}, u32[]{:S(2)}) async-start(bf16[8,4,40,1024]{3,2,1,0:T(8,128)(2,1)} %get-tuple-element.70), calls=%async_computation.8 | async-start | bytes 5242880 | tf_op jit(solution)/shard_map/all_to_all | solution.py:635
  439.1 49.2 %collective-permute-start.13 = (bf16[512,1024]{1,0:T(8,128)(2,1)}, bf16[512,1024]{1,0:T(8,128)(2,1)}, u32[]{:S(2)}, u32[]{:S(2)}) collective-permute-start(bf16[512,1024]{1,0:T(8,128)(2,1)} %to_tokens.4.refs_2_), channel_id=1, source_target_pairs={{0,2},{1,3},{2,0},{3,1},{4,6},{5,7},{6,4},{7,5},{8,10},{9,11},{10,... | collective-permute-start | bytes 3145736 | tf_op jit(solution)/shard_map/ppermute | solution.py:632
  475.2 49.4 %all-to-all-start.7 = ((bf16[8,4,40,1024]{3,2,1,0:T(8,128)(2,1)}), bf16[8,4,40,1024]{3,2,1,0:T(8,128)(2,1)S(1)}, u32[]{:S(2)}, u32[]{:S(2)}) async-start(bf16[8,4,40,1024]{3,2,1,0:T(8,128)(2,1)} %add.298.refs_2_), calls=%async_computation.7 | async-start | bytes 5242880 | tf_op jit(solution)/shard_map/all_to_all | solution.py:635
  479.0 280.5 %reduce-scatter.2.cloned.1.call-start = ((), (), s32[]{:S(2)}) async-start(), calls=%async_computation.15 | async-start | bytes 13107200 | tf_op jit(solution)/shard_map/reduce_scatter | solution.py:824
  492.7 31.9 %collective-permute-start.14 = (bf16[512,1024]{1,0:T(8,128)(2,1)}, bf16[512,1024]{1,0:T(8,128)(2,1)}, u32[]{:S(2)}, u32[]{:S(2)}) collective-permute-start(bf16[512,1024]{1,0:T(8,128)(2,1)} %to_tokens.5.refs_20_), channel_id=1, source_target_pairs={{0,3},{1,2},{2,1},{3,0},{4,7},{5,6},{6,5},{7,4},{8,11},{9,10},{10,... | collective-permute-start | bytes 3145736 | tf_op jit(solution)/shard_map/ppermute | solution.py:632
  587.3 21.5 %collective-permute-start.16 = (bf16[4,3,128,1024]{3,2,1,0:T(8,128)(2,1)}, bf16[4,3,128,1024]{3,2,1,0:T(8,128)(2,1)}, u32[]{:S(2)}, u32[]{:S(2)}) collective-permute-start(bf16[4,3,128,1024]{3,2,1,0:T(8,128)(2,1)} %dynamic-slice_bitcast_fusion), channel_id=1, source_target_pairs={{0,4},{4,0},{8,12},{12,8},{16,20},{20,16},{24,28},{28,24},{1,5},{5... | collective-permute-start | bytes 9437192 | tf_op jit(solution)/shard_map/ppermute | solution.py:836
  608.3 52.7 %collective-permute-start.15 = (bf16[4,1,128,1024]{3,2,0,1:T(8,128)(2,1)}, bf16[4,1,128,1024]{3,2,0,1:T(8,128)(2,1)}, u32[]{:S(2)}, u32[]{:S(2)}) collective-permute-start(bf16[4,1,128,1024]{3,2,0,1:T(8,128)(2,1)} %dynamic-slice_bitcast_fusion.1), channel_id=1, source_target_pairs={{0,4},{4,0},{8,12},{12,8},{16,20},{20,16},{24,28},{28,24},{1,5},{5... | collective-permute-start | bytes 3145736 | tf_op jit(solution)/shard_map/ppermute | solution.py:836
  614.9 49.0 %all-to-all-start.11 = ((bf16[4,3,128,1024]{3,2,1,0:T(8,128)(2,1)}), bf16[4,3,128,1024]{3,2,1,0:T(8,128)(2,1)}, u32[]{:S(2)}, u32[]{:S(2)}) async-start(bf16[4,3,128,1024]{3,2,1,0:T(8,128)(2,1)} %fusion), calls=%async_computation.12 | async-start | bytes 6291456 | tf_op jit(solution)/shard_map/all_to_all | solution.py:840
  663.9 53.4 %all-to-all-start.10 = ((bf16[4,1,128,1024]{3,2,1,0:T(8,128)(2,1)}), bf16[4,1,128,1024]{3,2,1,0:T(8,128)(2,1)}, u32[]{:S(2)}, u32[]{:S(2)}) async-start(bf16[4,1,128,1024]{3,2,1,0:T(8,128)(2,1)} %fusion.18), calls=%async_computation.11 | async-start | bytes 2097152 | tf_op jit(solution)/shard_map/all_to_all | solution.py:840
  668.2 141.2 %all-gather.8.cloned.1.call-start = ((), (), s32[]{:S(2)}) async-start(), calls=%async_computation.16 | async-start | bytes 2359296 | tf_op jit(solution)/shard_map/all_gather | solution.py:865
  668.3 24.2 %collective-permute-start.23 = (f32[35330]{0:T(1024)S(1)}, f32[35330]{0:T(1024)S(1)}, u32[]{:S(2)}, u32[]{:S(2)}) collective-permute-start(f32[35330]{0:T(1024)S(1)} %add.206), channel_id=1, source_target_pairs={{0,1},{1,0},{2,3},{3,2},{4,5},{5,4},{6,7},{7,6},{8,9},{9,8},{10,11... | collective-permute-start | bytes 423968 | tf_op jit(solution)/shard_map/ppermute | solution.py:686
  692.5 23.2 %collective-permute-start.24 = (f32[35330]{0:T(1024)S(1)}, f32[35330]{0:T(1024)}, u32[]{:S(2)}, u32[]{:S(2)}) collective-permute-start(f32[35330]{0:T(1024)S(1)} %add.207), channel_id=1, source_target_pairs={{0,2},{1,3},{2,0},{3,1},{4,6},{5,7},{6,4},{7,5},{8,10},{9,11},{10,... | collective-permute-start | bytes 423968 | tf_op jit(solution)/shard_map/ppermute | solution.py:686
  699.4 20.1 %collective-permute-start.19 = (bf16[128,1024]{1,0:T(8,128)(2,1)}, bf16[128,1024]{1,0:T(8,128)(2,1)}, u32[]{:S(2)}, u32[]{:S(2)}) collective-permute-start(bf16[128,1024]{1,0:T(8,128)(2,1)} %get-tuple-element.125), channel_id=1, source_target_pairs={{0,3},{1,2},{2,1},{3,0},{4,7},{5,6},{6,5},{7,4},{8,11},{9,10},{10,... | collective-permute-start | bytes 786440 | tf_op jit(solution)/shard_map/ppermute | solution.py:632
  701.4 56.1 %collective-permute-start.18 = (bf16[128,1024]{1,0:T(8,128)(2,1)}, bf16[128,1024]{1,0:T(8,128)(2,1)}, u32[]{:S(2)}, u32[]{:S(2)}) collective-permute-start(bf16[128,1024]{1,0:T(8,128)(2,1)} %get-tuple-element.126), channel_id=1, source_target_pairs={{0,2},{1,3},{2,0},{3,1},{4,6},{5,7},{6,4},{7,5},{8,10},{9,11},{10,... | collective-permute-start | bytes 786440 | tf_op jit(solution)/shard_map/ppermute | solution.py:632
  703.4 54.0 %collective-permute-start.17 = (bf16[128,1024]{1,0:T(8,128)(2,1)}, bf16[128,1024]{1,0:T(8,128)(2,1)}, u32[]{:S(2)}, u32[]{:S(2)}) collective-permute-start(bf16[128,1024]{1,0:T(8,128)(2,1)} %get-tuple-element.127), channel_id=1, source_target_pairs={{0,1},{1,0},{2,3},{3,2},{4,5},{5,4},{6,7},{7,6},{8,9},{9,8},{10,11... | collective-permute-start | bytes 786440 | tf_op jit(solution)/shard_map/ppermute | solution.py:632
  759.5 45.1 %all-to-all-start.9 = ((bf16[8,4,40,1024]{3,2,1,0:T(8,128)(2,1)}), bf16[8,4,40,1024]{3,2,1,0:T(8,128)(2,1)}, u32[]{:S(2)}, u32[]{:S(2)}) async-start(bf16[8,4,40,1024]{3,2,1,0:T(8,128)(2,1)} %reduce-scatter.2.cloned.1.call-done), calls=%async_computation.10 | async-start | bytes 5242880 | tf_op jit(solution)/shard_map/all_to_all | solution.py:635
  (58 other events, 386.6 us)
Sparse Core Ops, SparseCore 0:
  49.6 80.8 all-gather.3
  188.6 79.6 all-gather.5
  540.4 213.1 reduce-scatter.1
  759.6 43.0 all-gather.7

commit v4 on v3

--- a/solution.py
+++ b/solution.py
@@ -402,7 +402,7 @@
     _, rows, width = values.shape
     count = here[0] * here[1]
     held = [value for value in after if value is not None]
-    steps = 4
+    steps = 2
     part = here[0] // steps
 
     def kernel(place_ref, id_ref, x_ref, *refs):
@@ -426,7 +426,7 @@
             out_specs=pl.BlockSpec((part, 1, here[1], width), lambda c, j, at: (j, c, 0, 0)),
         ),
         out_shape=jax.ShapeDtypeStruct((here[0], chunks, here[1], width), BF),
-        compiler_params=pltpu.CompilerParams(vmem_limit_bytes=40 * MIB),
+        compiler_params=pltpu.CompilerParams(vmem_limit_bytes=58 * MIB),
         cost_estimate=pl.CostEstimate(
             flops=2 * chunks * count * rows * width, bytes_accessed=4 * chunks * count * width, transcendentals=0
         ),

time: 831 us -> 827 us (level)
    unnamed x104 -> x96, local copies, waits for them, and re-layouts: 17.2 us -> 12.2 us
where the time goes in v4:
time: 827 us; the launch traced here: 817 us
  Pallas kernels  318 us (38%)
  waiting for transfers between devices  283 us (34%)
  starting transfers between devices  92.6 us (11%)
  other arithmetic  55 us (7%)
  local copies, waits for them, and re-layouts  41.4 us (5%)
  between operations  16.5 us (2%)
  matrix products  9.38 us (1%)
    pallas_call x24, Pallas kernels, launch(): pl.pallas_call(drop(kernel, len(operands), len(held)), grid=grid, in_spec...  291 us
    all_to_all x10, waiting for transfers between devices, exchange(): lax.all_to_all(value, 'expert', split_axis=0, concat_axis=0, tiled=True)  135 us
    ppermute x12, waiting for transfers between devices, swap(): lax.ppermute(value, 'tensor', [(i, i ^ step) for i in range(n_tensor)])  91.3 us
    all_to_all x10, starting transfers between devices, exchange(): lax.all_to_all(value, 'expert', split_axis=0, concat_axis=0, tiled=True)  42.8 us
    ppermute x5, waiting for transfers between devices, everywhere(): lax.ppermute(total, axis, [(i, i ^ 1 << bit) for i in range(size)])  27.6 us
    ppermute x5, starting transfers between devices, everywhere(): lax.ppermute(total, axis, [(i, i ^ 1 << bit) for i in range(size)])  18.5 us
  transfers between devices with their start and end apart: 41, of which 23 were waited for; matrix products, arithmetic and copies ran while one was open for 12% of the time, Pallas kernels for 35%

profile of v4, /device:TPU:0, one launch (start us, length us, event | category | flops | bytes accessed | tf_op | source)
XLA Modules:
  0.0 816.5 jit_solution(6915580049820632071)
XLA Ops:
  33.0 13.2 %collective-permute-done.1 = bf16[128,1024]{1,0:T(8,128)(2,1)S(1)} collective-permute-done((bf16[128,1024]{1,0:T(8,128)(2,1)}, bf16[128,1024]{1,0:T(8,128)(2,1)S(1)}, u32[]{:S(2)}, u32[]{:S(2)}) %collective-permute-start.1) | collective-permute-done | bytes 262176 | tf_op jit(solution)/shard_map/ppermute | solution.py:632
  64.4 13.3 %attend.2 = (bf16[3,512,256]{2,1,0:T(8,128)(2,1)}, bf16[512,256]{1,0:T(8,128)(2,1)}, bf16[4,512,512]{2,1,0:T(8,128)(2,1)}, f32[512,1024]{1,0:T(8,128)}) custom-call(bf16[512,1024]{1,0:T(8,128)(2,1)} %fusion.5.refs_0_, bf16[4,2,1,128,1024]{4,3,2,1,0:T(8,128)(2,1)} %bitcast.159, s32[512,512]{1,0:T(8,128)} %refs_2_.5, f32[2,2,128]{2,1,0:T(2,128)} %bitcast.16.refs_3_, ...), custom_call_target="tpu_custom_call" | custom-call | flops 1610612736 | bytes 9439232 | tf_op jit(solution)/shard_map/attend/pallas_call | solution.py:47
  98.2 8.5 %assemble.1.refs_0_ = bf16[8,3,128,1024]{3,2,1,0:T(8,128)(2,1)} custom-call(s32[2,8]{1,0:T(2,128)} %pad_add_fusion.2.place_ref, bf16[8,3,128,512]{3,2,1,0:T(8,128)(2,1)} %pad_maximum_fusion.refs_0_, bf16[8,3,128,512]{3,2,1,0:T(8,128)(2,1)} %pad_maximum_fusion.1.refs_1_, bf16[1280,1024]{1,0:T(8,128)(2,1)} %to_slots.5.refs_2_), custom_call_target="tpu_custom_call" | custom-call | bytes 12582912 | tf_op jit(solution)/shard_map/assemble/pallas_call | solution.py:257
  106.6 15.2 %all-to-all-done.refs_1_ = bf16[8,4,40,1024]{3,2,1,0:T(8,128)(2,1)} async-done(((bf16[8,4,40,1024]{3,2,1,0:T(8,128)(2,1)}), bf16[8,4,40,1024]{3,2,1,0:T(8,128)(2,1)}, u32[]{:S(2)}, u32[]{:S(2)}) %all-to-all-start) | async-done | bytes 2621472 | tf_op jit(solution)/shard_map/all_to_all | solution.py:635
  121.9 8.7 %all-gather.4.cloned.1.call-done = bf16[2048,1024]{1,0:T(8,128)(2,1)} async-done(((bf16[512,1024]{1,0:T(8,128)(2,1)}), bf16[2048,1024]{1,0:T(8,128)(2,1)}) %all-gather.4.cloned.1.call-update) | async-done | bytes 4194320 | tf_op jit(solution)/shard_map/all_gather | solution.py:719
  130.6 9.9 %to_many_slots.1.refs_4_ = bf16[8,3,160,1024]{3,2,1,0:T(8,128)(2,1)} custom-call(s32[3]{0:T(128)} %add_xor_fusion.place_ref, s32[3,2,512]{2,1,0:T(2,128)} %pad_add_fusion.1.id_ref, bf16[4,512,1024]{2,1,0:T(8,128)(2,1)} %bitcast.161, bf16[8,3,128,1024]{3,2,1,0:T(8,128)(2,1)} %assemble.1.refs_0_, bf16[8,4,40,1024]{3,2,1,0:T(8,128)(2,1)} %all-to-all-done.refs_1_), custom_call_target="tpu_custom_call" | custom-call | flops 4026531840 | bytes 15728640 | tf_op jit(solution)/shard_map/to_many_slots/pallas_call | solution.py:416
  146.2 32.7 %attend.3 = (bf16[3,512,768]{2,1,0:T(8,128)(2,1)}, bf16[512,768]{1,0:T(8,128)(2,1)}, bf16[12,512,512]{2,1,0:T(8,128)(2,1)}, f32[512,1024]{1,0:T(8,128)}) custom-call(bf16[512,1024]{1,0:T(8,128)(2,1)} %fusion.5.refs_0_, bf16[4,2,3,128,1024]{4,3,2,1,0:T(8,128)(2,1)} %bitcast.149, s32[512,512]{1,0:T(8,128)} %refs_2_.5, f32[6,2,128]{2,1,0:T(2,128)} %bitcast.205, ...), custom_call_target="tpu_custom_call" | custom-call | flops 4831838208 | bytes 19929088 | tf_op jit(solution)/shard_map/attend/pallas_call | solution.py:47
  183.6 50.4 %all-to-all-done.1.refs_3_ = bf16[8,3,160,1024]{3,2,1,0:T(8,128)(2,1)} async-done(((bf16[8,3,160,1024]{3,2,1,0:T(8,128)(2,1)}), bf16[8,3,160,1024]{3,2,1,0:T(8,128)(2,1)}, u32[]{:S(2)}, u32[]{:S(2)}) %all-to-all-start.1) | async-done | bytes 7864352 | tf_op jit(solution)/shard_map/all_to_all | solution.py:635
  250.4 13.0 %all-gather.6.cloned.1.call-done = bf16[2048,1024]{1,0:T(8,128)(2,1)} async-done(((bf16[512,1024]{1,0:T(8,128)(2,1)}), bf16[2048,1024]{1,0:T(8,128)(2,1)}) %all-gather.6.cloned.1.call-update) | async-done | bytes 4194320 | tf_op jit(solution)/shard_map/all_gather | solution.py:679
  281.5 20.9 %experts.4 = (bf16[8,4,40,1024]{3,2,1,0:T(8,128)(2,1)}, bf16[8,4,40,1024]{3,2,1,0:T(8,128)(2,1)}, bf16[4,320,704]{2,1,0:T(8,128)(2,1)}, bf16[4,320,704]{2,1,0:T(...) custom-call(s32[1]{0:T(128)} %bitcast.9.refs_0_, bf16[8,1,4,40,1024]{4,3,2,1,0:T(8,128)(2,1)} %bitcast.163, ...), custom_call_target="tpu_custom_call" | custom-call | flops 22145925120 | bytes 34247684 | tf_op jit(solution)/shard_map/experts/pallas_call | solution.py:47
  306.9 6.0 all-to-all-done.3
  317.6 20.9 %experts.5 = (bf16[8,4,40,1024]{3,2,1,0:T(8,128)(2,1)}, bf16[8,4,40,1024]{3,2,1,0:T(8,128)(2,1)}, bf16[4,320,704]{2,1,0:T(8,128)(2,1)}, bf16[4,320,704]{2,1,0:T(...) custom-call(s32[1]{0:T(128)} %bitcast.9.refs_0_, bf16[8,1,4,40,1024]{4,3,2,1,0:T(8,128)(2,1)} %bitcast.52.refs_1_, ...), custom_call_target="tpu_custom_call" | custom-call | flops 22145925120 | bytes 39490564 | tf_op jit(solution)/shard_map/experts/pallas_call | solution.py:47
  343.0 5.7 all-to-all-done.4
  356.1 20.9 %experts.6 = (bf16[8,4,40,1024]{3,2,1,0:T(8,128)(2,1)}, bf16[8,4,40,1024]{3,2,1,0:T(8,128)(2,1)}, bf16[4,320,704]{2,1,0:T(8,128)(2,1)}, bf16[4,320,704]{2,1,0:T(...) custom-call(s32[1]{0:T(128)} %bitcast.9.refs_0_, bf16[8,1,4,40,1024]{4,3,2,1,0:T(8,128)(2,1)} %bitcast.165, ...), custom_call_target="tpu_custom_call" | custom-call | flops 22145925120 | bytes 39490564 | tf_op jit(solution)/shard_map/experts/pallas_call | solution.py:47
  377.0 10.3 %all-to-all-done.5 = bf16[8,4,40,1024]{3,2,1,0:T(8,128)(2,1)} async-done(((bf16[8,4,40,1024]{3,2,1,0:T(8,128)(2,1)}), bf16[8,4,40,1024]{3,2,1,0:T(8,128)(2,1)}, u32[]{:S(2)}, u32[]{:S(2)}) %all-to-all-start.5) | async-done | bytes 2621472 | tf_op jit(solution)/shard_map/all_to_all | solution.py:635
  392.0 20.9 %experts.7 = (bf16[8,4,40,1024]{3,2,1,0:T(8,128)(2,1)}, bf16[8,4,40,1024]{3,2,1,0:T(8,128)(2,1)}, bf16[4,320,704]{2,1,0:T(8,128)(2,1)}, bf16[4,320,704]{2,1,0:T(...) custom-call(s32[1]{0:T(128)} %bitcast.9.refs_0_, bf16[8,1,4,40,1024]{4,3,2,1,0:T(8,128)(2,1)} %bitcast.61.refs_1_.refs_3_, ...), custom_call_target="tpu_custom_call" | custom-call | flops 22145925120 | bytes 39490564 | tf_op jit(solution)/shard_map/experts/pallas_call | solution.py:47
  413.0 10.2 %all-to-all-done.6 = bf16[8,4,40,1024]{3,2,1,0:T(8,128)(2,1)S(1)} async-done(((bf16[8,4,40,1024]{3,2,1,0:T(8,128)(2,1)}), bf16[8,4,40,1024]{3,2,1,0:T(8,128)(2,1)S(1)}, u32[]{:S(2)}, u32[]{:S(2)}) %all-to-all-start.6) | async-done | bytes 2621472 | tf_op jit(solution)/shard_map/all_to_all | solution.py:635
  436.4 28.1 %collective-permute-done.12.refs_1_ = bf16[8,4,40,1024]{3,2,1,0:T(8,128)(2,1)} collective-permute-done((bf16[8,4,40,1024]{3,2,1,0:T(8,128)(2,1)}, bf16[8,4,40,1024]{3,2,1,0:T(8,128)(2,1)}, u32[]{:S(2)}, u32[]{:S(2)}) %collective-permute-start.12) | collective-permute-done | bytes 2621472 | tf_op jit(solution)/shard_map/ppermute | solution.py:632
  464.4 6.6 add.298.refs_2_
  475.0 9.0 %collective-permute-done.13.refs_3_.refs_2_ = bf16[512,1024]{1,0:T(8,128)(2,1)} collective-permute-done((bf16[512,1024]{1,0:T(8,128)(2,1)}, bf16[512,1024]{1,0:T(8,128)(2,1)}, u32[]{:S(2)}, u32[]{:S(2)}) %collective-permute-start.13) | collective-permute-done | bytes 1048608 | tf_op jit(solution)/shard_map/ppermute | solution.py:632
  489.1 31.3 %expert_weight_grads.1 = (f32[4,704,1024]{2,1,0:T(8,128)}, f32[4,704,1024]{2,1,0:T(8,128)}, f32[4,704,1024]{2,1,0:T(8,128)}) custom-call(bf16[8,1,4,40,1024]{4,3,2,1,0:T(8,128)(2,1)} %bitcast.164, bf16[8,1,4,40,1024]{4,3,2,1,0:T(8,128)(2,1)} %bitcast.52.refs_1_, bf16[8,1,4,40,1024]{4,3,2,1,0:T(8,128)(2,1)} %bitcast.166, ...), custom_call_target="tpu_custom_call" | custom-call | flops 29527900160 | bytes 92930048 | tf_op jit(solution)/shard_map/expert_weight_grads/pallas_call | solution.py:47
  521.9 5.1 to_tokens.6.refs_4_
  527.0 9.0 %stack.116.refs_6_ = bf16[32,4,40,1024]{3,2,1,0:T(8,128)(2,1)} custom-call(s32[4]{0:T(128)} %iota_xor_fusion.1.place_ref, bf16[8,4,40,1024]{3,2,1,0:T(8,128)(2,1)} %get-tuple-element.63.refs_2_.refs_0_, bf16[8,4,40,1024]{3,2,1,0:T(8,128)(2,1)} %get-tuple-element.64.refs_2_.refs_1_, bf16[8,4,40,1024]{3,2,1,0:T(8,128)(2,1)} %get-tuple-element.65.refs_8_.refs_2_, ...), custom_call_target="tpu_custom_call" | custom-call | tf_op jit(solution)/shard_map/stack/pallas_call | solution.py:332
  544.9 34.3 %attend_back.2 = (bf16[4,2,3,128,1024]{4,3,2,1,0:T(8,128)(2,1)}, bf16[12,512,512]{2,1,0:T(8,128)(2,1)}, f32[512,1024]{1,0:T(8,128)}) custom-call(bf16[512,1024]{1,0:T(8,128)(2,1)} %fusion.5.refs_0_, bf16[512,1024]{1,0:T(8,128)(2,1)} %fusion.38.refs_1_, bf16[4,2,3,128,1024]{4,3,2,1,0:T(8,128)(2,1)} %bitcast.150, ...), custom_call_target="tpu_custom_call" | custom-call | flops 9663676416 | bytes 32505856 | tf_op jit(solution)/shard_map/attend_back/pallas_call | solution.py:47
  587.7 14.2 %attend_back.3 = (bf16[4,2,1,128,1024]{4,3,2,1,0:T(8,128)(2,1)}, bf16[4,512,512]{2,1,0:T(8,128)(2,1)}, f32[512,1024]{1,0:T(8,128)}) custom-call(bf16[512,1024]{1,0:T(8,128)(2,1)} %fusion.5.refs_0_, bf16[512,1024]{1,0:T(8,128)(2,1)} %fusion.38.refs_1_, bf16[4,2,1,128,1024]{4,3,2,1,0:T(8,128)(2,1)} %bitcast.160, ...), custom_call_target="tpu_custom_call" | custom-call | flops 3221225472 | bytes 13631488 | tf_op jit(solution)/shard_map/attend_back/pallas_call | solution.py:47
  604.6 6.1 fusion
  615.7 23.6 %table_back.1 = f32[256,512]{1,0:T(8,128)} custom-call(bf16[4,512,512]{2,1,0:T(8,128)(2,1)} %get-tuple-element.90.refs_0_, bf16[12,512,512]{2,1,0:T(8,128)(2,1)} %get-tuple-element.91.refs_1_, s32[512,512]{1,0:T(8,128)} %refs_2_.5, bf16[4,2,1,128,1024]{4,3,2,1,0:T(8,128)(2,1)} %get-tuple-element.89.refs_3_), custom_call_target="tpu_custom_call" | custom-call | flops 17179869184 | bytes 9961472 | tf_op jit(solution)/shard_map/table_back/pallas_call | solution.py:47
  664.1 13.8 %collective-permute-start.23 = (f32[35330]{0:T(1024)S(1)}, f32[35330]{0:T(1024)S(1)}, u32[]{:S(2)}, u32[]{:S(2)}) collective-permute-start(f32[35330]{0:T(1024)S(1)} %add.206), channel_id=1, source_target_pairs={{0,1},{1,0},{2,3},{3,2},{4,5},{5,4},{6,7},{7,6},{8,9},{9,8},{10,11... | collective-permute-start | bytes 423968 | tf_op jit(solution)/shard_map/ppermute | solution.py:686
  677.9 10.5 %collective-permute-done.23 = f32[35330]{0:T(1024)S(1)} collective-permute-done((f32[35330]{0:T(1024)S(1)}, f32[35330]{0:T(1024)S(1)}, u32[]{:S(2)}, u32[]{:S(2)}) %collective-permute-start.23) | collective-permute-done | bytes 141352 | tf_op jit(solution)/shard_map/ppermute | solution.py:686
  700.3 11.4 %collective-permute-done.24 = f32[35330]{0:T(1024)} collective-permute-done((f32[35330]{0:T(1024)S(1)}, f32[35330]{0:T(1024)}, u32[]{:S(2)}, u32[]{:S(2)}) %collective-permute-start.24) | collective-permute-done | bytes 141352 | tf_op jit(solution)/shard_map/ppermute | solution.py:686
  715.4 37.9 %collective-permute-done.18.refs_2_ = bf16[128,1024]{1,0:T(8,128)(2,1)} collective-permute-done((bf16[128,1024]{1,0:T(8,128)(2,1)}, bf16[128,1024]{1,0:T(8,128)(2,1)}, u32[]{:S(2)}, u32[]{:S(2)}) %collective-permute-start.18) | collective-permute-done | bytes 262176 | tf_op jit(solution)/shard_map/ppermute | solution.py:632
  766.4 34.1 %all-to-all-done.9 = bf16[8,4,40,1024]{3,2,1,0:T(8,128)(2,1)} async-done(((bf16[8,4,40,1024]{3,2,1,0:T(8,128)(2,1)}), bf16[8,4,40,1024]{3,2,1,0:T(8,128)(2,1)}, u32[]{:S(2)}, u32[]{:S(2)}) %all-to-all-start.9) | async-done | bytes 2621472 | tf_op jit(solution)/shard_map/all_to_all | solution.py:635
  (288 shorter events, 244.5 us)
Async XLA Ops:
  7.2 123.4 %all-gather.4.cloned.1.call-start = ((), (), s32[]{:S(2)}) async-start(), calls=%async_computation.13 | async-start | bytes 5242880 | tf_op jit(solution)/shard_map/all_gather | solution.py:719
  8.5 17.9 %collective-permute-start.4 = (f32[4,128]{1,0:T(4,128)}, f32[4,128]{1,0:T(4,128)S(1)}, u32[]{:S(2)}, u32[]{:S(2)}) collective-permute-start(f32[4,128]{1,0:T(4,128)} %get-tuple-element.153), channel_id=1, source_target_pairs={{0,2},{1,3},{2,0},{3,1},{4,6},{5,7},{6,4},{7,5},{8,10},{9,11},{10,... | collective-permute-start | bytes 6152 | tf_op jit(solution)/shard_map/ppermute | solution.py:632
  12.6 16.7 %collective-permute-start.3 = (f32[4,128]{1,0:T(4,128)}, f32[4,128]{1,0:T(4,128)S(1)}, u32[]{:S(2)}, u32[]{:S(2)}) collective-permute-start(f32[4,128]{1,0:T(4,128)} %get-tuple-element.153), channel_id=1, source_target_pairs={{0,1},{1,0},{2,3},{3,2},{4,5},{5,4},{6,7},{7,6},{8,9},{9,8},{10,11... | collective-permute-start | bytes 6152 | tf_op jit(solution)/shard_map/ppermute | solution.py:632
  25.4 20.8 %collective-permute-start.1 = (bf16[128,1024]{1,0:T(8,128)(2,1)}, bf16[128,1024]{1,0:T(8,128)(2,1)S(1)}, u32[]{:S(2)}, u32[]{:S(2)}) collective-permute-start(bf16[128,1024]{1,0:T(8,128)(2,1)} %hold.2.refs_1_), channel_id=1, source_target_pairs={{0,2},{1,3},{2,0},{3,1},{4,6},{5,7},{6,4},{7,5},{8,10},{9,11},{10,... | collective-permute-start | bytes 786440 | tf_op jit(solution)/shard_map/ppermute | solution.py:632
  26.5 19.7 %collective-permute-start = (bf16[128,1024]{1,0:T(8,128)(2,1)S(1)}, bf16[128,1024]{1,0:T(8,128)(2,1)S(1)}, u32[]{:S(2)}, u32[]{:S(2)}) collective-permute-start(bf16[128,1024]{1,0:T(8,128)(2,1)S(1)} %copy-done.19), channel_id=1, source_target_pairs={{0,1},{1,0},{2,3},{3,2},{4,5},{5,4},{6,7},{7,6},{8,9},{9,8},{10,11... | collective-permute-start | bytes 786440 | tf_op jit(solution)/shard_map/ppermute | solution.py:632
  59.0 18.8 %collective-permute-start.7 = (bf16[2,3,128,512]{3,2,1,0:T(8,128)(2,1)S(1)}, bf16[2,3,128,512]{3,2,1,0:T(8,128)(2,1)S(1)}, u32[]{:S(2)}, u32[]{:S(2)}) collective-permute-start(bf16[2,3,128,512]{3,2,1,0:T(8,128)(2,1)S(1)} %pad_maximum_fusion.6), channel_id=1, source_target_pairs={{0,16},{4,20},{8,24},{12,28},{16,0},{20,4},{24,8},{28,12},{1,17},{... | collective-permute-start | bytes 2359304 | tf_op jit(solution)/shard_map/ppermute | solution.py:729
  63.0 16.1 %collective-permute-start.10 = (bf16[2,3,128,512]{3,2,1,0:T(8,128)(2,1)S(1)}, bf16[2,3,128,512]{3,2,1,0:T(8,128)(2,1)S(1)}, u32[]{:S(2)}, u32[]{:S(2)}) collective-permute-start(bf16[2,3,128,512]{3,2,1,0:T(8,128)(2,1)S(1)} %pad_maximum_fusion.7), channel_id=1, source_target_pairs={{0,8},{4,12},{8,0},{12,4},{16,24},{20,28},{24,16},{28,20},{1,9},{5... | collective-permute-start | bytes 2359304 | tf_op jit(solution)/shard_map/ppermute | solution.py:729
  85.0 36.9 %all-to-all-start = ((bf16[8,4,40,1024]{3,2,1,0:T(8,128)(2,1)}), bf16[8,4,40,1024]{3,2,1,0:T(8,128)(2,1)}, u32[]{:S(2)}, u32[]{:S(2)}) async-start(bf16[8,4,40,1024]{3,2,1,0:T(8,128)(2,1)} %bitcast.152), calls=%async_computation | async-start | bytes 5242880 | tf_op jit(solution)/shard_map/all_to_all | solution.py:635
  140.5 93.5 %all-to-all-start.1 = ((bf16[8,3,160,1024]{3,2,1,0:T(8,128)(2,1)}), bf16[8,3,160,1024]{3,2,1,0:T(8,128)(2,1)}, u32[]{:S(2)}, u32[]{:S(2)}) async-start(bf16[8,3,160,1024]{3,2,1,0:T(8,128)(2,1)} %to_many_slots.1.refs_4_), calls=%async_computation.1 | async-start | bytes 15728640 | tf_op jit(solution)/shard_map/all_to_all | solution.py:635
  145.6 117.8 %all-gather.6.cloned.1.call-start = ((), (), s32[]{:S(2)}) async-start(), calls=%async_computation.14 | async-start | bytes 5242880 | tf_op jit(solution)/shard_map/all_gather | solution.py:679
  238.5 36.0 %all-to-all-start.2 = ((bf16[8,4,40,1024]{3,2,1,0:T(8,128)(2,1)}), bf16[8,4,40,1024]{3,2,1,0:T(8,128)(2,1)S(1)}, u32[]{:S(2)}, u32[]{:S(2)}) async-start(bf16[8,4,40,1024]{3,2,1,0:T(8,128)(2,1)} %bitcast.151), calls=%async_computation.2 | async-start | bytes 5242880 | tf_op jit(solution)/shard_map/all_to_all | solution.py:635
  276.0 36.9 %all-to-all-start.3 = ((bf16[8,4,40,1024]{3,2,1,0:T(8,128)(2,1)}), bf16[8,4,40,1024]{3,2,1,0:T(8,128)(2,1)}, u32[]{:S(2)}, u32[]{:S(2)}) async-start(bf16[8,4,40,1024]{3,2,1,0:T(8,128)(2,1)} %bitcast.156), calls=%async_computation.3 | async-start | bytes 5242880 | tf_op jit(solution)/shard_map/all_to_all | solution.py:635
  312.9 35.8 %all-to-all-start.4 = ((bf16[8,4,40,1024]{3,2,1,0:T(8,128)(2,1)}), bf16[8,4,40,1024]{3,2,1,0:T(8,128)(2,1)S(1)}, u32[]{:S(2)}, u32[]{:S(2)}) async-start(bf16[8,4,40,1024]{3,2,1,0:T(8,128)(2,1)} %bitcast.157), calls=%async_computation.4 | async-start | bytes 5242880 | tf_op jit(solution)/shard_map/all_to_all | solution.py:635
  350.2 37.1 %all-to-all-start.5 = ((bf16[8,4,40,1024]{3,2,1,0:T(8,128)(2,1)}), bf16[8,4,40,1024]{3,2,1,0:T(8,128)(2,1)}, u32[]{:S(2)}, u32[]{:S(2)}) async-start(bf16[8,4,40,1024]{3,2,1,0:T(8,128)(2,1)} %bitcast.158), calls=%async_computation.5 | async-start | bytes 5242880 | tf_op jit(solution)/shard_map/all_to_all | solution.py:635
  387.3 35.8 %all-to-all-start.6 = ((bf16[8,4,40,1024]{3,2,1,0:T(8,128)(2,1)}), bf16[8,4,40,1024]{3,2,1,0:T(8,128)(2,1)S(1)}, u32[]{:S(2)}, u32[]{:S(2)}) async-start(bf16[8,4,40,1024]{3,2,1,0:T(8,128)(2,1)} %get-tuple-element.69), calls=%async_computation.6 | async-start | bytes 5242880 | tf_op jit(solution)/shard_map/all_to_all | solution.py:635
  392.0 72.4 %collective-permute-start.12 = (bf16[8,4,40,1024]{3,2,1,0:T(8,128)(2,1)}, bf16[8,4,40,1024]{3,2,1,0:T(8,128)(2,1)}, u32[]{:S(2)}, u32[]{:S(2)}) collective-permute-start(bf16[8,4,40,1024]{3,2,1,0:T(8,128)(2,1)} %get-tuple-element.68), channel_id=1, source_target_pairs={{0,1},{1,0},{2,3},{3,2},{4,5},{5,4},{6,7},{7,6},{8,9},{9,8},{10,11... | collective-permute-start | bytes 7864328 | tf_op jit(solution)/shard_map/ppermute | solution.py:632
  424.6 46.4 %all-to-all-start.8 = ((bf16[8,4,40,1024]{3,2,1,0:T(8,128)(2,1)}), bf16[8,4,40,1024]{3,2,1,0:T(8,128)(2,1)}, u32[]{:S(2)}, u32[]{:S(2)}) async-start(bf16[8,4,40,1024]{3,2,1,0:T(8,128)(2,1)} %get-tuple-element.70), calls=%async_computation.8 | async-start | bytes 5242880 | tf_op jit(solution)/shard_map/all_to_all | solution.py:635
  434.9 49.2 %collective-permute-start.13 = (bf16[512,1024]{1,0:T(8,128)(2,1)}, bf16[512,1024]{1,0:T(8,128)(2,1)}, u32[]{:S(2)}, u32[]{:S(2)}) collective-permute-start(bf16[512,1024]{1,0:T(8,128)(2,1)} %to_tokens.4.refs_2_), channel_id=1, source_target_pairs={{0,2},{1,3},{2,0},{3,1},{4,6},{5,7},{6,4},{7,5},{8,10},{9,11},{10,... | collective-permute-start | bytes 3145736 | tf_op jit(solution)/shard_map/ppermute | solution.py:632
  471.0 49.4 %all-to-all-start.7 = ((bf16[8,4,40,1024]{3,2,1,0:T(8,128)(2,1)}), bf16[8,4,40,1024]{3,2,1,0:T(8,128)(2,1)S(1)}, u32[]{:S(2)}, u32[]{:S(2)}) async-start(bf16[8,4,40,1024]{3,2,1,0:T(8,128)(2,1)} %add.298.refs_2_), calls=%async_computation.7 | async-start | bytes 5242880 | tf_op jit(solution)/shard_map/all_to_all | solution.py:635
  474.8 280.6 %reduce-scatter.2.cloned.1.call-start = ((), (), s32[]{:S(2)}) async-start(), calls=%async_computation.15 | async-start | bytes 13107200 | tf_op jit(solution)/shard_map/reduce_scatter | solution.py:824
  488.5 31.9 %collective-permute-start.14 = (bf16[512,1024]{1,0:T(8,128)(2,1)}, bf16[512,1024]{1,0:T(8,128)(2,1)}, u32[]{:S(2)}, u32[]{:S(2)}) collective-permute-start(bf16[512,1024]{1,0:T(8,128)(2,1)} %to_tokens.5.refs_20_), channel_id=1, source_target_pairs={{0,3},{1,2},{2,1},{3,0},{4,7},{5,6},{6,5},{7,4},{8,11},{9,10},{10,... | collective-permute-start | bytes 3145736 | tf_op jit(solution)/shard_map/ppermute | solution.py:632
  583.1 21.5 %collective-permute-start.16 = (bf16[4,3,128,1024]{3,2,1,0:T(8,128)(2,1)}, bf16[4,3,128,1024]{3,2,1,0:T(8,128)(2,1)}, u32[]{:S(2)}, u32[]{:S(2)}) collective-permute-start(bf16[4,3,128,1024]{3,2,1,0:T(8,128)(2,1)} %dynamic-slice_bitcast_fusion), channel_id=1, source_target_pairs={{0,4},{4,0},{8,12},{12,8},{16,20},{20,16},{24,28},{28,24},{1,5},{5... | collective-permute-start | bytes 9437192 | tf_op jit(solution)/shard_map/ppermute | solution.py:836
  604.1 52.7 %collective-permute-start.15 = (bf16[4,1,128,1024]{3,2,0,1:T(8,128)(2,1)}, bf16[4,1,128,1024]{3,2,0,1:T(8,128)(2,1)}, u32[]{:S(2)}, u32[]{:S(2)}) collective-permute-start(bf16[4,1,128,1024]{3,2,0,1:T(8,128)(2,1)} %dynamic-slice_bitcast_fusion.1), channel_id=1, source_target_pairs={{0,4},{4,0},{8,12},{12,8},{16,20},{20,16},{24,28},{28,24},{1,5},{5... | collective-permute-start | bytes 3145736 | tf_op jit(solution)/shard_map/ppermute | solution.py:836
  610.7 49.0 %all-to-all-start.11 = ((bf16[4,3,128,1024]{3,2,1,0:T(8,128)(2,1)}), bf16[4,3,128,1024]{3,2,1,0:T(8,128)(2,1)}, u32[]{:S(2)}, u32[]{:S(2)}) async-start(bf16[4,3,128,1024]{3,2,1,0:T(8,128)(2,1)} %fusion), calls=%async_computation.12 | async-start | bytes 6291456 | tf_op jit(solution)/shard_map/all_to_all | solution.py:840
  659.7 53.5 %all-to-all-start.10 = ((bf16[4,1,128,1024]{3,2,1,0:T(8,128)(2,1)}), bf16[4,1,128,1024]{3,2,1,0:T(8,128)(2,1)}, u32[]{:S(2)}, u32[]{:S(2)}) async-start(bf16[4,1,128,1024]{3,2,1,0:T(8,128)(2,1)} %fusion.18), calls=%async_computation.11 | async-start | bytes 2097152 | tf_op jit(solution)/shard_map/all_to_all | solution.py:840
  664.0 141.3 %all-gather.8.cloned.1.call-start = ((), (), s32[]{:S(2)}) async-start(), calls=%async_computation.16 | async-start | bytes 2359296 | tf_op jit(solution)/shard_map/all_gather | solution.py:865
  664.1 24.3 %collective-permute-start.23 = (f32[35330]{0:T(1024)S(1)}, f32[35330]{0:T(1024)S(1)}, u32[]{:S(2)}, u32[]{:S(2)}) collective-permute-start(f32[35330]{0:T(1024)S(1)} %add.206), channel_id=1, source_target_pairs={{0,1},{1,0},{2,3},{3,2},{4,5},{5,4},{6,7},{7,6},{8,9},{9,8},{10,11... | collective-permute-start | bytes 423968 | tf_op jit(solution)/shard_map/ppermute | solution.py:686
  688.4 23.3 %collective-permute-start.24 = (f32[35330]{0:T(1024)S(1)}, f32[35330]{0:T(1024)}, u32[]{:S(2)}, u32[]{:S(2)}) collective-permute-start(f32[35330]{0:T(1024)S(1)} %add.207), channel_id=1, source_target_pairs={{0,2},{1,3},{2,0},{3,1},{4,6},{5,7},{6,4},{7,5},{8,10},{9,11},{10,... | collective-permute-start | bytes 423968 | tf_op jit(solution)/shard_map/ppermute | solution.py:686
  695.2 20.2 %collective-permute-start.19 = (bf16[128,1024]{1,0:T(8,128)(2,1)}, bf16[128,1024]{1,0:T(8,128)(2,1)}, u32[]{:S(2)}, u32[]{:S(2)}) collective-permute-start(bf16[128,1024]{1,0:T(8,128)(2,1)} %get-tuple-element.125), channel_id=1, source_target_pairs={{0,3},{1,2},{2,1},{3,0},{4,7},{5,6},{6,5},{7,4},{8,11},{9,10},{10,... | collective-permute-start | bytes 786440 | tf_op jit(solution)/shard_map/ppermute | solution.py:632
  697.2 56.1 %collective-permute-start.18 = (bf16[128,1024]{1,0:T(8,128)(2,1)}, bf16[128,1024]{1,0:T(8,128)(2,1)}, u32[]{:S(2)}, u32[]{:S(2)}) collective-permute-start(bf16[128,1024]{1,0:T(8,128)(2,1)} %get-tuple-element.126), channel_id=1, source_target_pairs={{0,2},{1,3},{2,0},{3,1},{4,6},{5,7},{6,4},{7,5},{8,10},{9,11},{10,... | collective-permute-start | bytes 786440 | tf_op jit(solution)/shard_map/ppermute | solution.py:632
  699.2 54.1 %collective-permute-start.17 = (bf16[128,1024]{1,0:T(8,128)(2,1)}, bf16[128,1024]{1,0:T(8,128)(2,1)}, u32[]{:S(2)}, u32[]{:S(2)}) collective-permute-start(bf16[128,1024]{1,0:T(8,128)(2,1)} %get-tuple-element.127), channel_id=1, source_target_pairs={{0,1},{1,0},{2,3},{3,2},{4,5},{5,4},{6,7},{7,6},{8,9},{9,8},{10,11... | collective-permute-start | bytes 786440 | tf_op jit(solution)/shard_map/ppermute | solution.py:632
  755.4 45.1 %all-to-all-start.9 = ((bf16[8,4,40,1024]{3,2,1,0:T(8,128)(2,1)}), bf16[8,4,40,1024]{3,2,1,0:T(8,128)(2,1)}, u32[]{:S(2)}, u32[]{:S(2)}) async-start(bf16[8,4,40,1024]{3,2,1,0:T(8,128)(2,1)} %reduce-scatter.2.cloned.1.call-done), calls=%async_computation.10 | async-start | bytes 5242880 | tf_op jit(solution)/shard_map/all_to_all | solution.py:635
  (54 other events, 415.3 us)
Sparse Core Ops, SparseCore 0:
  49.6 80.8 all-gather.3
  183.7 79.6 all-gather.5
  536.2 213.1 reduce-scatter.1
  755.5 42.9 all-gather.7

commit v5 on v4

--- a/solution.py
+++ b/solution.py
@@ -380,7 +380,7 @@
 
 def to_slots(ids, value, slots, after):
     rows, width = value.shape
-    steps = 4
+    steps = 2
     return launch(
         dispatch_kernel,
         (ids, value),

time: 827 us -> 827 us (level)
  no operation moved by 1% of the time
where the time goes in v5:
time: 827 us; the launch traced here: 816 us
  Pallas kernels  316 us (38%)
  waiting for transfers between devices  285 us (34%)
  starting transfers between devices  92.6 us (11%)
  other arithmetic  55 us (7%)
  local copies, waits for them, and re-layouts  41.4 us (5%)
  between operations  16.5 us (2%)
  matrix products  9.38 us (1%)
    pallas_call x24, Pallas kernels, launch(): pl.pallas_call(drop(kernel, len(operands), len(held)), grid=grid, in_spec...  289 us
    all_to_all x10, waiting for transfers between devices, exchange(): lax.all_to_all(value, 'expert', split_axis=0, concat_axis=0, tiled=True)  136 us
    ppermute x12, waiting for transfers between devices, swap(): lax.ppermute(value, 'tensor', [(i, i ^ step) for i in range(n_tensor)])  91.3 us
    all_to_all x10, starting transfers between devices, exchange(): lax.all_to_all(value, 'expert', split_axis=0, concat_axis=0, tiled=True)  42.8 us
    ppermute x5, waiting for transfers between devices, everywhere(): lax.ppermute(total, axis, [(i, i ^ 1 << bit) for i in range(size)])  27.5 us
    ppermute x5, starting transfers between devices, everywhere(): lax.ppermute(total, axis, [(i, i ^ 1 << bit) for i in range(size)])  18.5 us
  transfers between devices with their start and end apart: 41, of which 23 were waited for; matrix products, arithmetic and copies ran while one was open for 12% of the time, Pallas kernels for 35%

profile of v5, /device:TPU:0, one launch (start us, length us, event | category | flops | bytes accessed | tf_op | source)
XLA Modules:
  0.0 816.1 jit_solution(15318335317745506940)
XLA Ops:
  33.0 13.2 %collective-permute-done.1 = bf16[128,1024]{1,0:T(8,128)(2,1)S(1)} collective-permute-done((bf16[128,1024]{1,0:T(8,128)(2,1)}, bf16[128,1024]{1,0:T(8,128)(2,1)S(1)}, u32[]{:S(2)}, u32[]{:S(2)}) %collective-permute-start.1) | collective-permute-done | bytes 262176 | tf_op jit(solution)/shard_map/ppermute | solution.py:632
  64.4 13.3 %attend.2 = (bf16[3,512,256]{2,1,0:T(8,128)(2,1)}, bf16[512,256]{1,0:T(8,128)(2,1)}, bf16[4,512,512]{2,1,0:T(8,128)(2,1)}, f32[512,1024]{1,0:T(8,128)}) custom-call(bf16[512,1024]{1,0:T(8,128)(2,1)} %fusion.5.refs_0_, bf16[4,2,1,128,1024]{4,3,2,1,0:T(8,128)(2,1)} %bitcast.159, s32[512,512]{1,0:T(8,128)} %refs_2_.5, f32[2,2,128]{2,1,0:T(2,128)} %bitcast.16.refs_3_, ...), custom_call_target="tpu_custom_call" | custom-call | flops 1610612736 | bytes 9439232 | tf_op jit(solution)/shard_map/attend/pallas_call | solution.py:47
  97.7 8.5 %assemble.1.refs_0_ = bf16[8,3,128,1024]{3,2,1,0:T(8,128)(2,1)} custom-call(s32[2,8]{1,0:T(2,128)} %pad_add_fusion.2.place_ref, bf16[8,3,128,512]{3,2,1,0:T(8,128)(2,1)} %pad_maximum_fusion.refs_0_, bf16[8,3,128,512]{3,2,1,0:T(8,128)(2,1)} %pad_maximum_fusion.1.refs_1_, bf16[1280,1024]{1,0:T(8,128)(2,1)} %to_slots.5.refs_2_), custom_call_target="tpu_custom_call" | custom-call | bytes 12582912 | tf_op jit(solution)/shard_map/assemble/pallas_call | solution.py:257
  106.2 15.2 %all-to-all-done.refs_1_ = bf16[8,4,40,1024]{3,2,1,0:T(8,128)(2,1)} async-done(((bf16[8,4,40,1024]{3,2,1,0:T(8,128)(2,1)}), bf16[8,4,40,1024]{3,2,1,0:T(8,128)(2,1)}, u32[]{:S(2)}, u32[]{:S(2)}) %all-to-all-start) | async-done | bytes 2621472 | tf_op jit(solution)/shard_map/all_to_all | solution.py:635
  121.4 9.2 %all-gather.4.cloned.1.call-done = bf16[2048,1024]{1,0:T(8,128)(2,1)} async-done(((bf16[512,1024]{1,0:T(8,128)(2,1)}), bf16[2048,1024]{1,0:T(8,128)(2,1)}) %all-gather.4.cloned.1.call-update) | async-done | bytes 4194320 | tf_op jit(solution)/shard_map/all_gather | solution.py:719
  130.6 9.9 %to_many_slots.1.refs_4_ = bf16[8,3,160,1024]{3,2,1,0:T(8,128)(2,1)} custom-call(s32[3]{0:T(128)} %add_xor_fusion.place_ref, s32[3,2,512]{2,1,0:T(2,128)} %pad_add_fusion.1.id_ref, bf16[4,512,1024]{2,1,0:T(8,128)(2,1)} %bitcast.161, bf16[8,3,128,1024]{3,2,1,0:T(8,128)(2,1)} %assemble.1.refs_0_, bf16[8,4,40,1024]{3,2,1,0:T(8,128)(2,1)} %all-to-all-done.refs_1_), custom_call_target="tpu_custom_call" | custom-call | flops 4026531840 | bytes 15728640 | tf_op jit(solution)/shard_map/to_many_slots/pallas_call | solution.py:416
  146.2 32.7 %attend.3 = (bf16[3,512,768]{2,1,0:T(8,128)(2,1)}, bf16[512,768]{1,0:T(8,128)(2,1)}, bf16[12,512,512]{2,1,0:T(8,128)(2,1)}, f32[512,1024]{1,0:T(8,128)}) custom-call(bf16[512,1024]{1,0:T(8,128)(2,1)} %fusion.5.refs_0_, bf16[4,2,3,128,1024]{4,3,2,1,0:T(8,128)(2,1)} %bitcast.149, s32[512,512]{1,0:T(8,128)} %refs_2_.5, f32[6,2,128]{2,1,0:T(2,128)} %bitcast.205, ...), custom_call_target="tpu_custom_call" | custom-call | flops 4831838208 | bytes 19929088 | tf_op jit(solution)/shard_map/attend/pallas_call | solution.py:47
  183.6 50.4 %all-to-all-done.1.refs_3_ = bf16[8,3,160,1024]{3,2,1,0:T(8,128)(2,1)} async-done(((bf16[8,3,160,1024]{3,2,1,0:T(8,128)(2,1)}), bf16[8,3,160,1024]{3,2,1,0:T(8,128)(2,1)}, u32[]{:S(2)}, u32[]{:S(2)}) %all-to-all-start.1) | async-done | bytes 7864352 | tf_op jit(solution)/shard_map/all_to_all | solution.py:635
  249.9 13.5 %all-gather.6.cloned.1.call-done = bf16[2048,1024]{1,0:T(8,128)(2,1)} async-done(((bf16[512,1024]{1,0:T(8,128)(2,1)}), bf16[2048,1024]{1,0:T(8,128)(2,1)}) %all-gather.6.cloned.1.call-update) | async-done | bytes 4194320 | tf_op jit(solution)/shard_map/all_gather | solution.py:679
  281.0 20.9 %experts.4 = (bf16[8,4,40,1024]{3,2,1,0:T(8,128)(2,1)}, bf16[8,4,40,1024]{3,2,1,0:T(8,128)(2,1)}, bf16[4,320,704]{2,1,0:T(8,128)(2,1)}, bf16[4,320,704]{2,1,0:T(...) custom-call(s32[1]{0:T(128)} %bitcast.9.refs_0_, bf16[8,1,4,40,1024]{4,3,2,1,0:T(8,128)(2,1)} %bitcast.163, ...), custom_call_target="tpu_custom_call" | custom-call | flops 22145925120 | bytes 34247684 | tf_op jit(solution)/shard_map/experts/pallas_call | solution.py:47
  306.0 6.4 all-to-all-done.3
  317.1 20.9 %experts.5 = (bf16[8,4,40,1024]{3,2,1,0:T(8,128)(2,1)}, bf16[8,4,40,1024]{3,2,1,0:T(8,128)(2,1)}, bf16[4,320,704]{2,1,0:T(8,128)(2,1)}, bf16[4,320,704]{2,1,0:T(...) custom-call(s32[1]{0:T(128)} %bitcast.9.refs_0_, bf16[8,1,4,40,1024]{4,3,2,1,0:T(8,128)(2,1)} %bitcast.52.refs_1_, ...), custom_call_target="tpu_custom_call" | custom-call | flops 22145925120 | bytes 39490564 | tf_op jit(solution)/shard_map/experts/pallas_call | solution.py:47
  342.1 6.2 all-to-all-done.4
  355.6 20.9 %experts.6 = (bf16[8,4,40,1024]{3,2,1,0:T(8,128)(2,1)}, bf16[8,4,40,1024]{3,2,1,0:T(8,128)(2,1)}, bf16[4,320,704]{2,1,0:T(8,128)(2,1)}, bf16[4,320,704]{2,1,0:T(...) custom-call(s32[1]{0:T(128)} %bitcast.9.refs_0_, bf16[8,1,4,40,1024]{4,3,2,1,0:T(8,128)(2,1)} %bitcast.165, ...), custom_call_target="tpu_custom_call" | custom-call | flops 22145925120 | bytes 39490564 | tf_op jit(solution)/shard_map/experts/pallas_call | solution.py:47
  376.5 10.3 %all-to-all-done.5 = bf16[8,4,40,1024]{3,2,1,0:T(8,128)(2,1)} async-done(((bf16[8,4,40,1024]{3,2,1,0:T(8,128)(2,1)}), bf16[8,4,40,1024]{3,2,1,0:T(8,128)(2,1)}, u32[]{:S(2)}, u32[]{:S(2)}) %all-to-all-start.5) | async-done | bytes 2621472 | tf_op jit(solution)/shard_map/all_to_all | solution.py:635
  391.6 20.9 %experts.7 = (bf16[8,4,40,1024]{3,2,1,0:T(8,128)(2,1)}, bf16[8,4,40,1024]{3,2,1,0:T(8,128)(2,1)}, bf16[4,320,704]{2,1,0:T(8,128)(2,1)}, bf16[4,320,704]{2,1,0:T(...) custom-call(s32[1]{0:T(128)} %bitcast.9.refs_0_, bf16[8,1,4,40,1024]{4,3,2,1,0:T(8,128)(2,1)} %bitcast.61.refs_1_.refs_3_, ...), custom_call_target="tpu_custom_call" | custom-call | flops 22145925120 | bytes 39490564 | tf_op jit(solution)/shard_map/experts/pallas_call | solution.py:47
  412.5 10.2 %all-to-all-done.6 = bf16[8,4,40,1024]{3,2,1,0:T(8,128)(2,1)S(1)} async-done(((bf16[8,4,40,1024]{3,2,1,0:T(8,128)(2,1)}), bf16[8,4,40,1024]{3,2,1,0:T(8,128)(2,1)S(1)}, u32[]{:S(2)}, u32[]{:S(2)}) %all-to-all-start.6) | async-done | bytes 2621472 | tf_op jit(solution)/shard_map/all_to_all | solution.py:635
  435.9 28.1 %collective-permute-done.12.refs_1_ = bf16[8,4,40,1024]{3,2,1,0:T(8,128)(2,1)} collective-permute-done((bf16[8,4,40,1024]{3,2,1,0:T(8,128)(2,1)}, bf16[8,4,40,1024]{3,2,1,0:T(8,128)(2,1)}, u32[]{:S(2)}, u32[]{:S(2)}) %collective-permute-start.12) | collective-permute-done | bytes 2621472 | tf_op jit(solution)/shard_map/ppermute | solution.py:632
  464.0 6.6 add.298.refs_2_
  474.6 9.0 %collective-permute-done.13.refs_3_.refs_2_ = bf16[512,1024]{1,0:T(8,128)(2,1)} collective-permute-done((bf16[512,1024]{1,0:T(8,128)(2,1)}, bf16[512,1024]{1,0:T(8,128)(2,1)}, u32[]{:S(2)}, u32[]{:S(2)}) %collective-permute-start.13) | collective-permute-done | bytes 1048608 | tf_op jit(solution)/shard_map/ppermute | solution.py:632
  488.6 31.3 %expert_weight_grads.1 = (f32[4,704,1024]{2,1,0:T(8,128)}, f32[4,704,1024]{2,1,0:T(8,128)}, f32[4,704,1024]{2,1,0:T(8,128)}) custom-call(bf16[8,1,4,40,1024]{4,3,2,1,0:T(8,128)(2,1)} %bitcast.164, bf16[8,1,4,40,1024]{4,3,2,1,0:T(8,128)(2,1)} %bitcast.52.refs_1_, bf16[8,1,4,40,1024]{4,3,2,1,0:T(8,128)(2,1)} %bitcast.166, ...), custom_call_target="tpu_custom_call" | custom-call | flops 29527900160 | bytes 92930048 | tf_op jit(solution)/shard_map/expert_weight_grads/pallas_call | solution.py:47
  521.4 5.1 to_tokens.6.refs_4_
  526.5 9.0 %stack.116.refs_6_ = bf16[32,4,40,1024]{3,2,1,0:T(8,128)(2,1)} custom-call(s32[4]{0:T(128)} %iota_xor_fusion.1.place_ref, bf16[8,4,40,1024]{3,2,1,0:T(8,128)(2,1)} %get-tuple-element.63.refs_2_.refs_0_, bf16[8,4,40,1024]{3,2,1,0:T(8,128)(2,1)} %get-tuple-element.64.refs_2_.refs_1_, bf16[8,4,40,1024]{3,2,1,0:T(8,128)(2,1)} %get-tuple-element.65.refs_8_.refs_2_, ...), custom_call_target="tpu_custom_call" | custom-call | tf_op jit(solution)/shard_map/stack/pallas_call | solution.py:332
  544.5 34.3 %attend_back.2 = (bf16[4,2,3,128,1024]{4,3,2,1,0:T(8,128)(2,1)}, bf16[12,512,512]{2,1,0:T(8,128)(2,1)}, f32[512,1024]{1,0:T(8,128)}) custom-call(bf16[512,1024]{1,0:T(8,128)(2,1)} %fusion.5.refs_0_, bf16[512,1024]{1,0:T(8,128)(2,1)} %fusion.38.refs_1_, bf16[4,2,3,128,1024]{4,3,2,1,0:T(8,128)(2,1)} %bitcast.150, ...), custom_call_target="tpu_custom_call" | custom-call | flops 9663676416 | bytes 32505856 | tf_op jit(solution)/shard_map/attend_back/pallas_call | solution.py:47
  587.2 14.2 %attend_back.3 = (bf16[4,2,1,128,1024]{4,3,2,1,0:T(8,128)(2,1)}, bf16[4,512,512]{2,1,0:T(8,128)(2,1)}, f32[512,1024]{1,0:T(8,128)}) custom-call(bf16[512,1024]{1,0:T(8,128)(2,1)} %fusion.5.refs_0_, bf16[512,1024]{1,0:T(8,128)(2,1)} %fusion.38.refs_1_, bf16[4,2,1,128,1024]{4,3,2,1,0:T(8,128)(2,1)} %bitcast.160, ...), custom_call_target="tpu_custom_call" | custom-call | flops 3221225472 | bytes 13631488 | tf_op jit(solution)/shard_map/attend_back/pallas_call | solution.py:47
  604.2 6.1 fusion
  615.2 23.6 %table_back.1 = f32[256,512]{1,0:T(8,128)} custom-call(bf16[4,512,512]{2,1,0:T(8,128)(2,1)} %get-tuple-element.90.refs_0_, bf16[12,512,512]{2,1,0:T(8,128)(2,1)} %get-tuple-element.91.refs_1_, s32[512,512]{1,0:T(8,128)} %refs_2_.5, bf16[4,2,1,128,1024]{4,3,2,1,0:T(8,128)(2,1)} %get-tuple-element.89.refs_3_), custom_call_target="tpu_custom_call" | custom-call | flops 17179869184 | bytes 9961472 | tf_op jit(solution)/shard_map/table_back/pallas_call | solution.py:47
  663.6 13.8 %collective-permute-start.23 = (f32[35330]{0:T(1024)S(1)}, f32[35330]{0:T(1024)S(1)}, u32[]{:S(2)}, u32[]{:S(2)}) collective-permute-start(f32[35330]{0:T(1024)S(1)} %add.206), channel_id=1, source_target_pairs={{0,1},{1,0},{2,3},{3,2},{4,5},{5,4},{6,7},{7,6},{8,9},{9,8},{10,11... | collective-permute-start | bytes 423968 | tf_op jit(solution)/shard_map/ppermute | solution.py:686
  677.4 10.5 %collective-permute-done.23 = f32[35330]{0:T(1024)S(1)} collective-permute-done((f32[35330]{0:T(1024)S(1)}, f32[35330]{0:T(1024)S(1)}, u32[]{:S(2)}, u32[]{:S(2)}) %collective-permute-start.23) | collective-permute-done | bytes 141352 | tf_op jit(solution)/shard_map/ppermute | solution.py:686
  699.9 11.3 %collective-permute-done.24 = f32[35330]{0:T(1024)} collective-permute-done((f32[35330]{0:T(1024)S(1)}, f32[35330]{0:T(1024)}, u32[]{:S(2)}, u32[]{:S(2)}) %collective-permute-start.24) | collective-permute-done | bytes 141352 | tf_op jit(solution)/shard_map/ppermute | solution.py:686
  714.9 37.9 %collective-permute-done.18.refs_2_ = bf16[128,1024]{1,0:T(8,128)(2,1)} collective-permute-done((bf16[128,1024]{1,0:T(8,128)(2,1)}, bf16[128,1024]{1,0:T(8,128)(2,1)}, u32[]{:S(2)}, u32[]{:S(2)}) %collective-permute-start.18) | collective-permute-done | bytes 262176 | tf_op jit(solution)/shard_map/ppermute | solution.py:632
  765.9 34.1 %all-to-all-done.9 = bf16[8,4,40,1024]{3,2,1,0:T(8,128)(2,1)} async-done(((bf16[8,4,40,1024]{3,2,1,0:T(8,128)(2,1)}), bf16[8,4,40,1024]{3,2,1,0:T(8,128)(2,1)}, u32[]{:S(2)}, u32[]{:S(2)}) %all-to-all-start.9) | async-done | bytes 2621472 | tf_op jit(solution)/shard_map/all_to_all | solution.py:635
  (288 shorter events, 242.2 us)
Async XLA Ops:
  7.2 123.4 %all-gather.4.cloned.1.call-start = ((), (), s32[]{:S(2)}) async-start(), calls=%async_computation.13 | async-start | bytes 5242880 | tf_op jit(solution)/shard_map/all_gather | solution.py:719
  8.5 17.9 %collective-permute-start.4 = (f32[4,128]{1,0:T(4,128)}, f32[4,128]{1,0:T(4,128)S(1)}, u32[]{:S(2)}, u32[]{:S(2)}) collective-permute-start(f32[4,128]{1,0:T(4,128)} %get-tuple-element.153), channel_id=1, source_target_pairs={{0,2},{1,3},{2,0},{3,1},{4,6},{5,7},{6,4},{7,5},{8,10},{9,11},{10,... | collective-permute-start | bytes 6152 | tf_op jit(solution)/shard_map/ppermute | solution.py:632
  12.6 16.7 %collective-permute-start.3 = (f32[4,128]{1,0:T(4,128)}, f32[4,128]{1,0:T(4,128)S(1)}, u32[]{:S(2)}, u32[]{:S(2)}) collective-permute-start(f32[4,128]{1,0:T(4,128)} %get-tuple-element.153), channel_id=1, source_target_pairs={{0,1},{1,0},{2,3},{3,2},{4,5},{5,4},{6,7},{7,6},{8,9},{9,8},{10,11... | collective-permute-start | bytes 6152 | tf_op jit(solution)/shard_map/ppermute | solution.py:632
  25.4 20.8 %collective-permute-start.1 = (bf16[128,1024]{1,0:T(8,128)(2,1)}, bf16[128,1024]{1,0:T(8,128)(2,1)S(1)}, u32[]{:S(2)}, u32[]{:S(2)}) collective-permute-start(bf16[128,1024]{1,0:T(8,128)(2,1)} %hold.2.refs_1_), channel_id=1, source_target_pairs={{0,2},{1,3},{2,0},{3,1},{4,6},{5,7},{6,4},{7,5},{8,10},{9,11},{10,... | collective-permute-start | bytes 786440 | tf_op jit(solution)/shard_map/ppermute | solution.py:632
  26.5 19.7 %collective-permute-start = (bf16[128,1024]{1,0:T(8,128)(2,1)S(1)}, bf16[128,1024]{1,0:T(8,128)(2,1)S(1)}, u32[]{:S(2)}, u32[]{:S(2)}) collective-permute-start(bf16[128,1024]{1,0:T(8,128)(2,1)S(1)} %copy-done.19), channel_id=1, source_target_pairs={{0,1},{1,0},{2,3},{3,2},{4,5},{5,4},{6,7},{7,6},{8,9},{9,8},{10,11... | collective-permute-start | bytes 786440 | tf_op jit(solution)/shard_map/ppermute | solution.py:632
  59.0 18.8 %collective-permute-start.7 = (bf16[2,3,128,512]{3,2,1,0:T(8,128)(2,1)S(1)}, bf16[2,3,128,512]{3,2,1,0:T(8,128)(2,1)S(1)}, u32[]{:S(2)}, u32[]{:S(2)}) collective-permute-start(bf16[2,3,128,512]{3,2,1,0:T(8,128)(2,1)S(1)} %pad_maximum_fusion.6), channel_id=1, source_target_pairs={{0,16},{4,20},{8,24},{12,28},{16,0},{20,4},{24,8},{28,12},{1,17},{... | collective-permute-start | bytes 2359304 | tf_op jit(solution)/shard_map/ppermute | solution.py:729
  63.0 16.1 %collective-permute-start.10 = (bf16[2,3,128,512]{3,2,1,0:T(8,128)(2,1)S(1)}, bf16[2,3,128,512]{3,2,1,0:T(8,128)(2,1)S(1)}, u32[]{:S(2)}, u32[]{:S(2)}) collective-permute-start(bf16[2,3,128,512]{3,2,1,0:T(8,128)(2,1)S(1)} %pad_maximum_fusion.7), channel_id=1, source_target_pairs={{0,8},{4,12},{8,0},{12,4},{16,24},{20,28},{24,16},{28,20},{1,9},{5... | collective-permute-start | bytes 2359304 | tf_op jit(solution)/shard_map/ppermute | solution.py:729
  84.5 36.9 %all-to-all-start = ((bf16[8,4,40,1024]{3,2,1,0:T(8,128)(2,1)}), bf16[8,4,40,1024]{3,2,1,0:T(8,128)(2,1)}, u32[]{:S(2)}, u32[]{:S(2)}) async-start(bf16[8,4,40,1024]{3,2,1,0:T(8,128)(2,1)} %bitcast.152), calls=%async_computation | async-start | bytes 5242880 | tf_op jit(solution)/shard_map/all_to_all | solution.py:635
  140.5 93.5 %all-to-all-start.1 = ((bf16[8,3,160,1024]{3,2,1,0:T(8,128)(2,1)}), bf16[8,3,160,1024]{3,2,1,0:T(8,128)(2,1)}, u32[]{:S(2)}, u32[]{:S(2)}) async-start(bf16[8,3,160,1024]{3,2,1,0:T(8,128)(2,1)} %to_many_slots.1.refs_4_), calls=%async_computation.1 | async-start | bytes 15728640 | tf_op jit(solution)/shard_map/all_to_all | solution.py:635
  145.6 117.8 %all-gather.6.cloned.1.call-start = ((), (), s32[]{:S(2)}) async-start(), calls=%async_computation.14 | async-start | bytes 5242880 | tf_op jit(solution)/shard_map/all_gather | solution.py:679
  238.1 36.0 %all-to-all-start.2 = ((bf16[8,4,40,1024]{3,2,1,0:T(8,128)(2,1)}), bf16[8,4,40,1024]{3,2,1,0:T(8,128)(2,1)S(1)}, u32[]{:S(2)}, u32[]{:S(2)}) async-start(bf16[8,4,40,1024]{3,2,1,0:T(8,128)(2,1)} %bitcast.151), calls=%async_computation.2 | async-start | bytes 5242880 | tf_op jit(solution)/shard_map/all_to_all | solution.py:635
  275.5 36.9 %all-to-all-start.3 = ((bf16[8,4,40,1024]{3,2,1,0:T(8,128)(2,1)}), bf16[8,4,40,1024]{3,2,1,0:T(8,128)(2,1)}, u32[]{:S(2)}, u32[]{:S(2)}) async-start(bf16[8,4,40,1024]{3,2,1,0:T(8,128)(2,1)} %bitcast.156), calls=%async_computation.3 | async-start | bytes 5242880 | tf_op jit(solution)/shard_map/all_to_all | solution.py:635
  312.4 35.8 %all-to-all-start.4 = ((bf16[8,4,40,1024]{3,2,1,0:T(8,128)(2,1)}), bf16[8,4,40,1024]{3,2,1,0:T(8,128)(2,1)S(1)}, u32[]{:S(2)}, u32[]{:S(2)}) async-start(bf16[8,4,40,1024]{3,2,1,0:T(8,128)(2,1)} %bitcast.157), calls=%async_computation.4 | async-start | bytes 5242880 | tf_op jit(solution)/shard_map/all_to_all | solution.py:635
  349.8 37.1 %all-to-all-start.5 = ((bf16[8,4,40,1024]{3,2,1,0:T(8,128)(2,1)}), bf16[8,4,40,1024]{3,2,1,0:T(8,128)(2,1)}, u32[]{:S(2)}, u32[]{:S(2)}) async-start(bf16[8,4,40,1024]{3,2,1,0:T(8,128)(2,1)} %bitcast.158), calls=%async_computation.5 | async-start | bytes 5242880 | tf_op jit(solution)/shard_map/all_to_all | solution.py:635
  386.8 35.8 %all-to-all-start.6 = ((bf16[8,4,40,1024]{3,2,1,0:T(8,128)(2,1)}), bf16[8,4,40,1024]{3,2,1,0:T(8,128)(2,1)S(1)}, u32[]{:S(2)}, u32[]{:S(2)}) async-start(bf16[8,4,40,1024]{3,2,1,0:T(8,128)(2,1)} %get-tuple-element.69), calls=%async_computation.6 | async-start | bytes 5242880 | tf_op jit(solution)/shard_map/all_to_all | solution.py:635
  391.5 72.4 %collective-permute-start.12 = (bf16[8,4,40,1024]{3,2,1,0:T(8,128)(2,1)}, bf16[8,4,40,1024]{3,2,1,0:T(8,128)(2,1)}, u32[]{:S(2)}, u32[]{:S(2)}) collective-permute-start(bf16[8,4,40,1024]{3,2,1,0:T(8,128)(2,1)} %get-tuple-element.68), channel_id=1, source_target_pairs={{0,1},{1,0},{2,3},{3,2},{4,5},{5,4},{6,7},{7,6},{8,9},{9,8},{10,11... | collective-permute-start | bytes 7864328 | tf_op jit(solution)/shard_map/ppermute | solution.py:632
  424.2 46.4 %all-to-all-start.8 = ((bf16[8,4,40,1024]{3,2,1,0:T(8,128)(2,1)}), bf16[8,4,40,1024]{3,2,1,0:T(8,128)(2,1)}, u32[]{:S(2)}, u32[]{:S(2)}) async-start(bf16[8,4,40,1024]{3,2,1,0:T(8,128)(2,1)} %get-tuple-element.70), calls=%async_computation.8 | async-start | bytes 5242880 | tf_op jit(solution)/shard_map/all_to_all | solution.py:635
  434.4 49.2 %collective-permute-start.13 = (bf16[512,1024]{1,0:T(8,128)(2,1)}, bf16[512,1024]{1,0:T(8,128)(2,1)}, u32[]{:S(2)}, u32[]{:S(2)}) collective-permute-start(bf16[512,1024]{1,0:T(8,128)(2,1)} %to_tokens.4.refs_2_), channel_id=1, source_target_pairs={{0,2},{1,3},{2,0},{3,1},{4,6},{5,7},{6,4},{7,5},{8,10},{9,11},{10,... | collective-permute-start | bytes 3145736 | tf_op jit(solution)/shard_map/ppermute | solution.py:632
  470.5 49.4 %all-to-all-start.7 = ((bf16[8,4,40,1024]{3,2,1,0:T(8,128)(2,1)}), bf16[8,4,40,1024]{3,2,1,0:T(8,128)(2,1)S(1)}, u32[]{:S(2)}, u32[]{:S(2)}) async-start(bf16[8,4,40,1024]{3,2,1,0:T(8,128)(2,1)} %add.298.refs_2_), calls=%async_computation.7 | async-start | bytes 5242880 | tf_op jit(solution)/shard_map/all_to_all | solution.py:635
  474.4 280.6 %reduce-scatter.2.cloned.1.call-start = ((), (), s32[]{:S(2)}) async-start(), calls=%async_computation.15 | async-start | bytes 13107200 | tf_op jit(solution)/shard_map/reduce_scatter | solution.py:824
  488.0 31.9 %collective-permute-start.14 = (bf16[512,1024]{1,0:T(8,128)(2,1)}, bf16[512,1024]{1,0:T(8,128)(2,1)}, u32[]{:S(2)}, u32[]{:S(2)}) collective-permute-start(bf16[512,1024]{1,0:T(8,128)(2,1)} %to_tokens.5.refs_20_), channel_id=1, source_target_pairs={{0,3},{1,2},{2,1},{3,0},{4,7},{5,6},{6,5},{7,4},{8,11},{9,10},{10,... | collective-permute-start | bytes 3145736 | tf_op jit(solution)/shard_map/ppermute | solution.py:632
  582.6 21.5 %collective-permute-start.16 = (bf16[4,3,128,1024]{3,2,1,0:T(8,128)(2,1)}, bf16[4,3,128,1024]{3,2,1,0:T(8,128)(2,1)}, u32[]{:S(2)}, u32[]{:S(2)}) collective-permute-start(bf16[4,3,128,1024]{3,2,1,0:T(8,128)(2,1)} %dynamic-slice_bitcast_fusion), channel_id=1, source_target_pairs={{0,4},{4,0},{8,12},{12,8},{16,20},{20,16},{24,28},{28,24},{1,5},{5... | collective-permute-start | bytes 9437192 | tf_op jit(solution)/shard_map/ppermute | solution.py:836
  603.7 52.7 %collective-permute-start.15 = (bf16[4,1,128,1024]{3,2,0,1:T(8,128)(2,1)}, bf16[4,1,128,1024]{3,2,0,1:T(8,128)(2,1)}, u32[]{:S(2)}, u32[]{:S(2)}) collective-permute-start(bf16[4,1,128,1024]{3,2,0,1:T(8,128)(2,1)} %dynamic-slice_bitcast_fusion.1), channel_id=1, source_target_pairs={{0,4},{4,0},{8,12},{12,8},{16,20},{20,16},{24,28},{28,24},{1,5},{5... | collective-permute-start | bytes 3145736 | tf_op jit(solution)/shard_map/ppermute | solution.py:836
  610.3 49.0 %all-to-all-start.11 = ((bf16[4,3,128,1024]{3,2,1,0:T(8,128)(2,1)}), bf16[4,3,128,1024]{3,2,1,0:T(8,128)(2,1)}, u32[]{:S(2)}, u32[]{:S(2)}) async-start(bf16[4,3,128,1024]{3,2,1,0:T(8,128)(2,1)} %fusion), calls=%async_computation.12 | async-start | bytes 6291456 | tf_op jit(solution)/shard_map/all_to_all | solution.py:840
  659.3 53.5 %all-to-all-start.10 = ((bf16[4,1,128,1024]{3,2,1,0:T(8,128)(2,1)}), bf16[4,1,128,1024]{3,2,1,0:T(8,128)(2,1)}, u32[]{:S(2)}, u32[]{:S(2)}) async-start(bf16[4,1,128,1024]{3,2,1,0:T(8,128)(2,1)} %fusion.18), calls=%async_computation.11 | async-start | bytes 2097152 | tf_op jit(solution)/shard_map/all_to_all | solution.py:840
  663.5 141.3 %all-gather.8.cloned.1.call-start = ((), (), s32[]{:S(2)}) async-start(), calls=%async_computation.16 | async-start | bytes 2359296 | tf_op jit(solution)/shard_map/all_gather | solution.py:865
  663.6 24.3 %collective-permute-start.23 = (f32[35330]{0:T(1024)S(1)}, f32[35330]{0:T(1024)S(1)}, u32[]{:S(2)}, u32[]{:S(2)}) collective-permute-start(f32[35330]{0:T(1024)S(1)} %add.206), channel_id=1, source_target_pairs={{0,1},{1,0},{2,3},{3,2},{4,5},{5,4},{6,7},{7,6},{8,9},{9,8},{10,11... | collective-permute-start | bytes 423968 | tf_op jit(solution)/shard_map/ppermute | solution.py:686
  687.9 23.3 %collective-permute-start.24 = (f32[35330]{0:T(1024)S(1)}, f32[35330]{0:T(1024)}, u32[]{:S(2)}, u32[]{:S(2)}) collective-permute-start(f32[35330]{0:T(1024)S(1)} %add.207), channel_id=1, source_target_pairs={{0,2},{1,3},{2,0},{3,1},{4,6},{5,7},{6,4},{7,5},{8,10},{9,11},{10,... | collective-permute-start | bytes 423968 | tf_op jit(solution)/shard_map/ppermute | solution.py:686
  694.8 20.1 %collective-permute-start.19 = (bf16[128,1024]{1,0:T(8,128)(2,1)}, bf16[128,1024]{1,0:T(8,128)(2,1)}, u32[]{:S(2)}, u32[]{:S(2)}) collective-permute-start(bf16[128,1024]{1,0:T(8,128)(2,1)} %get-tuple-element.125), channel_id=1, source_target_pairs={{0,3},{1,2},{2,1},{3,0},{4,7},{5,6},{6,5},{7,4},{8,11},{9,10},{10,... | collective-permute-start | bytes 786440 | tf_op jit(solution)/shard_map/ppermute | solution.py:632
  696.7 56.1 %collective-permute-start.18 = (bf16[128,1024]{1,0:T(8,128)(2,1)}, bf16[128,1024]{1,0:T(8,128)(2,1)}, u32[]{:S(2)}, u32[]{:S(2)}) collective-permute-start(bf16[128,1024]{1,0:T(8,128)(2,1)} %get-tuple-element.126), channel_id=1, source_target_pairs={{0,2},{1,3},{2,0},{3,1},{4,6},{5,7},{6,4},{7,5},{8,10},{9,11},{10,... | collective-permute-start | bytes 786440 | tf_op jit(solution)/shard_map/ppermute | solution.py:632
  698.8 54.1 %collective-permute-start.17 = (bf16[128,1024]{1,0:T(8,128)(2,1)}, bf16[128,1024]{1,0:T(8,128)(2,1)}, u32[]{:S(2)}, u32[]{:S(2)}) collective-permute-start(bf16[128,1024]{1,0:T(8,128)(2,1)} %get-tuple-element.127), channel_id=1, source_target_pairs={{0,1},{1,0},{2,3},{3,2},{4,5},{5,4},{6,7},{7,6},{8,9},{9,8},{10,11... | collective-permute-start | bytes 786440 | tf_op jit(solution)/shard_map/ppermute | solution.py:632
  754.9 45.1 %all-to-all-start.9 = ((bf16[8,4,40,1024]{3,2,1,0:T(8,128)(2,1)}), bf16[8,4,40,1024]{3,2,1,0:T(8,128)(2,1)}, u32[]{:S(2)}, u32[]{:S(2)}) async-start(bf16[8,4,40,1024]{3,2,1,0:T(8,128)(2,1)} %reduce-scatter.2.cloned.1.call-done), calls=%async_computation.10 | async-start | bytes 5242880 | tf_op jit(solution)/shard_map/all_to_all | solution.py:635
  (54 other events, 413.5 us)
Sparse Core Ops, SparseCore 0:
  49.6 80.8 all-gather.3
  183.7 79.6 all-gather.5
  535.7 213.1 reduce-scatter.1
  755.0 43.0 all-gather.7
